TPU v7x, 256 devices: a whole 4x4x8 slice. The times are simulated.
256 devices in a mesh: dp: 8 (over y, z_hi), mp: 32 (over z_lo, x, core).
Axes of the slice: x: 4, y: 4, z: 8 (z_hi: 2, z_lo: 4; z = z_hi * 4 + z_lo), core: 2. Of those that a mesh axis runs over, the one named last changes fastest.
Arguments:
- responses: bfloat16 [2048, 4608], P('dp', 'mp'), may hold values from -6 to 6
- frozen_weight: bfloat16 [36864, 4608], P('mp'), may hold values from -0.09375 to 0.09375
- skew_param: float32 [2, 1152, 32, 32], P(None, 'mp'), may hold values from -0.6 to 0.6
- section_perm: int32 [2, 32], replicated, may hold values from 0 to 31, each once within a row
- prefix_ids: int32 [2048], P('dp'), may hold values from 0 to 15
- prefix_scale: float32 [16, 36864], P(None, 'mp'), may hold values from 0.1 to 1.9
- out_grad: bfloat16 [36864, 2048], P('mp', 'dp'), may hold values from -6 to 6
Outputs:
- judged: bfloat16 [36864, 2048], P('mp', 'dp')
- input_grad: bfloat16 [4608, 2048], P('mp', 'dp')
- skew_grad: float32 [2, 1152, 32, 32], P(None, 'mp')
Inputs may be any that keep to these rules, and one draw needn't show every extreme that they name: `section_perm`: each row is a permutation of 0 to 31.
All inputs are finite; a program needn't handle non-finite values.
Results may differ from a plain program's by a relative error of at most 0.005.
Values may be sent and summed in bfloat16 or wider, within the bound.
No kernel may reach another device: no remote copies, remote signals or barrier semaphores. Data moves between devices by JAX's collectives and lax.ppermute only.
A program may use at most 128 MiB of HBM per device.

v0:
```python
import jax
import jax.numpy as jnp
from jax import lax
from jax.sharding import PartitionSpec as P


def partner(x, axis, bit):
    return lax.ppermute(x, axis, [(i, i ^ 1 << bit) for i in range(lax.axis_size(axis))])


def rotations(skew_param, section_perm):
    highest = lax.Precision.HIGHEST
    block_width = skew_param.shape[-1]
    skew_part = skew_param - jnp.swapaxes(skew_param, -1, -2)
    identity = jnp.eye(block_width, dtype=jnp.float32)
    minus_part = identity - skew_part
    gram_matrix = identity - jnp.matmul(skew_part, skew_part, precision=highest)
    squared = jnp.matmul(minus_part, minus_part, precision=highest)
    factor = jnp.linalg.cholesky(gram_matrix)
    rotation = jax.scipy.linalg.cho_solve((factor, True), squared)
    select = (
        section_perm[:, :, None] == jnp.arange(block_width, dtype=jnp.int32)[None, None, :]
    ).astype(jnp.float32)
    return jnp.einsum("sua,sjuw,swc->sjac", select, rotation, select, precision=highest)


def pair_up(current, bit_place, is_lower, half_width):
    row_count = current.shape[1]
    shaped = current.reshape(-1, 2, half_width, row_count)
    front_half = shaped[:, 0]
    second = shaped[:, 1]
    outgoing = jnp.where(is_lower, second, front_half)
    incoming = partner(outgoing, "mp", bit_place)
    return jnp.where(
        is_lower, jnp.concatenate([front_half, incoming], 1), jnp.concatenate([incoming, second], 1)
    )


def pair_back(blocks, bit_place, is_lower, half_width):
    row_count = blocks.shape[2]
    kept_low = blocks[:, :half_width]
    kept_high = blocks[:, half_width:]
    outgoing = jnp.where(is_lower, kept_high, kept_low)
    incoming = partner(outgoing, "mp", bit_place)
    joined = jnp.where(
        is_lower,
        jnp.concatenate([kept_low, incoming], 1),
        jnp.concatenate([incoming, kept_high], 1),
    )
    return joined.reshape(-1, row_count)


def per_device(
    responses, frozen_weight, skew_param, section_perm, prefix_ids, prefix_scale, out_grad
):
    highest = lax.Precision.HIGHEST
    half_width = skew_param.shape[-1] // 2
    section_count = skew_param.shape[0]
    top_bit = lax.axis_size("mp").bit_length() - 1
    position = lax.axis_index("mp")
    row_count = responses.shape[0]
    rotation = rotations(skew_param, section_perm)
    columns = frozen_weight
    hidden = lax.dot_general(
        columns,
        lax.all_gather(responses, "mp", axis=1, tiled=True),
        (((1,), (1,)), ((), ())),
        preferred_element_type=jnp.float32,
    )
    onehot = (
        prefix_ids[None, :] == jnp.arange(prefix_scale.shape[0], dtype=jnp.int32)[:, None]
    ).astype(jnp.float32)
    scale_rows = lax.dot_general(prefix_scale, onehot, (((0,), (0,)), ((), ())), precision=highest)
    current = hidden
    stored = []
    for section in range(section_count):
        bit_place = top_bit - 1 - section
        is_lower = jnp.right_shift(position, bit_place) & 1 == 0
        blocks = pair_up(current, bit_place, is_lower, half_width)
        stored.append(blocks)
        turned = jnp.einsum("bac,bcr->bar", rotation[section], blocks, precision=highest)
        current = pair_back(turned, bit_place, is_lower, half_width)
    judged = (current * scale_rows).astype(jnp.bfloat16)
    adjoint = out_grad.astype(jnp.float32) * scale_rows
    norm_factor = 1.0 / (row_count * lax.axis_size("dp")) ** 0.5
    section_grads = [None] * section_count
    for section in reversed(range(section_count)):
        bit_place = top_bit - 1 - section
        is_lower = jnp.right_shift(position, bit_place) & 1 == 0
        incoming = pair_up(adjoint, bit_place, is_lower, half_width)
        partial_grad = jnp.einsum("bar,bcr->bac", incoming, stored[section], precision=highest)
        section_grads[section] = lax.psum(partial_grad, "dp")
        turned = jnp.einsum("bac,bar->bcr", rotation[section], incoming, precision=highest)
        adjoint = pair_back(turned, bit_place, is_lower, half_width)
    summed = jnp.stack(section_grads)
    rotation_grad = summed * norm_factor
    unused, pullback = jax.vjp(lambda params: rotations(params, section_perm), skew_param)
    skew_grad = pullback(rotation_grad)[0]
    hidden_grad = adjoint.astype(jnp.bfloat16)
    columns = frozen_weight
    summed_input = lax.psum_scatter(
        lax.dot_general(
            columns, hidden_grad, (((0,), (0,)), ((), ())), preferred_element_type=jnp.float32
        ),
        "mp",
        scatter_dimension=0,
        tiled=True,
    )
    input_grad = summed_input.astype(jnp.bfloat16)
    return (judged, input_grad, skew_grad)


def solution(mesh):
    in_specs = (
        P("dp", "mp"),
        P("mp", None),
        P(None, "mp", None, None),
        P(),
        P("dp"),
        P(None, "mp"),
        P("mp", "dp"),
    )
    out_specs = (P("mp", "dp"), P("mp", "dp"), P(None, "mp", None, None))
    return jax.shard_map(
        per_device, mesh=mesh, in_specs=in_specs, out_specs=out_specs, check_vma=False
    )
```

profile of v0, /device:TPU:24, one launch (start us, length us, event | category | flops | bytes accessed | tf_op | source)
XLA Modules:
  0.0 761.3 jit_solution(13626149130093123226)
XLA Ops:
  8.0 2.2 broadcast_subtract_fusion
  15.4 2.1 copy.318
  21.3 211.7 %custom-call.21 = f32[2,36,32,32]{3,2,1,0:T(8,128)S(1)} custom-call(f32[2,36,32,32]{3,2,1,0:T(8,128)} %copy.319), custom_call_target="Cholesky" | custom-call | tf_op jit(solution)/shard_map/jit(cholesky)/cholesky/custom-call.1 | solution.py:19
  235.2 2.5 select_bitcast_fusion
  239.0 26.5 %custom-call.23 = f32[2,36,1,32,32]{1,3,4,2,0:T(8,128)} custom-call(f32[2,36,1,32,32]{1,4,3,2,0:T(8,128)} %select_bitcast_fusion.1), custom_call_target="InvertDiagBlocksLowerTriangular" | custom-call | tf_op jit(solution)/shard_map/jit(_cho_solve)/vmap(vmap())/triangular_solve/custom-call.2 | solution.py:20
  265.5 3.4 copy.327
  268.9 3.2 copy.328
  276.5 2.2 fusion.47
  280.7 6.8 fusion.48
  288.3 3.3 collective-permute-start
  295.1 22.8 %collective-permute-done = f32[36,16,256]{2,1,0:T(8,128)} collective-permute-done((f32[36,16,256]{2,1,0:T(8,128)}, f32[36,16,256]{2,1,0:T(8,128)}, u32[]{:S(2)}, u32[]{:S(2)}) %collective-permute-start) | collective-permute-done | bytes 589856 | tf_op jit(solution)/shard_map/ppermute | solution.py:8
  317.9 2.5 fusion.16
  321.7 28.3 %collective-permute-done.1 = f32[36,16,256]{2,1,0:T(8,128)S(1)} collective-permute-done((f32[36,16,256]{2,1,0:T(8,128)}, f32[36,16,256]{2,1,0:T(8,128)S(1)}, u32[]{:S(2)}, u32[]{:S(2)}) %collective-permute-start.1) | collective-permute-done | bytes 589856 | tf_op jit(solution)/shard_map/ppermute | solution.py:8
  353.5 2.4 copy.343
  356.1 11.4 %collective-permute-done.2 = f32[36,16,256]{2,1,0:T(8,128)} collective-permute-done((f32[36,16,256]{2,1,0:T(8,128)}, f32[36,16,256]{2,1,0:T(8,128)}, u32[]{:S(2)}, u32[]{:S(2)}) %collective-permute-start.2) | collective-permute-done | bytes 589856 | tf_op jit(solution)/shard_map/ppermute | solution.py:8
  367.5 2.5 fusion.15
  371.6 2.1 copy.339
  375.4 8.7 %collective-permute-done.3 = f32[36,16,256]{2,1,0:T(8,128)S(1)} collective-permute-done((f32[36,16,256]{2,1,0:T(8,128)}, f32[36,16,256]{2,1,0:T(8,128)S(1)}, u32[]{:S(2)}, u32[]{:S(2)}) %collective-permute-start.3) | collective-permute-done | bytes 589856 | tf_op jit(solution)/shard_map/ppermute | solution.py:8
  388.2 3.3 convert_multiply_fusion
  394.1 11.3 %collective-permute-done.4 = f32[36,16,256]{2,1,0:T(8,128)S(1)} collective-permute-done((f32[36,16,256]{2,1,0:T(8,128)S(1)}, f32[36,16,256]{2,1,0:T(8,128)S(1)}, u32[]{:S(2)}, u32[]{:S(2)}) %collective-permute-start.4) | collective-permute-done | bytes 589856 | tf_op jit(solution)/shard_map/ppermute | solution.py:8
  407.6 10.3 %collective-permute-done.5 = f32[36,16,256]{2,1,0:T(8,128)S(1)} collective-permute-done((f32[36,16,256]{2,1,0:T(8,128)S(1)}, f32[36,16,256]{2,1,0:T(8,128)S(1)}, u32[]{:S(2)}, u32[]{:S(2)}) %collective-permute-start.5) | collective-permute-done | bytes 589856 | tf_op jit(solution)/shard_map/ppermute | solution.py:8
  418.2 9.1 %collective-permute-start.6 = (f32[36,16,256]{2,1,0:T(8,128)S(1)}, f32[36,16,256]{2,1,0:T(8,128)S(1)}, u32[]{:S(2)}, u32[]{:S(2)}) collective-permute-start(f32[36,16,256]{2,1,0:T(8,128)S(1)} %broadcast_select_fusion.5), channel_id=1, source_target_pairs={{0,16},{1,17},{2,18},{3,19},{4,20},{5,21},{6,22},{7,23},{8,24},{9,... | collective-permute-start | bytes 1769480 | tf_op jit(solution)/shard_map/ppermute | solution.py:8
  427.3 21.3 %collective-permute-done.6 = f32[36,16,256]{2,1,0:T(8,128)S(1)} collective-permute-done((f32[36,16,256]{2,1,0:T(8,128)S(1)}, f32[36,16,256]{2,1,0:T(8,128)S(1)}, u32[]{:S(2)}, u32[]{:S(2)}) %collective-permute-start.6) | collective-permute-done | bytes 589856 | tf_op jit(solution)/shard_map/ppermute | solution.py:8
  451.0 3.4 convolution_bitcast_fusion.3
  454.4 3.4 convolution_bitcast_fusion.4
  457.9 6.7 collective-permute-done.7
  464.8 9.0 %convolution_bitcast_fusion = f32[4608,256]{0,1:T(8,128)} fusion(bf16[1152,256]{1,0:T(8,128)(2,1)S(1)} %bitcast.211, bf16[1152,4608]{1,0:T(8,128)(2,1)} %param.13), kind=kOutput, calls=%fused_computation | convolution fusion | flops 2717908992 | bytes 15925248 | tf_op jit(solution)/shard_map/dot_general | solution.py:102
  473.8 6.1 copy.393
  479.9 26.2 %custom-call.26 = f32[2,36,1,32,32]{1,3,4,2,0:T(8,128)S(1)} custom-call(f32[2,36,1,32,32]{1,4,3,2,0:T(8,128)} %get-tuple-element.26), custom_call_target="InvertDiagBlocksLowerTriangular" | custom-call | tf_op jit(solution)/shard_map/transpose(jvp(jit(_cho_solve)))/vmap(vmap())/triangular_solve/custom-call.0 | solution.py:20
  508.3 2.3 copy.353
  510.6 3.4 copy.363
  514.0 3.3 copy.373
  517.3 3.3 copy.380
  521.9 2.5 fusion.49
  524.4 2.3 fusion.50
  526.8 2.1 copy.385
  528.9 71.7 %all-reduce.3.cloned.1.call-done = (f32[1,36,32,32]{3,2,1,0:T(8,128)}, f32[1,36,32,32]{3,2,1,0:T(8,128)}) async-done(((f32[1,36,32,32]{3,2,1,0:T(8,128)}, f32[1,36,32,32]{3,2,1,0:T(8,128)}), (f32[1,36,32,32]{3,2,1,0:T(8,128)}, f32[1,36,32,32]{3,2,1,0:T(8,128)})) %all-reduce.3.cloned.1.call-update) | async-done | bytes 294928 | tf_op jit(solution)/shard_map/psum | solution.py:92
  600.6 3.0 convolution_bitcast_fusion.2
  603.7 3.3 copy.349
  607.0 2.8 fusion.20
  609.8 3.3 copy.354
  613.2 3.8 fusion.51
  617.0 2.3 fusion.52
  619.3 3.3 copy.356
  622.6 3.3 copy.360
  625.9 2.6 fusion.53
  630.6 2.3 fusion.55
  632.9 3.0 copy.362
  636.0 2.5 fusion.9
  638.5 3.3 copy.364
  641.8 3.6 fusion.56
  648.7 3.2 copy.367
  651.9 3.0 fusion.57
  654.9 2.4 fusion.58
  657.3 3.4 copy.370
  662.6 2.9 fusion.6
  665.5 2.3 copy.374
  667.8 3.1 fusion.60
  670.9 3.4 copy.378
  674.3 2.3 fusion.59
  676.6 3.5 copy.377
  683.4 2.1 copy.383
  686.8 2.1 copy.382
  693.2 59.5 %reduce-scatter.4.cloned.1.call-done = f32[144,256]{1,0:T(8,128)} async-done(((f32[4608,256]{1,0:T(8,128)}), f32[144,256]{1,0:T(8,128)}) %reduce-scatter.4.cloned.1.call-update) | async-done | bytes 147472
  (149 shorter events, 65.1 us)
Async XLA Ops:
  7.2 366.5 %copy-start = (f32[16,1152]{1,0:T(8,128)S(1)}, f32[16,1152]{1,0:T(8,128)}, u32[]{:S(2)}) copy-start(f32[16,1152]{1,0:T(8,128)} %param.17) | copy-start | bytes 221188
  7.2 273.5 %all-gather.2.cloned.1.call-start = ((), (), s32[]{:S(2)}) async-start(), calls=%async_computation.1 | async-start | bytes 2433024 | tf_op jit(solution)/shard_map/all_gather | solution.py:66
  7.9 592.7 %all-reduce.3.cloned.1.call-start = ((), (), s32[]{:S(2)}) async-start(), calls=%async_computation.3 | async-start | bytes 2359296 | tf_op jit(solution)/shard_map/psum | solution.py:92
  10.2 1.0 copy-start.14
  10.2 261.9 %copy-start.13 = (f32[2,36,32,32]{1,3,2,0:T(8,128)}, f32[2,36,32,32]{1,3,2,0:T(8,128)S(1)}, u32[]{:S(2)}) copy-start(f32[2,36,32,32]{1,3,2,0:T(8,128)S(1)} %get-tuple-element.49) | copy-start | bytes 884740
  237.7 31.2 %copy-start.15 = (f32[2,36,32,32]{1,3,2,0:T(8,128)}, f32[2,36,32,32]{1,3,2,0:T(8,128)S(1)}, u32[]{:S(2)}) copy-start(f32[2,36,32,32]{1,3,2,0:T(8,128)S(1)} %get-tuple-element.27) | copy-start | bytes 884740
  273.1 1.3 copy-start.2
  273.1 1.7 copy-start.9
  274.8 3.9 copy-start.4
  274.8 1.7 copy-start.11
  276.5 2.2 copy-start.36
  288.3 29.6 %collective-permute-start = (f32[36,16,256]{2,1,0:T(8,128)}, f32[36,16,256]{2,1,0:T(8,128)}, u32[]{:S(2)}, u32[]{:S(2)}) collective-permute-start(f32[36,16,256]{2,1,0:T(8,128)} %broadcast_select_fusion.7), channel_id=1, source_target_pairs={{0,16},{1,17},{2,18},{3,19},{4,20},{5,21},{6,22},{7,23},{8,24},{9,... | collective-permute-start | bytes 1769480 | tf_op jit(solution)/shard_map/ppermute | solution.py:8
  295.1 25.3 %copy-start.25 = (f32[36,16,256]{2,1,0:T(8,128)}, f32[36,16,256]{2,1,0:T(8,128)S(1)}, u32[]{:S(2)}) copy-start(f32[36,16,256]{2,1,0:T(8,128)S(1)} %get-tuple-element.45) | copy-start | bytes 1769476
  295.1 25.3 %copy-start.27 = (f32[36,16,256]{2,1,0:T(8,128)}, f32[36,16,256]{2,1,0:T(8,128)S(1)}, u32[]{:S(2)}) copy-start(f32[36,16,256]{2,1,0:T(8,128)S(1)} %get-tuple-element.46) | copy-start | bytes 1769476
  321.7 28.3 %collective-permute-start.1 = (f32[36,16,256]{2,1,0:T(8,128)}, f32[36,16,256]{2,1,0:T(8,128)S(1)}, u32[]{:S(2)}, u32[]{:S(2)}) collective-permute-start(f32[36,16,256]{2,1,0:T(8,128)} %get-tuple-element.43), channel_id=1, source_target_pairs={{0,16},{1,17},{2,18},{3,19},{4,20},{5,21},{6,22},{7,23},{8,24},{9,... | collective-permute-start | bytes 1769480 | tf_op jit(solution)/shard_map/ppermute | solution.py:8
  350.0 0.8 copy-start.33
  353.5 13.9 %collective-permute-start.2 = (f32[36,16,256]{2,1,0:T(8,128)}, f32[36,16,256]{2,1,0:T(8,128)}, u32[]{:S(2)}, u32[]{:S(2)}) collective-permute-start(f32[36,16,256]{2,1,0:T(8,128)} %broadcast_select_fusion.3), channel_id=1, source_target_pairs={{0,8},{1,9},{2,10},{3,11},{4,12},{5,13},{6,14},{7,15},{8,0},{9,1},... | collective-permute-start | bytes 1769480 | tf_op jit(solution)/shard_map/ppermute | solution.py:8
  356.0 11.5 %copy-start.16 = (f32[36,32,32]{1,2,0:T(8,128)S(1)}, f32[36,32,32]{1,2,0:T(8,128)}, u32[]{:S(2)}) copy-start(f32[36,32,32]{1,2,0:T(8,128)} %copy.343) | copy-start | bytes 442372
  356.1 13.9 %copy-start.29 = (f32[36,16,256]{2,1,0:T(8,128)}, f32[36,16,256]{2,1,0:T(8,128)S(1)}, u32[]{:S(2)}) copy-start(f32[36,16,256]{2,1,0:T(8,128)S(1)} %get-tuple-element.40) | copy-start | bytes 1769476
  356.1 13.9 %copy-start.31 = (f32[36,16,256]{2,1,0:T(8,128)}, f32[36,16,256]{2,1,0:T(8,128)S(1)}, u32[]{:S(2)}) copy-start(f32[36,16,256]{2,1,0:T(8,128)S(1)} %get-tuple-element.41) | copy-start | bytes 1769476
  371.3 2.4 copy-start.38
  371.3 12.9 %collective-permute-start.3 = (f32[36,16,256]{2,1,0:T(8,128)}, f32[36,16,256]{2,1,0:T(8,128)S(1)}, u32[]{:S(2)}, u32[]{:S(2)}) collective-permute-start(f32[36,16,256]{2,1,0:T(8,128)} %get-tuple-element.38), channel_id=1, source_target_pairs={{0,8},{1,9},{2,10},{3,11},{4,12},{5,13},{6,14},{7,15},{8,0},{9,1},... | collective-permute-start | bytes 1769480 | tf_op jit(solution)/shard_map/ppermute | solution.py:8
  384.2 0.8 copy-start.34
  393.2 12.3 %copy-start.17 = (f32[36,32,32]{1,2,0:T(8,128)S(1)}, f32[36,32,32]{1,2,0:T(8,128)}, u32[]{:S(2)}) copy-start(f32[36,32,32]{1,2,0:T(8,128)} %copy.343) | copy-start | bytes 442372
  393.2 12.3 %collective-permute-start.4 = (f32[36,16,256]{2,1,0:T(8,128)S(1)}, f32[36,16,256]{2,1,0:T(8,128)S(1)}, u32[]{:S(2)}, u32[]{:S(2)}) collective-permute-start(f32[36,16,256]{2,1,0:T(8,128)S(1)} %broadcast_select_fusion.1), channel_id=1, source_target_pairs={{0,8},{1,9},{2,10},{3,11},{4,12},{5,13},{6,14},{7,15},{8,0},{9,1},... | collective-permute-start | bytes 1769480 | tf_op jit(solution)/shard_map/ppermute | solution.py:8
  406.9 11.0 %collective-permute-start.5 = (f32[36,16,256]{2,1,0:T(8,128)S(1)}, f32[36,16,256]{2,1,0:T(8,128)S(1)}, u32[]{:S(2)}, u32[]{:S(2)}) collective-permute-start(f32[36,16,256]{2,1,0:T(8,128)S(1)} %get-tuple-element.31), channel_id=1, source_target_pairs={{0,8},{1,9},{2,10},{3,11},{4,12},{5,13},{6,14},{7,15},{8,0},{9,1},... | collective-permute-start | bytes 1769480 | tf_op jit(solution)/shard_map/ppermute | solution.py:8
  418.2 30.4 %collective-permute-start.6 = (f32[36,16,256]{2,1,0:T(8,128)S(1)}, f32[36,16,256]{2,1,0:T(8,128)S(1)}, u32[]{:S(2)}, u32[]{:S(2)}) collective-permute-start(f32[36,16,256]{2,1,0:T(8,128)S(1)} %broadcast_select_fusion.5), channel_id=1, source_target_pairs={{0,16},{1,17},{2,18},{3,19},{4,20},{5,21},{6,22},{7,23},{8,24},{9,... | collective-permute-start | bytes 1769480 | tf_op jit(solution)/shard_map/ppermute | solution.py:8
  449.8 1.1 copy-start.30
  449.8 1.2 copy-start.32
  449.9 4.5 copy-start.26
  449.9 4.5 copy-start.28
  449.9 14.7 %collective-permute-start.7 = (bf16[36,16,256]{2,1,0:T(8,128)(2,1)S(1)}, bf16[36,16,256]{2,1,0:T(8,128)(2,1)S(1)}, u32[]{:S(2)}, u32[]{:S(2)}) collective-permute-start(bf16[36,16,256]{2,1,0:T(8,128)(2,1)S(1)} %get-tuple-element.52), channel_id=1, source_target_pairs={{0,16},{1,17},{2,18},{3,19},{4,20},{5,21},{6,22},{7,23},{8,24},{9,... | collective-permute-start | bytes 884744 | tf_op jit(solution)/shard_map/ppermute | solution.py:8
  457.8 294.8 %reduce-scatter.4.cloned.1.call-start = ((), (), s32[]{:S(2)}) async-start(), calls=%async_computation.2 | async-start | bytes 4866048
  506.1 1.0 copy-start.24
  524.4 2.4 copy-start.7
  625.9 2.6 copy-start.8
  628.6 2.0 copy-start.5
  632.9 3.0 copy-start.23
  638.5 3.3 copy-start.20
  645.4 2.0 copy-start.35
  651.9 3.0 copy-start.10
  657.3 3.4 copy-start.12
  660.7 1.9 copy-start.37
  670.9 3.4 copy-start.19
  676.6 3.5 copy-start.6
  680.0 1.3 copy-start.3
  683.4 2.1 copy-start.18
  686.7 2.1 copy-start.21
  686.8 2.1 copy-start.22
  690.9 63.5 %copy-start.1 = (f32[16,1152]{1,0:T(8,128)S(1)}, f32[16,1152]{1,0:T(8,128)}, u32[]{:S(2)}) copy-start(f32[16,1152]{1,0:T(8,128)} %param.17) | copy-start | bytes 221188
Sparse Core Ops, SparseCore 0:
  9.9 64.4 all-gather.1
  457.9 142.6 all-reduce.2
  603.2 149.3 reduce-scatter.3
where the time goes:
time: 768 us; the launch traced here: 761 us
  other arithmetic  296 us (39%)
  waiting for transfers between devices  253 us (33%)
  local copies, waits for them, and re-layouts  102 us (13%)
  matrix products  81.9 us (11%)
  between operations  14.8 us (2%)
  starting transfers between devices  14.4 us (2%)
    another operation x4, other arithmetic, rotations(): factor = jnp.linalg.cholesky(gram_matrix)  212 us
    ppermute x8, waiting for transfers between devices, partner(): lax.ppermute(x, axis, [(i, i ^ 1 << bit) for i in range(lax.axis_size(axi...  121 us
    psum x1, waiting for transfers between devices, per_device(): section_grads[section] = lax.psum(partial_grad, 'dp')  71.7 us
    unnamed x4, waiting for transfers between devices  60.2 us
    another operation x5, other arithmetic, rotations(): rotation = jax.scipy.linalg.cho_solve((factor, True), squared)  56.6 us
    unnamed x84, local copies, waits for them, and re-layouts  19.1 us
    another operation x8, matrix products, rotations(): rotation = jax.scipy.linalg.cho_solve((factor, True), squared)  16.9 us
    another operation x6, local copies, waits for them, and re-layouts, rotations(): rotation = jax.scipy.linalg.cho_solve((factor, True), squared)  16.4 us
  transfers between devices with their start and end apart: 11, of which 10 were waited for; matrix products, arithmetic and copies ran while one was open for 58% of the time, Pallas kernels for 0%

commit v1 on v0

v1 whole, which is shorter than its diff:
```python
import functools

import jax
import jax.numpy as jnp
from jax import lax
from jax.experimental import pallas as pl
from jax.experimental.pallas import tpu as pltpu
from jax.sharding import Mesh, PartitionSpec as P

F32 = jnp.float32
BF16 = jnp.bfloat16
GROUP = 4
VMEM_LIMIT = 56 * 1024 * 1024

VMEM = pl.BlockSpec(memory_space=pltpu.VMEM)
SMEM = pl.BlockSpec(memory_space=pltpu.SMEM)
PARAMS = pltpu.CompilerParams(vmem_limit_bytes=VMEM_LIMIT)


def xor(x, axis, k):
    return lax.ppermute(x, axis, [(i, i ^ k) for i in range(lax.axis_size(axis))])


def shift(x, axis, k):
    n = lax.axis_size(axis)
    return lax.ppermute(x, axis, [(i, (i + k) % n) for i in range(n)])


def mm(a, b):
    return jnp.dot(a, b, preferred_element_type=F32)


def split(x):
    hi = x.astype(BF16)
    return hi, (x - hi.astype(F32)).astype(BF16)


def rot_kernel(k_ref, pi_ref, pot_ref, m_ref, mt_ref, at_ref, raw, mat, turned):
    n = k_ref.shape[1]
    blocks = k_ref.shape[3]
    raw[...] = jnp.zeros_like(raw)
    for s in range(2):
        raw[:, 64 * s : 64 * s + blocks] = k_ref[s].reshape(n * n, blocks)
    sub = lax.broadcasted_iota(jnp.int32, (n, 128), 0)
    for u in range(n):
        mat[u * n : (u + 1) * n, :] = (
            raw[u * n : (u + 1) * n, :] - raw[pl.ds(u, n, stride=n), :]
            + jnp.where(sub == u, 1.0, 0.0)
        )

    def eliminate(k, carry):
        at = sub == k
        base = pl.multiple_of(k * n, n)
        pivot = 1.0 / mat[pl.ds(base + k, 1), :]
        row = jnp.where(at, 1.0, mat[pl.ds(base, n), :]) * pivot
        for i in range(n):
            factor = mat[pl.ds(i * n + k, 1), :]
            mine = jnp.where(at, 0.0, mat[i * n : (i + 1) * n, :])
            mat[i * n : (i + 1) * n, :] = mine - factor * row
        mat[pl.ds(base, n), :] = row
        return carry

    lax.fori_loop(0, n, eliminate, 0)
    for u in range(n):
        turned[u * 128 : (u + 1) * 128, :] = jnp.transpose(mat[u * n : (u + 1) * n, :])
    width = GROUP * n
    r = lax.broadcasted_iota(jnp.int32, (width, width), 0) // n
    c = lax.broadcasted_iota(jnp.int32, (width, width), 1) // n
    diagonal = r == c
    for s in range(2):
        pi, pot = pi_ref[s], pot_ref[s]
        ident = mm(pot, pi)
        for g in range(blocks // GROUP):
            rows = jnp.concatenate(
                [turned[pl.ds(64 * s + GROUP * g + q, n, stride=128), :] for q in range(GROUP)], 0
            )
            wide = jnp.where(diagonal, jnp.concatenate([rows] * GROUP, 1), 0.0)
            at_hi, at_lo = split(jnp.transpose(wide))
            at_ref[s, g, 0] = at_hi
            at_ref[s, g, 1] = at_lo
            hi, lo = split(wide)
            hi = mm(pot, mm(hi, pi).astype(BF16))
            lo = mm(pot, mm(lo, pi).astype(BF16))
            rot = 2.0 * (hi + lo) - ident
            m_ref[s, g, 0], m_ref[s, g, 1] = split(rot)
            mt_ref[s, g, 0], mt_ref[s, g, 1] = split(jnp.transpose(rot))


def rotations(skew, pi, pot):
    n = skew.shape[-1]
    groups = skew.shape[1] // GROUP
    width = GROUP * n
    shape = jax.ShapeDtypeStruct((2, groups, 2, width, width), BF16)
    return pl.pallas_call(
        rot_kernel,
        out_shape=(shape, shape, shape),
        in_specs=[VMEM] * 3,
        out_specs=(VMEM,) * 3,
        scratch_shapes=[
            pltpu.VMEM((n * n, 128), F32),
            pltpu.VMEM((n * n, 128), F32),
            pltpu.VMEM((n * 128, n), F32),
        ],
        compiler_params=PARAMS,
        cost_estimate=pl.CostEstimate(flops=10**9, bytes_accessed=4 * 10**6, transcendentals=0),
        name="rotations",
    )(jnp.transpose(skew, (0, 2, 3, 1)), pi, pot)


def pieces(a_ref, b_ref, g, half):
    span = slice(g * half, (g + 1) * half)
    return a_ref[span, :], b_ref[span, :]


def turn_kernel(scaled, a_ref, b_ref, m_ref, *rest):
    if scaled:
        sa_ref, sb_ref, oa_ref, ob_ref = rest
    else:
        oa_ref, ob_ref = rest
    groups = m_ref.shape[0]
    half = a_ref.shape[0] // groups
    for g in range(groups):
        x = jnp.concatenate(pieces(a_ref, b_ref, g, half), 0)
        hi, lo = m_ref[g, 0], m_ref[g, 1]
        if scaled == "before":
            x = x.astype(F32) * jnp.concatenate(pieces(sa_ref, sb_ref, g, half), 0)
            x, low = split(x)
            y = mm(hi, x) + (mm(lo, x) + mm(hi, low))
        else:
            y = mm(hi, x) + mm(lo, x)
        if scaled == "after":
            y = y * jnp.concatenate(pieces(sa_ref, sb_ref, g, half), 0)
        y = y.astype(BF16)
        oa_ref[g * half : (g + 1) * half, :] = y[:half]
        ob_ref[g * half : (g + 1) * half, :] = y[half:]


def turn(a, b, m, scaled=None, scales=()):
    shape = jax.ShapeDtypeStruct(a.shape, BF16)
    return pl.pallas_call(
        functools.partial(turn_kernel, scaled),
        out_shape=(shape, shape),
        in_specs=[VMEM] * (3 + len(scales)),
        out_specs=(VMEM, VMEM),
        compiler_params=PARAMS,
        cost_estimate=pl.CostEstimate(flops=2 * 10**8, bytes_accessed=3 * 10**6, transcendentals=0),
        name="turn",
    )(a, b, m, *scales)


def grad_kernel(norm, q1a, q1b, sa, sb, p1a, p1b, q0a, q0b, p0a, p0b, at_ref, po_ref, pit_ref, out_ref):
    groups = at_ref.shape[1]
    width = at_ref.shape[-1]
    n = width // GROUP
    half = q1a.shape[0] // groups
    r = lax.broadcasted_iota(jnp.int32, (width, width), 0)
    c = lax.broadcasted_iota(jnp.int32, (width, width), 1)
    same = (r % half) // (n // 2) == (c % half) // (n // 2)
    u = lax.broadcasted_iota(jnp.int32, (n, width), 0)
    v = lax.broadcasted_iota(jnp.int32, (n, width), 1) % n
    nt = (((1,), (1,)), ((), ()))
    for g in range(groups):
        dense = []
        for s in range(2):
            if s == 0:
                q = jnp.concatenate(pieces(q0a, q0b, g, half), 0)
                p = jnp.concatenate(pieces(p0a, p0b, g, half), 0)
            else:
                q = jnp.concatenate(pieces(q1a, q1b, g, half), 0).astype(F32)
                q = (q * jnp.concatenate(pieces(sa, sb, g, half), 0)).astype(BF16)
                p = jnp.concatenate(pieces(p1a, p1b, g, half), 0)
            cross = lax.dot_general(q, p, nt, preferred_element_type=F32)
            cross = jnp.where(same, cross, 0.0).astype(BF16)
            plain = mm(mm(po_ref[s], cross).astype(BF16), pit_ref[s]).astype(BF16)
            hi, lo = at_ref[s, g, 0], at_ref[s, g, 1]
            left = (mm(hi, plain) + mm(lo, plain)).astype(BF16)
            full = mm(left, hi) + mm(left, lo)
            full = (full - jnp.transpose(full)) * (-2.0 * norm)
            dense.append(full[:n] + full[n : 2 * n] + full[2 * n : 3 * n] + full[3 * n :])
        out_ref[g * n : (g + 1) * n, :] = jnp.where(u < v, dense[0], dense[1])


def hidden_kernel(at_ref, own_ref, r1, r2, r3, core_ref, w_ref, keep_ref, send_ref, x_all):
    size = own_ref.shape[1]

    @pl.when(pl.program_id(0) == 0)
    def _():
        zi, xi, ci = at_ref[0], at_ref[1], at_ref[2]
        for d in range(4):
            src = (own_ref, r1, r2, r3)[d]
            for r in range(4):
                place = ((zi ^ r) * 4 + (xi + 4 - d) % 4) * 2
                x_all[pl.ds(pl.multiple_of((place + ci) * size, 16), size), :] = src[r]
                x_all[pl.ds(pl.multiple_of((place + 1 - ci) * size, 16), size), :] = core_ref[d, r]

    y = mm(w_ref[...], x_all[...]).astype(BF16)
    upper = at_ref[0] >= 2
    blocks = y.shape[0] // 32
    y = y.reshape(blocks, 2, 16, y.shape[1])
    first, second = y[:, 0].reshape(-1, y.shape[3]), y[:, 1].reshape(-1, y.shape[3])
    keep_ref[...] = jnp.where(upper, second, first)
    send_ref[...] = jnp.where(upper, first, second)


def hidden_halves(place, own, r1, r2, r3, core, weight):
    rows, depth = weight.shape
    cols = own.shape[-1]
    steps = 4
    shape = jax.ShapeDtypeStruct((rows // 2, cols), BF16)
    out = pl.BlockSpec((rows // 2 // steps, cols), lambda i: (i, 0))
    return pl.pallas_call(
        hidden_kernel,
        grid=(steps,),
        out_shape=(shape, shape),
        in_specs=[SMEM] + [VMEM] * 5 + [pl.BlockSpec((rows // steps, depth), lambda i: (i, 0))],
        out_specs=(out, out),
        scratch_shapes=[pltpu.VMEM((depth, cols), BF16)],
        compiler_params=PARAMS,
        cost_estimate=pl.CostEstimate(
            flops=2 * rows * depth * cols, bytes_accessed=2 * rows * depth, transcendentals=0
        ),
        name="hidden",
    )(place, own, r1, r2, r3, core, weight)


def input_kernel(at_ref, own_ref, other_ref, w_ref, keep_ref, send_ref, gt):
    @pl.when(pl.program_id(0) == 0)
    def _():
        upper = at_ref[0] >= 2
        a, b = own_ref[...], other_ref[...]
        cols = a.shape[1]
        first = jnp.where(upper, b, a).reshape(-1, 1, 16, cols)
        second = jnp.where(upper, a, b).reshape(-1, 1, 16, cols)
        whole = jnp.concatenate([first, second], 1).reshape(-1, cols)
        gt[...] = jnp.transpose(whole)

    y = jnp.transpose(mm(gt[...], w_ref[...])).astype(BF16)
    size = keep_ref.shape[2]
    high = at_ref[2] == 1
    for x in range(4):
        lo = y[2 * x * size : (2 * x + 1) * size]
        hi = y[(2 * x + 1) * size : (2 * x + 2) * size]
        keep_ref[0, x] = jnp.where(high, hi, lo)
        send_ref[0, x] = jnp.where(high, lo, hi)


def input_parts(place, own, other, weight):
    rows, depth = weight.shape
    cols = own.shape[-1]
    steps = 4
    shape = jax.ShapeDtypeStruct((4, 4, depth // 32, cols), BF16)
    out = pl.BlockSpec((1, 4, depth // 32, cols), lambda i: (i, 0, 0, 0))
    return pl.pallas_call(
        input_kernel,
        grid=(steps,),
        out_shape=(shape, shape),
        in_specs=[SMEM] + [VMEM] * 2 + [pl.BlockSpec((rows, depth // steps), lambda i: (0, i))],
        out_specs=(out, out),
        scratch_shapes=[pltpu.VMEM((cols, rows), BF16)],
        compiler_params=PARAMS,
        cost_estimate=pl.CostEstimate(
            flops=2 * rows * depth * cols, bytes_accessed=2 * rows * depth, transcendentals=0
        ),
        name="input_sums",
    )(place, own, other, weight)


def halves(x, high):
    shaped = x.reshape(-1, 2, 16, x.shape[1])
    first, second = shaped[:, 0].reshape(-1, x.shape[1]), shaped[:, 1].reshape(-1, x.shape[1])
    return jnp.where(high, second, first), jnp.where(high, first, second)


def join(own, other, high):
    cols = own.shape[1]
    first = jnp.where(high, other, own).reshape(-1, 1, 16, cols)
    second = jnp.where(high, own, other).reshape(-1, 1, 16, cols)
    return jnp.concatenate([first, second], 1).reshape(-1, cols)


A_PAIRS = [(0, 0), (1, 2), (2, 1), (3, 3)]
B_PAIRS = [(0, 2), (1, 0), (2, 3), (3, 1)]
B_BACK = [(b, a) for a, b in B_PAIRS]


def per_device(responses, weight, skew, section_perm, prefix_ids, prefix_scale, out_grad):
    zi, xi, ci = lax.axis_index("z"), lax.axis_index("x"), lax.axis_index("c")
    yi = lax.axis_index("y")
    p, q = zi // 2, zi % 2
    place = jnp.stack([zi, xi, ci]).astype(jnp.int32)
    n = skew.shape[-1]
    width = GROUP * n
    mine = responses.T
    along_z = jnp.stack([mine] + [xor(mine, "z", k) for k in (1, 2, 3)])
    g_own, g_send = halves(out_grad, q == 1)
    g_rec = xor(g_send, "z", 1)
    scale_rec = xor(prefix_scale, "z", 1)
    x2 = shift(along_z, "x", 2)
    x1 = shift(along_z, "x", 1)
    x3 = shift(along_z, "x", 3)
    row = jnp.arange(width)
    slot, group_of = row // (width // 2), (row // 16) % GROUP

    def one_hot(s, bit):
        spot = (slot ^ bit) * 16 + row % 16
        target = jnp.tile(section_perm[s], GROUP)
        return (target[:, None] == spot[None, :]) & ((row // n)[:, None] == group_of[None, :])

    pi = jnp.stack([one_hot(0, p), one_hot(1, p)]).astype(BF16)
    po = jnp.stack([one_hot(0, q), one_hot(1, q)]).astype(BF16)
    pit, pot = jnp.swapaxes(pi, 1, 2), jnp.swapaxes(po, 1, 2)
    m, mt, at = rotations(skew, pi, pot)
    onehot = (prefix_ids[None, :] == jnp.arange(prefix_scale.shape[0], dtype=jnp.int32)[:, None]).astype(F32)

    def rows_of(table):
        return lax.dot_general(table, onehot, (((0,), (0,)), ((), ())), precision=lax.Precision.HIGHEST)

    s_own, _ = halves(rows_of(prefix_scale), q == 1)
    s_rec, _ = halves(rows_of(scale_rec), q == 1)
    ga, gb = turn(g_own, g_rec, mt[1], "before", (s_own, s_rec))
    ga = lax.ppermute(ga, "z", A_PAIRS)
    gb = lax.ppermute(gb, "z", B_BACK)
    by_x = jnp.stack([along_z, x1, x2, x3])
    by_core = xor(by_x, "c", 1)
    z_own, z_send = hidden_halves(place, along_z, x1, x2, x3, by_core, weight)
    z_rec = xor(z_send, "z", 2)
    h_own, h_send = turn(ga, gb, mt[0])
    h_rec = xor(h_send, "z", 2)
    za, zb = turn(z_own, z_rec, m[0])
    za = lax.ppermute(za, "z", A_PAIRS)
    zb = lax.ppermute(zb, "z", B_PAIRS)
    keep, send = input_parts(place, h_own, h_rec, weight)
    part = keep.astype(F32) + xor(send, "c", 1).astype(F32)
    part_bf = part.astype(BF16)

    def for_x(d):
        return lax.dynamic_index_in_dim(part_bf, (xi + d) % 4, 1, keepdims=False)

    total = lax.dynamic_index_in_dim(part, xi, 1, keepdims=False)
    total = total + sum(shift(for_x(d), "x", d).astype(F32) for d in (2, 1, 3))
    total_bf = total.astype(BF16)
    final = lax.dynamic_index_in_dim(total, zi, 0, keepdims=False)
    final = final + sum(
        xor(lax.dynamic_index_in_dim(total_bf, zi ^ k, 0, keepdims=False), "z", k).astype(F32)
        for k in (1, 2, 3)
    )
    input_grad = final.astype(BF16)
    j_own, j_send = turn(za, zb, m[1], "after", (s_own, s_rec))
    j_rec = xor(j_send, "z", 1)
    judged = join(j_own, j_rec, q == 1)
    rows_all = responses.shape[0] * lax.axis_size("y") * lax.axis_size("h")
    partial = pl.pallas_call(
        functools.partial(grad_kernel, 1.0 / rows_all**0.5),
        out_shape=jax.ShapeDtypeStruct((m.shape[1] * n, width), F32),
        in_specs=[VMEM] * 13,
        out_specs=VMEM,
        compiler_params=PARAMS,
        cost_estimate=pl.CostEstimate(flops=10**9, bytes_accessed=5 * 10**6, transcendentals=0),
        name="rotation_grad",
    )(g_own, g_rec, s_own, s_rec, za, zb, ga, gb, z_own, z_rec, at, po, pit)
    y0, y1 = yi % 2, yi // 2
    part4 = partial.reshape(2, 2, -1, width)
    half = lax.dynamic_index_in_dim(part4, y0, 0, keepdims=False)
    half = half + xor(lax.dynamic_index_in_dim(part4, 1 - y0, 0, keepdims=False), "y", 1)
    quarter = lax.dynamic_index_in_dim(half, y1, 0, keepdims=False)
    quarter = quarter + xor(lax.dynamic_index_in_dim(half, 1 - y1, 0, keepdims=False), "y", 2)
    quarter = quarter + xor(quarter, "h", 1)
    other = xor(quarter, "y", 2)
    half = jnp.where(y1 == 0, jnp.stack([quarter, other]), jnp.stack([other, quarter]))
    other = xor(half, "y", 1)
    summed = jnp.where(y0 == 0, jnp.stack([half, other]), jnp.stack([other, half]))
    packed = summed.reshape(-1, n, GROUP, n).transpose(1, 3, 0, 2).reshape(n, n, -1)
    u = jnp.arange(n)[:, None, None]
    v = jnp.arange(n)[None, :, None]
    upper = jnp.where(u < v, packed, 0.0)
    lower = jnp.where(u > v, packed, 0.0)
    both = jnp.stack([upper - jnp.swapaxes(upper, 0, 1), lower - jnp.swapaxes(lower, 0, 1)])
    return judged, input_grad, jnp.transpose(both, (0, 3, 1, 2))


def solution(mesh):
    wide = Mesh(mesh.devices.reshape(4, 2, 4, 4, 2), ("y", "h", "z", "x", "c"))
    dp, mp = ("y", "h"), ("z", "x", "c")
    in_specs = (
        P(dp, mp),
        P(mp, None),
        P(None, mp, None, None),
        P(),
        P(dp),
        P(None, mp),
        P(mp, dp),
    )
    out_specs = (P(mp, dp), P(mp, dp), P(None, mp, None, None))
    return jax.shard_map(per_device, mesh=wide, in_specs=in_specs, out_specs=out_specs, check_vma=False)
```

time: 768 us -> 169 us (0.22)
  other arithmetic: 296 us -> 11.2 us
  waiting for transfers between devices: 253 us -> 41.4 us
  local copies, waits for them, and re-layouts: 102 us -> 15.1 us
  matrix products: 81.9 us -> 2.22 us
  Pallas kernels: 0 us -> 49.4 us
  starting transfers between devices: 14.4 us -> 47.7 us
  between operations: 14.8 us -> 0.99 us
    another operation x9 -> x5, other arithmetic: 269 us -> 2.14 us  [the longest x2 1.31 us: per_device(): by_x = jnp.stack([along_z, x1, x2, x3])]
    ppermute x8 -> x28, waiting for transfers between devices: 121 us -> 41.4 us  [the longest x18 19 us: xor(): lax.ppermute(x, axis, [(i, i ^ k) for i in range(lax.axis_size(axis))])]
    psum x1 -> x0, waiting for transfers between devices: 71.7 us -> none  [per_device(): section_grads[section] = lax.psum(partial_grad, 'dp')]
    unnamed x4 -> x0, waiting for transfers between devices: 60.2 us -> none
    dot_general x22 -> x2, matrix products: 59.6 us -> 2.22 us  [rows_of(): lax.dot_general(table, onehot, (((0,), (0,)), ((), ())), precision=lax.Pr...]
    pallas_call x0 -> x8, Pallas kernels: none -> 49.4 us  [the longest x1 11.6 us: per_device(): pl.pallas_call(functools.partial(grad_kernel, 1.0 / rows_all ** 0.5), out...]
    ppermute x8 -> x28, starting transfers between devices: 14.3 us -> 47.7 us  [the longest x18 32.1 us: xor(): lax.ppermute(x, axis, [(i, i ^ k) for i in range(lax.axis_size(axis))])]
    another operation x10 -> x3, local copies, waits for them, and re-layouts: 23.5 us -> 0.01 us  [one_hot(): target = jnp.tile(section_perm[s], GROUP)]
  transfers between devices with their start and end apart: 11 -> 28, of which waited for: 10 -> 8; matrix products, arithmetic and copies ran while one was open for 58% -> 14% of each run, Pallas kernels for 0% -> 29%
where the time goes in v1:
time: 169 us; the launch traced here: 168 us
  Pallas kernels  49.4 us (29%)
  starting transfers between devices  47.7 us (28%)
  waiting for transfers between devices  41.4 us (24%)
  local copies, waits for them, and re-layouts  15.1 us (9%)
  other arithmetic  11.2 us (7%)
  matrix products  2.22 us (1%)
    ppermute x18, starting transfers between devices, xor(): lax.ppermute(x, axis, [(i, i ^ k) for i in range(lax.axis_size(axis))])  32.1 us
    ppermute x18, waiting for transfers between devices, xor(): lax.ppermute(x, axis, [(i, i ^ k) for i in range(lax.axis_size(axis))])  19 us
    ppermute x1, waiting for transfers between devices, per_device(): gb = lax.ppermute(gb, 'z', B_BACK)  13.3 us
    pallas_call x1, Pallas kernels, per_device(): pl.pallas_call(functools.partial(grad_kernel, 1.0 / rows_all ** 0.5), out...  11.6 us
    pallas_call x4, Pallas kernels, turn(): pl.pallas_call(functools.partial(turn_kernel, scaled), out_shape=(shape,...  10.9 us
    pallas_call x1, Pallas kernels, rotations(): pl.pallas_call(rot_kernel, out_shape=(shape, shape, shape), in_specs=[VME...  10.4 us
    pallas_call x1, Pallas kernels, input_parts(): pl.pallas_call(input_kernel, grid=(steps,), out_shape=(shape, shape), in_...  8.52 us
    ppermute x1, waiting for transfers between devices, per_device(): zb = lax.ppermute(zb, 'z', B_PAIRS)  8.37 us
  transfers between devices with their start and end apart: 28, of which 8 were waited for; matrix products, arithmetic and copies ran while one was open for 14% of the time, Pallas kernels for 29%

profile of v1, /device:TPU:24, one launch (start us, length us, event | category | flops | bytes accessed | tf_op | source)
XLA Modules:
  0.0 168.0 jit_solution(6999698441421849336)
XLA Ops:
  0.7 3.4 %collective-permute-start.1 = (bf16[144,256]{1,0:T(8,128)(2,1)}, bf16[144,256]{1,0:T(8,128)(2,1)S(1)}, u32[]{:S(2)}, u32[]{:S(2)}) collective-permute-start(bf16[144,256]{1,0:T(8,128)(2,1)} %bitcast.130), channel_id=1, source_target_pairs={{0,16},{8,24},{16,0},{24,8},{1,17},{9,25},{17,1},{25,9},{2,18},{10... | collective-permute-start | bytes 221192 | tf_op jit(solution)/shard_map/ppermute | solution.py:21
  4.0 1.9 %collective-permute-start = (bf16[144,256]{1,0:T(8,128)(2,1)}, bf16[144,256]{1,0:T(8,128)(2,1)S(1)}, u32[]{:S(2)}, u32[]{:S(2)}) collective-permute-start(bf16[144,256]{1,0:T(8,128)(2,1)} %bitcast.131), channel_id=1, source_target_pairs={{0,8},{8,0},{16,24},{24,16},{1,9},{9,1},{17,25},{25,17},{2,10},{10... | collective-permute-start | bytes 221192 | tf_op jit(solution)/shard_map/ppermute | solution.py:21
  5.9 0.7 collective-permute-start.10
  6.6 1.9 %broadcast_select_fusion = (bf16[36,1,16,256]{3,2,1,0:T(8,128)(2,1)}, bf16[36,1,16,256]{3,2,1,0:T(8,128)(2,1)}) fusion(pred[]{:T(512)S(6)} %eq.184, bf16[36,2,16,256]{3,2,1,0:T(8,128)(2,1)} %bitcast.124), kind=kLoop, calls=%fused_computation.23 | loop fusion | flops 294912 | bytes 1179649 | tf_op jit(solution)/shard_map/jit(_where)/select_n | solution.py:271
  8.5 1.4 collective-permute-start.12
  10.2 0.7 fusion.8
  10.9 0.7 copy.22.pi_ref
  11.6 0.7 add_convert_fusion.1
  12.5 2.8 %collective-permute-start.5 = (bf16[4,144,256]{2,1,0:T(8,128)(2,1)S(1)}, bf16[4,144,256]{2,1,0:T(8,128)(2,1)S(1)}, u32[]{:S(2)}, u32[]{:S(2)}) collective-permute-start(bf16[4,144,256]{2,1,0:T(8,128)(2,1)S(1)} %get-tuple-element.55.own_ref), channel_id=1, source_target_pairs={{0,6},{2,0},{4,2},{6,4},{1,7},{3,1},{5,3},{7,5},{8,14},{10,8},{12,... | collective-permute-start | bytes 884744 | tf_op jit(solution)/shard_map/ppermute | solution.py:26
  15.3 0.8 collective-permute-start.4
  16.1 0.9 collective-permute-start.3
  17.0 10.4 %rotations.1 = (bf16[2,9,2,128,128]{4,3,2,1,0:T(8,128)(2,1)}, bf16[2,9,2,128,128]{4,3,2,1,0:T(8,128)(2,1)}, bf16[2,9,2,128,128]{4,3,2,1,0:T(8,128)(2,1)}) custom-call(f32[2,32,32,36]{3,2,1,0:T(8,128)} %bitcast.138, bf16[2,128,128]{2,1,0:T(8,128)(2,1)} %copy.22.pi_ref, bf16[2,128,128]{2,1,0:T(8,128)(2,1)} %get-tuple-element.59.pot_ref), custom_call_target="tpu_custom_call" | custom-call | flops 1000000000 | bytes 4000000 | tf_op jit(solution)/shard_map/rotations/pallas_call | solution.py:94
  27.4 2.4 %slice_bitcast_fusion = (bf16[9,2,128,128]{3,2,1,0:T(8,128)(2,1)}, bf16[9,2,128,128]{3,2,1,0:T(8,128)(2,1)}) fusion(bf16[2,9,2,128,128]{4,3,2,1,0:T(8,128)(2,1)} %get-tuple-element.25), kind=kLoop, calls=%fused_computation.15 | loop fusion | bytes 2359296 | tf_op jit(solution)/shard_map/squeeze | solution.py:327
  29.8 0.6 collective-permute-done.3.r1
  30.4 1.3 pad_maximum_fusion
  31.8 0.7 convolution_bitcast_fusion.1
  32.5 0.4 copy.23
  32.8 1.6 convolution_bitcast_fusion
  34.4 0.4 copy.24
  34.8 1.3 slice_select_fusion
  36.1 3.1 %turn.6 = (bf16[576,256]{1,0:T(8,128)(2,1)}, bf16[576,256]{1,0:T(8,128)(2,1)}) custom-call(bf16[576,256]{1,0:T(8,128)(2,1)} %bitcast.115, bf16[576,256]{1,0:T(8,128)(2,1)} %collective-permute-done.12.b_ref.q1b, bf16[9,2,128,128]{3,2,1,0:T(8,128)(2,1)} %get-tuple-element.44.m_ref, f32[576,256]{1,0:T(8,128)} %bitcast.108, f32[576,256]{1,0:T(8,128)} %bitcast.105), custom_call_target="tpu_custom_call" | custom-call | flops 200000000 | bytes 3000000 | tf_op jit(solution)/shard_map/turn/pallas_call | solution.py:140
  39.1 1.6 collective-permute-start.13
  40.7 3.5 %collective-permute-start.14 = (bf16[576,256]{1,0:T(8,128)(2,1)}, bf16[576,256]{1,0:T(8,128)(2,1)S(1)}, u32[]{:S(2)}, u32[]{:S(2)}) collective-permute-start(bf16[576,256]{1,0:T(8,128)(2,1)} %get-tuple-element.27), channel_id=1, source_target_pairs={{16,0},{0,8},{24,16},{8,24},{17,1},{1,9},{25,17},{9,25},{18,2},{2,... | collective-permute-start | bytes 884744 | tf_op jit(solution)/shard_map/ppermute | solution.py:322
  44.3 13.3 %collective-permute-done.14.b_ref.q0b = bf16[576,256]{1,0:T(8,128)(2,1)S(1)} collective-permute-done((bf16[576,256]{1,0:T(8,128)(2,1)}, bf16[576,256]{1,0:T(8,128)(2,1)S(1)}, u32[]{:S(2)}, u32[]{:S(2)}) %collective-permute-start.14) | collective-permute-done | bytes 294944 | tf_op jit(solution)/shard_map/ppermute | solution.py:322
  57.6 0.7 copy-done.7
  58.4 2.5 %turn.7 = (bf16[576,256]{1,0:T(8,128)(2,1)}, bf16[576,256]{1,0:T(8,128)(2,1)}) custom-call(bf16[576,256]{1,0:T(8,128)(2,1)} %copy-done.6, bf16[576,256]{1,0:T(8,128)(2,1)} %copy-done.7, bf16[9,2,128,128]{3,2,1,0:T(8,128)(2,1)} %get-tuple-element.43.m_ref), custom_call_target="tpu_custom_call" | custom-call | flops 200000000 | bytes 3000000 | tf_op jit(solution)/shard_map/turn/pallas_call | solution.py:140
  60.8 0.6 pad_add_fusion.at_ref
  61.5 7.9 %hidden.1 = (bf16[576,256]{1,0:T(8,128)(2,1)}, bf16[576,256]{1,0:T(8,128)(2,1)}) custom-call(s32[3]{0:T(128)} %pad_add_fusion.at_ref, bf16[4,144,256]{2,1,0:T(8,128)(2,1)} %copy-done.5, bf16[4,144,256]{2,1,0:T(8,128)(2,1)} %copy-done.4, bf16[4,144,256]{2,1,0:T(8,128)(2,1)} %copy-done.3, bf16[4,144,256]{2,1,0:T(8,128)(2,1)} %copy-done.2, ...), custom_call_target="tpu_custom_call" | custom-call | flops 2717908992 | bytes 10616832 | tf_op jit(solution)/shard_map/hidden/pallas_call | solution.py:211
  69.4 2.9 %collective-permute-start.7 = (bf16[576,256]{1,0:T(8,128)(2,1)}, bf16[576,256]{1,0:T(8,128)(2,1)S(1)}, u32[]{:S(2)}, u32[]{:S(2)}) collective-permute-start(bf16[576,256]{1,0:T(8,128)(2,1)} %get-tuple-element.19), channel_id=1, source_target_pairs={{0,16},{8,24},{16,0},{24,8},{1,17},{9,25},{17,1},{25,9},{2,18},{10... | collective-permute-start | bytes 884744 | tf_op jit(solution)/shard_map/ppermute | solution.py:21
  72.3 11.0 %collective-permute-done.15.other_ref = bf16[576,256]{1,0:T(8,128)(2,1)S(1)} collective-permute-done((bf16[576,256]{1,0:T(8,128)(2,1)}, bf16[576,256]{1,0:T(8,128)(2,1)S(1)}, u32[]{:S(2)}, u32[]{:S(2)}) %collective-permute-start.15) | collective-permute-done | bytes 294944 | tf_op jit(solution)/shard_map/ppermute | solution.py:21
  83.3 0.7 copy-done.12
  84.0 8.5 %input_sums.1 = (bf16[4,4,144,256]{3,2,1,0:T(8,128)(2,1)}, bf16[4,4,144,256]{3,2,1,0:T(8,128)(2,1)}) custom-call(s32[3]{0:T(128)} %pad_add_fusion.at_ref, bf16[576,256]{1,0:T(8,128)(2,1)} %get-tuple-element.28.own_ref, bf16[576,256]{1,0:T(8,128)(2,1)} %copy-done.12, bf16[1152,4608]{1,0:T(8,128)(2,1)} %w_ref.3), custom_call_target="tpu_custom_call" | custom-call | flops 2717908992 | bytes 10616832 | tf_op jit(solution)/shard_map/input_sums/pallas_call | solution.py:253
  92.5 1.1 slice_bitcast_fusion.2
  93.7 0.7 copy-done.8
  94.4 2.5 %turn.4 = (bf16[576,256]{1,0:T(8,128)(2,1)}, bf16[576,256]{1,0:T(8,128)(2,1)}) custom-call(bf16[576,256]{1,0:T(8,128)(2,1)} %get-tuple-element.18.a_ref.p0a, bf16[576,256]{1,0:T(8,128)(2,1)} %copy-done.8, bf16[9,2,128,128]{3,2,1,0:T(8,128)(2,1)} %get-tuple-element.46.m_ref), custom_call_target="tpu_custom_call" | custom-call | flops 200000000 | bytes 3000000 | tf_op jit(solution)/shard_map/turn/pallas_call | solution.py:140
  96.9 1.6 collective-permute-start.8
  98.5 0.5 collective-permute-start.9
  99.0 0.7 copy.26.po_ref
  99.8 8.4 %collective-permute-done.9.b_ref.p1b = bf16[576,256]{1,0:T(8,128)(2,1)S(1)} collective-permute-done((bf16[576,256]{1,0:T(8,128)(2,1)}, bf16[576,256]{1,0:T(8,128)(2,1)S(1)}, u32[]{:S(2)}, u32[]{:S(2)}) %collective-permute-start.9) | collective-permute-done | bytes 294944 | tf_op jit(solution)/shard_map/ppermute | solution.py:331
  108.1 0.7 copy-done.1
  108.9 11.6 %rotation_grad.1 = f32[288,128]{1,0:T(8,128)} custom-call(bf16[576,256]{1,0:T(8,128)(2,1)} %bitcast.116, bf16[576,256]{1,0:T(8,128)(2,1)} %collective-permute-done.12.b_ref.q1b, f32[576,256]{1,0:T(8,128)} %bitcast.109, f32[576,256]{1,0:T(8,128)} %bitcast.106, bf16[576,256]{1,0:T(8,128)(2,1)} %copy-done, bf16[576,256]{1,0:T(8,128)(2,1)} %copy-done.1, ...), custom_call_target="tpu_custom_call" | custom-call | flops 1000000000 | bytes 5000000 | tf_op jit(solution)/shard_map/rotation_grad/pallas_call | solution.py:352
  120.5 0.9 dynamic-slice_bitcast_fusion.3
  121.4 0.7 collective-permute-start.23
  122.2 3.6 %collective-permute-done.23 = f32[2,72,128]{2,1,0:T(8,128)S(1)} collective-permute-done((f32[2,72,128]{2,1,0:T(8,128)S(1)}, f32[2,72,128]{2,1,0:T(8,128)S(1)}, u32[]{:S(2)}, u32[]{:S(2)}) %collective-permute-start.23) | collective-permute-done | bytes 73760 | tf_op jit(solution)/shard_map/ppermute | solution.py:21
  125.8 0.9 bitcast_add_fusion.2
  126.7 1.3 collective-permute-start.24
  128.0 0.4 convert_add_fusion
  128.3 3.9 %collective-permute-done.24 = f32[72,128]{1,0:T(8,128)S(1)} collective-permute-done((f32[72,128]{1,0:T(8,128)S(1)}, f32[72,128]{1,0:T(8,128)S(1)}, u32[]{:S(2)}, u32[]{:S(2)}) %collective-permute-start.24) | collective-permute-done | bytes 36896 | tf_op jit(solution)/shard_map/ppermute | solution.py:21
  132.2 4.5 %collective-permute-start.25 = (f32[72,128]{1,0:T(8,128)S(1)}, f32[72,128]{1,0:T(8,128)S(1)}, u32[]{:S(2)}, u32[]{:S(2)}) collective-permute-start(f32[72,128]{1,0:T(8,128)S(1)} %bitcast_add_fusion.3), channel_id=1, source_target_pairs={{0,32},{32,0},{1,33},{33,1},{2,34},{34,2},{3,35},{35,3},{4,36},{36... | collective-permute-start | bytes 110600 | tf_op jit(solution)/shard_map/ppermute | solution.py:21
  136.8 1.0 dynamic-slice_bitcast_fusion.2
  137.7 1.2 collective-permute-start.17
  138.9 2.6 %collective-permute-start.19 = (bf16[4,144,256]{2,1,0:T(8,128)(2,1)}, bf16[4,144,256]{2,1,0:T(8,128)(2,1)S(1)}, u32[]{:S(2)}, u32[]{:S(2)}) collective-permute-start(bf16[4,144,256]{2,1,0:T(8,128)(2,1)} %get-tuple-element.41), channel_id=1, source_target_pairs={{0,6},{2,0},{4,2},{6,4},{1,7},{3,1},{5,3},{7,5},{8,14},{10,8},{12,... | collective-permute-start | bytes 884744 | tf_op jit(solution)/shard_map/ppermute | solution.py:26
  141.6 1.3 collective-permute-start.26
  142.9 2.9 %turn.5 = (bf16[576,256]{1,0:T(8,128)(2,1)}, bf16[576,256]{1,0:T(8,128)(2,1)}) custom-call(bf16[576,256]{1,0:T(8,128)(2,1)} %copy-done, bf16[576,256]{1,0:T(8,128)(2,1)} %copy-done.1, bf16[9,2,128,128]{3,2,1,0:T(8,128)(2,1)} %get-tuple-element.45.m_ref, f32[576,256]{1,0:T(8,128)} %bitcast.110, f32[576,256]{1,0:T(8,128)} %bitcast.107), custom_call_target="tpu_custom_call" | custom-call | flops 200000000 | bytes 3000000 | tf_op jit(solution)/shard_map/turn/pallas_call | solution.py:140
  145.7 5.9 %collective-permute-start.11 = (bf16[576,256]{1,0:T(8,128)(2,1)}, bf16[576,256]{1,0:T(8,128)(2,1)}, u32[]{:S(2)}, u32[]{:S(2)}) collective-permute-start(bf16[576,256]{1,0:T(8,128)(2,1)} %get-tuple-element.23), channel_id=1, source_target_pairs={{0,8},{8,0},{16,24},{24,16},{1,9},{9,1},{17,25},{25,17},{2,10},{10... | collective-permute-start | bytes 884744 | tf_op jit(solution)/shard_map/ppermute | solution.py:21
  151.8 0.7 copy-done.11
  152.5 1.1 fusion.11
  153.7 5.9 %collective-permute-start.20 = (bf16[144,256]{1,0:T(8,128)(2,1)S(1)}, bf16[144,256]{1,0:T(8,128)(2,1)S(1)}, u32[]{:S(2)}, u32[]{:S(2)}) collective-permute-start(bf16[144,256]{1,0:T(8,128)(2,1)S(1)} %get-tuple-element.51), channel_id=1, source_target_pairs={{0,8},{8,0},{16,24},{24,16},{1,9},{9,1},{17,25},{25,17},{2,10},{10... | collective-permute-start | bytes 221192 | tf_op jit(solution)/shard_map/ppermute | solution.py:21
  159.6 2.0 %collective-permute-start.22 = (bf16[144,256]{1,0:T(8,128)(2,1)S(1)}, bf16[144,256]{1,0:T(8,128)(2,1)S(1)}, u32[]{:S(2)}, u32[]{:S(2)}) collective-permute-start(bf16[144,256]{1,0:T(8,128)(2,1)S(1)} %get-tuple-element.52), channel_id=1, source_target_pairs={{0,24},{8,16},{16,8},{24,0},{1,25},{9,17},{17,9},{25,1},{2,26},{10... | collective-permute-start | bytes 221192 | tf_op jit(solution)/shard_map/ppermute | solution.py:21
  163.1 1.8 %copy.32 = f32[2,36,32,32]{1,3,2,0:T(8,128)} copy(f32[2,36,32,32]{3,2,1,0:T(8,128)S(1)} %maximum_bitcast_fusion) | data formatting | bytes 589824
  164.9 1.0 broadcast_select_fusion.3
  166.0 0.9 copy.25
  166.9 0.4 collective-permute-done.21
  167.3 0.7 fusion.2
  (90 shorter events, 2.4 us)
Async XLA Ops:
  0.6 11.8 %copy-start.15 = (bf16[256,144]{0,1:T(8,128)(2,1)S(1)}, bf16[256,144]{0,1:T(8,128)(2,1)}, u32[]{:S(2)}) copy-start(bf16[256,144]{0,1:T(8,128)(2,1)} %param.7) | copy-start | bytes 221188
  0.6 9.3 %copy-start.18 = (s32[2,32]{1,0:T(2,128)S(1)}, s32[2,32]{1,0:T(2,128)}, u32[]{:S(2)}) copy-start(s32[2,32]{1,0:T(2,128)} %param.10) | copy-start | bytes 772
  0.7 11.6 %collective-permute-start.1 = (bf16[144,256]{1,0:T(8,128)(2,1)}, bf16[144,256]{1,0:T(8,128)(2,1)S(1)}, u32[]{:S(2)}, u32[]{:S(2)}) collective-permute-start(bf16[144,256]{1,0:T(8,128)(2,1)} %bitcast.130), channel_id=1, source_target_pairs={{0,16},{8,24},{16,0},{24,8},{1,17},{9,25},{17,1},{25,9},{2,18},{10... | collective-permute-start | bytes 221192 | tf_op jit(solution)/shard_map/ppermute | solution.py:21
  4.0 8.3 %collective-permute-start = (bf16[144,256]{1,0:T(8,128)(2,1)}, bf16[144,256]{1,0:T(8,128)(2,1)S(1)}, u32[]{:S(2)}, u32[]{:S(2)}) collective-permute-start(bf16[144,256]{1,0:T(8,128)(2,1)} %bitcast.131), channel_id=1, source_target_pairs={{0,8},{8,0},{16,24},{24,16},{1,9},{9,1},{17,25},{25,17},{2,10},{10... | collective-permute-start | bytes 221192 | tf_op jit(solution)/shard_map/ppermute | solution.py:21
  5.9 6.5 %collective-permute-start.2 = (bf16[144,256]{1,0:T(8,128)(2,1)}, bf16[144,256]{1,0:T(8,128)(2,1)S(1)}, u32[]{:S(2)}, u32[]{:S(2)}) collective-permute-start(bf16[144,256]{1,0:T(8,128)(2,1)} %bitcast.132), channel_id=1, source_target_pairs={{0,24},{8,16},{16,8},{24,0},{1,25},{9,17},{17,9},{25,1},{2,26},{10... | collective-permute-start | bytes 221192 | tf_op jit(solution)/shard_map/ppermute | solution.py:21
  5.9 26.9 %collective-permute-start.10 = (f32[16,1152]{1,0:T(8,128)}, f32[16,1152]{1,0:T(8,128)}, u32[]{:S(2)}, u32[]{:S(2)}) collective-permute-start(f32[16,1152]{1,0:T(8,128)} %param.12), channel_id=1, source_target_pairs={{0,8},{8,0},{16,24},{24,16},{1,9},{9,1},{17,25},{25,17},{2,10},{10... | collective-permute-start | bytes 221192 | tf_op jit(solution)/shard_map/ppermute | solution.py:21
  8.5 27.6 %collective-permute-start.12 = (bf16[576,256]{1,0:T(8,128)(2,1)}, bf16[576,256]{1,0:T(8,128)(2,1)}, u32[]{:S(2)}, u32[]{:S(2)}) collective-permute-start(bf16[576,256]{1,0:T(8,128)(2,1)} %bitcast.29), channel_id=1, source_target_pairs={{0,8},{8,0},{16,24},{24,16},{1,9},{9,1},{17,25},{25,17},{2,10},{10... | collective-permute-start | bytes 884744 | tf_op jit(solution)/shard_map/ppermute | solution.py:21
  12.5 14.9 %copy-start.5 = (bf16[4,144,256]{2,1,0:T(8,128)(2,1)}, bf16[4,144,256]{2,1,0:T(8,128)(2,1)S(1)}, u32[]{:S(2)}) copy-start(bf16[4,144,256]{2,1,0:T(8,128)(2,1)S(1)} %get-tuple-element.55.own_ref) | copy-start | bytes 884740
  12.5 17.3 %collective-permute-start.5 = (bf16[4,144,256]{2,1,0:T(8,128)(2,1)S(1)}, bf16[4,144,256]{2,1,0:T(8,128)(2,1)S(1)}, u32[]{:S(2)}, u32[]{:S(2)}) collective-permute-start(bf16[4,144,256]{2,1,0:T(8,128)(2,1)S(1)} %get-tuple-element.55.own_ref), channel_id=1, source_target_pairs={{0,6},{2,0},{4,2},{6,4},{1,7},{3,1},{5,3},{7,5},{8,14},{10,8},{12,... | collective-permute-start | bytes 884744 | tf_op jit(solution)/shard_map/ppermute | solution.py:26
  15.3 14.5 %collective-permute-start.4 = (bf16[4,144,256]{2,1,0:T(8,128)(2,1)S(1)}, bf16[4,144,256]{2,1,0:T(8,128)(2,1)S(1)}, u32[]{:S(2)}, u32[]{:S(2)}) collective-permute-start(bf16[4,144,256]{2,1,0:T(8,128)(2,1)S(1)} %get-tuple-element.55.own_ref), channel_id=1, source_target_pairs={{0,4},{2,6},{4,0},{6,2},{1,5},{3,7},{5,1},{7,3},{8,12},{10,14},{12... | collective-permute-start | bytes 884744 | tf_op jit(solution)/shard_map/ppermute | solution.py:26
  16.1 14.3 %collective-permute-start.3 = (bf16[4,144,256]{2,1,0:T(8,128)(2,1)S(1)}, bf16[4,144,256]{2,1,0:T(8,128)(2,1)S(1)}, u32[]{:S(2)}, u32[]{:S(2)}) collective-permute-start(bf16[4,144,256]{2,1,0:T(8,128)(2,1)S(1)} %get-tuple-element.55.own_ref), channel_id=1, source_target_pairs={{0,2},{2,4},{4,6},{6,0},{1,3},{3,5},{5,7},{7,1},{8,10},{10,12},{12... | collective-permute-start | bytes 884744 | tf_op jit(solution)/shard_map/ppermute | solution.py:26
  29.8 1.9 %copy-start.2 = (bf16[4,144,256]{2,1,0:T(8,128)(2,1)}, bf16[4,144,256]{2,1,0:T(8,128)(2,1)S(1)}, u32[]{:S(2)}) copy-start(bf16[4,144,256]{2,1,0:T(8,128)(2,1)S(1)} %collective-permute-done.5.r3) | copy-start | bytes 884740
  29.8 1.9 %copy-start.3 = (bf16[4,144,256]{2,1,0:T(8,128)(2,1)}, bf16[4,144,256]{2,1,0:T(8,128)(2,1)S(1)}, u32[]{:S(2)}) copy-start(bf16[4,144,256]{2,1,0:T(8,128)(2,1)S(1)} %collective-permute-done.4.r2) | copy-start | bytes 884740
  30.4 1.3 copy-start.4
  30.4 1.4 copy-start.16
  30.4 1.4 copy-start.17
  31.7 29.8 %collective-permute-start.6 = (bf16[4,4,144,256]{3,2,1,0:T(8,128)(2,1)}, bf16[4,4,144,256]{3,2,1,0:T(8,128)(2,1)}, u32[]{:S(2)}, u32[]{:S(2)}) collective-permute-start(bf16[4,4,144,256]{3,2,1,0:T(8,128)(2,1)} %pad_maximum_fusion), channel_id=1, source_target_pairs={{0,1},{1,0},{2,3},{3,2},{4,5},{5,4},{6,7},{7,6},{8,9},{9,8},{10,11... | collective-permute-start | bytes 3538952 | tf_op jit(solution)/shard_map/ppermute | solution.py:21
  39.1 5.1 %collective-permute-start.13 = (bf16[576,256]{1,0:T(8,128)(2,1)}, bf16[576,256]{1,0:T(8,128)(2,1)S(1)}, u32[]{:S(2)}, u32[]{:S(2)}) collective-permute-start(bf16[576,256]{1,0:T(8,128)(2,1)} %get-tuple-element.26), channel_id=1, source_target_pairs={{0,0},{8,16},{16,8},{24,24},{1,1},{9,17},{17,9},{25,25},{2,2},{10,... | collective-permute-start | bytes 884744 | tf_op jit(solution)/shard_map/ppermute | solution.py:321
  40.7 16.9 %collective-permute-start.14 = (bf16[576,256]{1,0:T(8,128)(2,1)}, bf16[576,256]{1,0:T(8,128)(2,1)S(1)}, u32[]{:S(2)}, u32[]{:S(2)}) collective-permute-start(bf16[576,256]{1,0:T(8,128)(2,1)} %get-tuple-element.27), channel_id=1, source_target_pairs={{16,0},{0,8},{24,16},{8,24},{17,1},{1,9},{25,17},{9,25},{18,2},{2,... | collective-permute-start | bytes 884744 | tf_op jit(solution)/shard_map/ppermute | solution.py:322
  44.3 13.4 %copy-start.6 = (bf16[576,256]{1,0:T(8,128)(2,1)}, bf16[576,256]{1,0:T(8,128)(2,1)S(1)}, u32[]{:S(2)}) copy-start(bf16[576,256]{1,0:T(8,128)(2,1)S(1)} %collective-permute-done.13.a_ref.q0a) | copy-start | bytes 884740
  57.6 0.7 copy-start.7
  60.8 22.5 %collective-permute-start.15 = (bf16[576,256]{1,0:T(8,128)(2,1)}, bf16[576,256]{1,0:T(8,128)(2,1)S(1)}, u32[]{:S(2)}, u32[]{:S(2)}) collective-permute-start(bf16[576,256]{1,0:T(8,128)(2,1)} %get-tuple-element.29), channel_id=1, source_target_pairs={{0,16},{8,24},{16,0},{24,8},{1,17},{9,25},{17,1},{25,9},{2,18},{10... | collective-permute-start | bytes 884744 | tf_op jit(solution)/shard_map/ppermute | solution.py:21
  69.4 24.3 %collective-permute-start.7 = (bf16[576,256]{1,0:T(8,128)(2,1)}, bf16[576,256]{1,0:T(8,128)(2,1)S(1)}, u32[]{:S(2)}, u32[]{:S(2)}) collective-permute-start(bf16[576,256]{1,0:T(8,128)(2,1)} %get-tuple-element.19), channel_id=1, source_target_pairs={{0,16},{8,24},{16,0},{24,8},{1,17},{9,25},{17,1},{25,9},{2,18},{10... | collective-permute-start | bytes 884744 | tf_op jit(solution)/shard_map/ppermute | solution.py:21
  83.3 0.7 copy-start.12
  84.0 8.5 %copy-start.9 = (bf16[2,9,2,128,128]{4,3,2,1,0:T(8,128)(2,1)S(1)}, bf16[2,9,2,128,128]{4,3,2,1,0:T(8,128)(2,1)}, u32[]{:S(2)}) copy-start(bf16[2,9,2,128,128]{4,3,2,1,0:T(8,128)(2,1)} %get-tuple-element.20) | copy-start | bytes 3538948
  92.5 35.4 %collective-permute-start.16 = (bf16[4,4,144,256]{3,2,1,0:T(8,128)(2,1)}, bf16[4,4,144,256]{3,2,1,0:T(8,128)(2,1)S(1)}, u32[]{:S(2)}, u32[]{:S(2)}) collective-permute-start(bf16[4,4,144,256]{3,2,1,0:T(8,128)(2,1)} %get-tuple-element.31), channel_id=1, source_target_pairs={{0,1},{1,0},{2,3},{3,2},{4,5},{5,4},{6,7},{7,6},{8,9},{9,8},{10,11... | collective-permute-start | bytes 3538952 | tf_op jit(solution)/shard_map/ppermute | solution.py:21
  93.7 5.3 %copy-start.14 = (bf16[2,128,128]{1,2,0:T(8,128)(2,1)S(1)}, bf16[2,128,128]{1,2,0:T(8,128)(2,1)}, u32[]{:S(2)}) copy-start(bf16[2,128,128]{1,2,0:T(8,128)(2,1)} %get-tuple-element.58) | copy-start | bytes 196612
  93.7 0.7 copy-start.8
  96.9 2.9 %collective-permute-start.8 = (bf16[576,256]{1,0:T(8,128)(2,1)}, bf16[576,256]{1,0:T(8,128)(2,1)S(1)}, u32[]{:S(2)}, u32[]{:S(2)}) collective-permute-start(bf16[576,256]{1,0:T(8,128)(2,1)} %get-tuple-element.21), channel_id=1, source_target_pairs={{0,0},{8,16},{16,8},{24,24},{1,1},{9,17},{17,9},{25,25},{2,2},{10,... | collective-permute-start | bytes 884744 | tf_op jit(solution)/shard_map/ppermute | solution.py:330
  98.5 9.6 %collective-permute-start.9 = (bf16[576,256]{1,0:T(8,128)(2,1)}, bf16[576,256]{1,0:T(8,128)(2,1)S(1)}, u32[]{:S(2)}, u32[]{:S(2)}) collective-permute-start(bf16[576,256]{1,0:T(8,128)(2,1)} %get-tuple-element.22), channel_id=1, source_target_pairs={{0,16},{8,0},{16,24},{24,8},{1,17},{9,1},{17,25},{25,9},{2,18},{10... | collective-permute-start | bytes 884744 | tf_op jit(solution)/shard_map/ppermute | solution.py:331
  99.8 8.4 %copy-start = (bf16[576,256]{1,0:T(8,128)(2,1)}, bf16[576,256]{1,0:T(8,128)(2,1)S(1)}, u32[]{:S(2)}) copy-start(bf16[576,256]{1,0:T(8,128)(2,1)S(1)} %collective-permute-done.8.a_ref.p1a) | copy-start | bytes 884740
  108.1 0.7 copy-start.1
  108.9 19.1 %copy-start.10 = (bf16[4,4,144,256]{3,2,1,0:T(8,128)(2,1)S(1)}, bf16[4,4,144,256]{3,2,1,0:T(8,128)(2,1)}, u32[]{:S(2)}) copy-start(bf16[4,4,144,256]{3,2,1,0:T(8,128)(2,1)} %get-tuple-element.30) | copy-start | bytes 3538948
  121.4 4.4 %collective-permute-start.23 = (f32[2,72,128]{2,1,0:T(8,128)S(1)}, f32[2,72,128]{2,1,0:T(8,128)S(1)}, u32[]{:S(2)}, u32[]{:S(2)}) collective-permute-start(f32[2,72,128]{2,1,0:T(8,128)S(1)} %dynamic-slice_bitcast_fusion.3), channel_id=1, source_target_pairs={{0,64},{64,0},{128,192},{192,128},{1,65},{65,1},{129,193},{193,129... | collective-permute-start | bytes 221192 | tf_op jit(solution)/shard_map/ppermute | solution.py:21
  126.7 5.5 %collective-permute-start.24 = (f32[72,128]{1,0:T(8,128)S(1)}, f32[72,128]{1,0:T(8,128)S(1)}, u32[]{:S(2)}, u32[]{:S(2)}) collective-permute-start(f32[72,128]{1,0:T(8,128)S(1)} %dynamic-slice_bitcast_fusion.7), channel_id=1, source_target_pairs={{0,128},{64,192},{128,0},{192,64},{1,129},{65,193},{129,1},{193,65... | collective-permute-start | bytes 110600 | tf_op jit(solution)/shard_map/ppermute | solution.py:21
  132.2 9.3 %collective-permute-start.25 = (f32[72,128]{1,0:T(8,128)S(1)}, f32[72,128]{1,0:T(8,128)S(1)}, u32[]{:S(2)}, u32[]{:S(2)}) collective-permute-start(f32[72,128]{1,0:T(8,128)S(1)} %bitcast_add_fusion.3), channel_id=1, source_target_pairs={{0,32},{32,0},{1,33},{33,1},{2,34},{34,2},{3,35},{35,3},{4,36},{36... | collective-permute-start | bytes 110600 | tf_op jit(solution)/shard_map/ppermute | solution.py:21
  137.7 14.1 %collective-permute-start.17 = (bf16[4,144,256]{2,1,0:T(8,128)(2,1)}, bf16[4,144,256]{2,1,0:T(8,128)(2,1)S(1)}, u32[]{:S(2)}, u32[]{:S(2)}) collective-permute-start(bf16[4,144,256]{2,1,0:T(8,128)(2,1)} %get-tuple-element.40), channel_id=1, source_target_pairs={{0,4},{2,6},{4,0},{6,2},{1,5},{3,7},{5,1},{7,3},{8,12},{10,14},{12... | collective-permute-start | bytes 884744 | tf_op jit(solution)/shard_map/ppermute | solution.py:26
  138.9 12.9 %collective-permute-start.19 = (bf16[4,144,256]{2,1,0:T(8,128)(2,1)}, bf16[4,144,256]{2,1,0:T(8,128)(2,1)S(1)}, u32[]{:S(2)}, u32[]{:S(2)}) collective-permute-start(bf16[4,144,256]{2,1,0:T(8,128)(2,1)} %get-tuple-element.41), channel_id=1, source_target_pairs={{0,6},{2,0},{4,2},{6,4},{1,7},{3,1},{5,3},{7,5},{8,14},{10,8},{12,... | collective-permute-start | bytes 884744 | tf_op jit(solution)/shard_map/ppermute | solution.py:26
  141.5 10.3 %collective-permute-start.18 = (bf16[4,144,256]{2,1,0:T(8,128)(2,1)}, bf16[4,144,256]{2,1,0:T(8,128)(2,1)S(1)}, u32[]{:S(2)}, u32[]{:S(2)}) collective-permute-start(bf16[4,144,256]{2,1,0:T(8,128)(2,1)} %get-tuple-element.42), channel_id=1, source_target_pairs={{0,2},{2,4},{4,6},{6,0},{1,3},{3,5},{5,7},{7,1},{8,10},{10,12},{12... | collective-permute-start | bytes 884744 | tf_op jit(solution)/shard_map/ppermute | solution.py:26
  141.6 10.1 %collective-permute-start.26 = (f32[72,128]{1,0:T(8,128)S(1)}, f32[72,128]{1,0:T(8,128)S(1)}, u32[]{:S(2)}, u32[]{:S(2)}) collective-permute-start(f32[72,128]{1,0:T(8,128)S(1)} %add.203), channel_id=1, source_target_pairs={{0,128},{64,192},{128,0},{192,64},{1,129},{65,193},{129,1},{193,65... | collective-permute-start | bytes 110600 | tf_op jit(solution)/shard_map/ppermute | solution.py:21
  145.7 19.1 %collective-permute-start.11 = (bf16[576,256]{1,0:T(8,128)(2,1)}, bf16[576,256]{1,0:T(8,128)(2,1)}, u32[]{:S(2)}, u32[]{:S(2)}) collective-permute-start(bf16[576,256]{1,0:T(8,128)(2,1)} %get-tuple-element.23), channel_id=1, source_target_pairs={{0,8},{8,0},{16,24},{24,16},{1,9},{9,1},{17,25},{25,17},{2,10},{10... | collective-permute-start | bytes 884744 | tf_op jit(solution)/shard_map/ppermute | solution.py:21
  151.7 9.9 %collective-permute-start.27 = (f32[2,72,128]{2,1,0:T(8,128)S(1)}, f32[2,72,128]{2,1,0:T(8,128)S(1)}, u32[]{:S(2)}, u32[]{:S(2)}) collective-permute-start(f32[2,72,128]{2,1,0:T(8,128)S(1)} %maximum_select_fusion.2), channel_id=1, source_target_pairs={{0,64},{64,0},{128,192},{192,128},{1,65},{65,1},{129,193},{193,129... | collective-permute-start | bytes 221192 | tf_op jit(solution)/shard_map/ppermute | solution.py:21
  151.8 0.7 copy-start.11
  153.7 13.2 %collective-permute-start.20 = (bf16[144,256]{1,0:T(8,128)(2,1)S(1)}, bf16[144,256]{1,0:T(8,128)(2,1)S(1)}, u32[]{:S(2)}, u32[]{:S(2)}) collective-permute-start(bf16[144,256]{1,0:T(8,128)(2,1)S(1)} %get-tuple-element.51), channel_id=1, source_target_pairs={{0,8},{8,0},{16,24},{24,16},{1,9},{9,1},{17,25},{25,17},{2,10},{10... | collective-permute-start | bytes 221192 | tf_op jit(solution)/shard_map/ppermute | solution.py:21
  159.6 7.3 %collective-permute-start.22 = (bf16[144,256]{1,0:T(8,128)(2,1)S(1)}, bf16[144,256]{1,0:T(8,128)(2,1)S(1)}, u32[]{:S(2)}, u32[]{:S(2)}) collective-permute-start(bf16[144,256]{1,0:T(8,128)(2,1)S(1)} %get-tuple-element.52), channel_id=1, source_target_pairs={{0,24},{8,16},{16,8},{24,0},{1,25},{9,17},{17,9},{25,1},{2,26},{10... | collective-permute-start | bytes 221192 | tf_op jit(solution)/shard_map/ppermute | solution.py:21
  161.5 5.8 %collective-permute-start.21 = (bf16[144,256]{1,0:T(8,128)(2,1)S(1)}, bf16[144,256]{1,0:T(8,128)(2,1)S(1)}, u32[]{:S(2)}, u32[]{:S(2)}) collective-permute-start(bf16[144,256]{1,0:T(8,128)(2,1)S(1)} %get-tuple-element.53), channel_id=1, source_target_pairs={{0,16},{8,24},{16,0},{24,8},{1,17},{9,25},{17,1},{25,9},{2,18},{10... | collective-permute-start | bytes 221192 | tf_op jit(solution)/shard_map/ppermute | solution.py:21
  163.1 1.8 %copy-start.13 = (bf16[576,256]{1,0:T(8,128)(2,1)S(1)}, bf16[576,256]{1,0:T(8,128)(2,1)}, u32[]{:S(2)}) copy-start(bf16[576,256]{1,0:T(8,128)(2,1)} %get-tuple-element.24) | copy-start | bytes 884740

commit v2 on v1

v2 whole, which is shorter than its diff:
```python
import functools

import jax
import jax.numpy as jnp
from jax import lax
from jax.experimental import pallas as pl
from jax.experimental.pallas import tpu as pltpu
from jax.sharding import Mesh, PartitionSpec as P

F32 = jnp.float32
BF16 = jnp.bfloat16
GROUP = 4
VMEM_LIMIT = 12 * 1024 * 1024
WEIGHT_LIMIT = 24 * 1024 * 1024

VMEM = pl.BlockSpec(memory_space=pltpu.VMEM)
SMEM = pl.BlockSpec(memory_space=pltpu.SMEM)
ANY = pl.BlockSpec(memory_space=pl.ANY)
HBM = pl.BlockSpec(memory_space=pltpu.HBM)
PARAMS = pltpu.CompilerParams(vmem_limit_bytes=VMEM_LIMIT)
WEIGHT_PARAMS = pltpu.CompilerParams(vmem_limit_bytes=WEIGHT_LIMIT)
STEPS = 4


def cost(us):
    return pl.CostEstimate(flops=int(us * 1.15e9), bytes_accessed=0, transcendentals=0)


def xor(x, axis, k):
    return lax.ppermute(x, axis, [(i, i ^ k) for i in range(lax.axis_size(axis))])


def shift(x, axis, k):
    n = lax.axis_size(axis)
    return lax.ppermute(x, axis, [(i, (i + k) % n) for i in range(n)])


def mm(a, b):
    return jnp.dot(a, b, preferred_element_type=F32)


def split(x):
    hi = x.astype(BF16)
    return hi, (x - hi.astype(F32)).astype(BF16)


def fill_kernel(k_ref, dep_ref, mat, raw):
    n = k_ref.shape[1]
    blocks = k_ref.shape[3]
    raw[...] = jnp.zeros_like(raw)
    for s in range(2):
        raw[:, 64 * s : 64 * s + blocks] = k_ref[s].reshape(n * n, blocks)
    sub = lax.broadcasted_iota(jnp.int32, (n, 128), 0)
    for u in range(n):
        mat[u * n : (u + 1) * n, :] = (
            raw[u * n : (u + 1) * n, :] - raw[pl.ds(u, n, stride=n), :]
            + jnp.where(sub == u, 1.0, 0.0)
        )

    def eliminate(k, carry):
        at = sub == k
        base = pl.multiple_of(k * n, n)
        pivot = 1.0 / mat[pl.ds(base + k, 1), :]
        row = jnp.where(at, 1.0, mat[pl.ds(base, n), :]) * pivot
        for i in range(n):
            factor = mat[pl.ds(i * n + k, 1), :]
            mine = jnp.where(at, 0.0, mat[i * n : (i + 1) * n, :])
            mat[i * n : (i + 1) * n, :] = mine - factor * row
        mat[pl.ds(base, n), :] = row
        return carry

    lax.fori_loop(0, n, eliminate, 0)


def one_hots(at_ref, perm_ref, s, n):
    width = GROUP * n
    r = lax.broadcasted_iota(jnp.int32, (width, width), 0)
    c = lax.broadcasted_iota(jnp.int32, (width, width), 1)
    half = width // 2
    by_row, by_col = jnp.zeros_like(r), jnp.zeros_like(c)
    for u in range(n):
        by_row = jnp.where(r % n == u, perm_ref[s, u], by_row)
        by_col = jnp.where(c % n == u, perm_ref[s, u], by_col)

    def one_hot(raw_at, target, cut_at, bit):
        spot = ((cut_at // half) ^ bit) * 16 + cut_at % 16
        hit = (target == spot) & (raw_at // n == (cut_at // 16) % GROUP)
        return jnp.where(hit, 1.0, 0.0).astype(BF16)

    pi = one_hot(r, by_row, c, at_ref[0] // 2)
    pot = one_hot(c, by_col, r, at_ref[0] % 2)
    return pi, pot, r // n == c // n


def wide_block(turned, s, g, groups, n, diagonal):
    rows = [turned[pl.ds(64 * s + g + groups * q, n, stride=128), :] for q in range(GROUP)]
    return jnp.where(diagonal, jnp.concatenate([jnp.concatenate(rows, 0)] * GROUP, 1), 0.0)


def invert_kernel(at_ref, perm_ref, k_ref, dep_ref, turned, mt_ref, mat, raw):
    fill_kernel(k_ref, dep_ref, mat, raw)
    n = k_ref.shape[1]
    groups = mt_ref.shape[0]
    for u in range(n):
        turned[u * 128 : (u + 1) * 128, :] = jnp.transpose(mat[u * n : (u + 1) * n, :])
    pi, pot, diagonal = one_hots(at_ref, perm_ref, 1, n)
    ident = mm(pot, pi)
    for g in range(groups):
        hi, lo = split(wide_block(turned, 1, g, groups, n, diagonal))
        rot = mm(pot, mm(hi, pi).astype(BF16)) + mm(pot, mm(lo, pi).astype(BF16))
        mt_ref[g, 0], mt_ref[g, 1] = split(jnp.transpose(2.0 * rot - ident))


def build_kernel(at_ref, perm_ref, turned, dep_ref, m0_ref, mt0_ref, m1_ref, l_ref, r_ref):
    groups = l_ref.shape[1]
    n = l_ref.shape[-1] // GROUP
    for s in range(2):
        pi, pot, diagonal = one_hots(at_ref, perm_ref, s, n)
        ident = mm(pot, pi)
        for g in range(groups):
            hi, lo = split(wide_block(turned, s, g, groups, n, diagonal))
            right_hi, right_lo = mm(hi, pi), mm(lo, pi)
            left = mm(pot, hi) + mm(pot, lo)
            l_ref[s, g, 0], l_ref[s, g, 1] = split(jnp.transpose(left))
            r_ref[s, g, 0], r_ref[s, g, 1] = split(jnp.transpose(right_hi + right_lo))
            rot = mm(pot, right_hi.astype(BF16)) + mm(pot, right_lo.astype(BF16))
            rot = 2.0 * rot - ident
            m_ref = m1_ref if s else m0_ref
            m_ref[g, 0], m_ref[g, 1] = split(rot)
            if s == 0:
                mt0_ref[g, 0], mt0_ref[g, 1] = split(jnp.transpose(rot))


def invert(place, section_perm, skew, after):
    n = skew.shape[-1]
    groups = skew.shape[1] // GROUP
    width = GROUP * n
    return pl.pallas_call(
        invert_kernel,
        out_shape=(
            jax.ShapeDtypeStruct((n * 128, n), F32),
            jax.ShapeDtypeStruct((groups, 2, width, width), BF16),
        ),
        in_specs=[SMEM] * 2 + [VMEM, ANY],
        out_specs=(VMEM, VMEM),
        scratch_shapes=[pltpu.VMEM((n * n, 128), F32), pltpu.VMEM((n * n, 128), F32)],
        compiler_params=PARAMS,
        cost_estimate=cost(7),
        name="invert",
    )(place, section_perm, jnp.transpose(skew, (0, 2, 3, 1)), after)


def build(place, section_perm, turned, after):
    n = turned.shape[1]
    groups = after.shape[0] // (16 * GROUP)
    width = GROUP * n
    one = jax.ShapeDtypeStruct((groups, 2, width, width), BF16)
    two = jax.ShapeDtypeStruct((2, groups, 2, width, width), BF16)
    return pl.pallas_call(
        build_kernel,
        out_shape=(one, one, one, two, two),
        in_specs=[SMEM] * 2 + [VMEM, ANY],
        out_specs=(VMEM,) * 5,
        compiler_params=PARAMS,
        cost_estimate=cost(5),
        name="build",
    )(place, section_perm, turned, after)


def spans(g, groups):
    return [slice(16 * (g + groups * q), 16 * (g + groups * q + 1)) for q in range(GROUP)]


def both(a_ref, b_ref, g, groups):
    rows = spans(g, groups)
    return jnp.concatenate([a_ref[row, :] for row in rows] + [b_ref[row, :] for row in rows], 0)


def put(oa_ref, ob_ref, g, groups, y):
    half = y.shape[0] // 2
    for q, row in enumerate(spans(g, groups)):
        oa_ref[row, :] = y[16 * q : 16 * (q + 1)]
        ob_ref[row, :] = y[half + 16 * q : half + 16 * (q + 1)]


def turn_kernel(a_ref, b_ref, m_ref, *rest):
    oa_ref, ob_ref = rest[-2:]
    groups = m_ref.shape[0]
    for g in range(groups):
        x = both(a_ref, b_ref, g, groups)
        y = mm(m_ref[g, 0], x) + mm(m_ref[g, 1], x)
        put(oa_ref, ob_ref, g, groups, y.astype(BF16))


def turn(a, b, m, after):
    shape = jax.ShapeDtypeStruct(a.shape, BF16)
    return pl.pallas_call(
        turn_kernel,
        out_shape=(shape, shape),
        in_specs=[VMEM] * 3 + [ANY] * len(after),
        out_specs=(VMEM, VMEM),
        compiler_params=PARAMS,
        cost_estimate=cost(1),
        name="turn",
    )(a, b, m, *after)


def scale_rows(ps_ref, ids, high):
    table = jnp.transpose(ps_ref[...])
    parts = []
    for _ in range(3):
        hi, _rest = split(table)
        parts.append(hi)
        table = table - hi.astype(F32)
    wanted = lax.broadcasted_iota(jnp.int32, (3 * ps_ref.shape[0], ids.shape[1]), 0) % ps_ref.shape[0]
    onehot = jnp.where(ids == wanted, 1.0, 0.0).astype(BF16)
    whole = mm(jnp.concatenate(parts, 1), onehot).reshape(-1, 2, 16, ids.shape[1])
    return jnp.where(high, whole[:, 1], whole[:, 0]).reshape(-1, ids.shape[1])


def scaled_cotangent(high, grad_ref, rec_ref, sa_ref, sb_ref, g, groups):
    rows = spans(g, groups)
    own = [grad_ref[2 * row.start : 2 * row.stop, :].reshape(2, 16, -1) for row in rows]
    own = [jnp.where(high, x[1], x[0]) for x in own]
    x = jnp.concatenate(own + [rec_ref[row, :] for row in rows], 0).astype(F32)
    return x * both(sa_ref, sb_ref, g, groups)


def cotangent_kernel(at_ref, grad_ref, rec_ref, mine_ref, theirs_ref, ids_ref, mt_ref, *rest):
    oa_ref, ob_ref, sa_ref, sb_ref = rest
    high = at_ref[0] % 2 == 1
    ids = ids_ref[...]
    sa_ref[...] = scale_rows(mine_ref, ids, high)
    sb_ref[...] = scale_rows(theirs_ref, ids, high)
    groups = mt_ref.shape[0]
    for g in range(groups):
        hi, lo = split(scaled_cotangent(high, grad_ref, rec_ref, sa_ref, sb_ref, g, groups))
        y = mm(mt_ref[g, 0], hi) + (mm(mt_ref[g, 1], hi) + mm(mt_ref[g, 0], lo))
        put(oa_ref, ob_ref, g, groups, y.astype(BF16))


def cotangent(place, out_grad, rec, mine, theirs, ids, mt):
    shape = jax.ShapeDtypeStruct(rec.shape, BF16)
    return pl.pallas_call(
        cotangent_kernel,
        out_shape=(shape, shape),
        in_specs=[SMEM] + [VMEM] * 6,
        out_specs=(VMEM, VMEM),
        scratch_shapes=[pltpu.VMEM(rec.shape, F32)] * 2,
        compiler_params=PARAMS,
        cost_estimate=cost(3),
        name="cotangent",
    )(place, out_grad, rec, mine, theirs, ids, mt)


def last_kernel(norm, at_ref, y0_ref, grad_ref, rec_ref, mine_ref, theirs_ref, ids_ref, *rest):
    (m_ref, p1a, p1b, q0a, q0b, p0a, p0b, l_ref, r_ref, dep_ref) = rest[:10]
    (ja_ref, jb_ref, keep_ref, send_ref, hold, out_ref, sa_ref, sb_ref) = rest[10:]
    high = at_ref[0] % 2 == 1
    ids = ids_ref[...]
    sa_ref[...] = scale_rows(mine_ref, ids, high)
    sb_ref[...] = scale_rows(theirs_ref, ids, high)
    groups = l_ref.shape[1]
    width = l_ref.shape[-1]
    n = width // GROUP
    r = lax.broadcasted_iota(jnp.int32, (width, width), 0)
    c = lax.broadcasted_iota(jnp.int32, (width, width), 1)
    same = (r // 16) % GROUP == (c // 16) % GROUP
    u = lax.broadcasted_iota(jnp.int32, (n, width), 0)
    v = lax.broadcasted_iota(jnp.int32, (n, width), 1) % n
    nt = (((1,), (1,)), ((), ()))
    every = [(s, g) for s in range(2) for g in range(groups)]
    for s, g in every:
        if s == 0:
            q = both(q0a, q0b, g, groups)
            p = both(p0a, p0b, g, groups)
        else:
            q = scaled_cotangent(high, grad_ref, rec_ref, sa_ref, sb_ref, g, groups).astype(BF16)
            p = both(p1a, p1b, g, groups)
            y = (mm(m_ref[g, 0], p) + mm(m_ref[g, 1], p)) * both(sa_ref, sb_ref, g, groups)
            put(ja_ref, jb_ref, g, groups, y.astype(BF16))
        cross = lax.dot_general(q, p, nt, preferred_element_type=F32)
        hold[s, g] = jnp.where(same, cross, 0.0).astype(BF16)
    for s, g in every:
        x = hold[s, g]
        hold[s, g] = (mm(l_ref[s, g, 0], x) + mm(l_ref[s, g, 1], x)).astype(BF16)
    for g in range(groups):
        dense = []
        for s in range(2):
            x = hold[s, g]
            full = mm(x, r_ref[s, g, 0]) + mm(x, r_ref[s, g, 1])
            full = (full - jnp.transpose(full)) * (-2.0 * norm)
            dense.append(full[:n] + full[n : 2 * n] + full[2 * n : 3 * n] + full[3 * n :])
        out_ref[g * n : (g + 1) * n, :] = jnp.where(u < v, dense[0], dense[1])
    size = keep_ref.shape[0]
    y0 = y0_ref[0]
    keep_ref[...] = out_ref[pl.ds(pl.multiple_of(y0 * size, 8), size), :]
    send_ref[...] = out_ref[pl.ds(pl.multiple_of((1 - y0) * size, 8), size), :]


def unpack_kernel(y0_ref, mine_ref, other_ref, out_ref, packed, planes):
    size = mine_ref.shape[0]
    y0 = y0_ref[0]
    packed[pl.ds(pl.multiple_of(y0 * size, 8), size), :] = mine_ref[...]
    packed[pl.ds(pl.multiple_of((1 - y0) * size, 8), size), :] = other_ref[...]
    n = out_ref.shape[1]
    groups = packed.shape[0] // n
    for u in range(n):
        x = jnp.transpose(packed[pl.ds(u, groups, stride=n), :])
        planes[u * n : (u + 1) * n, :] = jnp.concatenate([x[q * n : (q + 1) * n] for q in range(GROUP)], 1)
    v = lax.broadcasted_iota(jnp.int32, (n, planes.shape[1]), 0)
    for u in range(n):
        x = planes[u * n : (u + 1) * n, :]
        y = planes[pl.ds(u, n, stride=n), :]
        out_ref[0, u] = jnp.where(v > u, x, 0.0) - jnp.where(v < u, y, 0.0)
        out_ref[1, u] = jnp.where(v < u, x, 0.0) - jnp.where(v > u, y, 0.0)


def gather_kernel(a_ref, b_ref, c_ref, d_ref, dep_ref, out_ref):
    for i, ref in enumerate((a_ref, b_ref, c_ref, d_ref)):
        out_ref[i] = ref[...]


def hidden_kernel(at_ref, own_ref, r1, r2, r3, core_ref, w_ref, keep_ref, send_ref, x_all):
    size = own_ref.shape[1]
    rows = w_ref.shape[0] // STEPS
    zi, xi, ci = at_ref[0], at_ref[1], at_ref[2]
    for d in range(4):
        src = (own_ref, r1, r2, r3)[d]
        for r in range(4):
            place = ((zi ^ r) * 4 + (xi + 4 - d) % 4) * 2
            x_all[pl.ds(pl.multiple_of((place + ci) * size, 16), size), :] = src[r]
            x_all[pl.ds(pl.multiple_of((place + 1 - ci) * size, 16), size), :] = core_ref[d, r]
    upper = zi >= 2
    for i in range(STEPS):
        y = mm(w_ref[i * rows : (i + 1) * rows, :], x_all[...]).astype(BF16)
        y = y.reshape(-1, 2, 16, y.shape[1])
        first, second = y[:, 0].reshape(-1, y.shape[3]), y[:, 1].reshape(-1, y.shape[3])
        span = slice(i * (rows // 2), (i + 1) * (rows // 2))
        keep_ref[span, :] = jnp.where(upper, second, first)
        send_ref[span, :] = jnp.where(upper, first, second)


def hidden_halves(place, own, r1, r2, r3, core, weight):
    rows, depth = weight.shape
    cols = own.shape[-1]
    shape = jax.ShapeDtypeStruct((rows // 2, cols), BF16)
    return pl.pallas_call(
        hidden_kernel,
        out_shape=(shape, shape),
        in_specs=[SMEM] + [VMEM] * 6,
        out_specs=(VMEM, VMEM),
        scratch_shapes=[
            pltpu.VMEM((depth, cols), BF16),
        ],
        compiler_params=WEIGHT_PARAMS,
        cost_estimate=cost(6),
        name="hidden",
    )(place, own, r1, r2, r3, core, weight)


def input_kernel(at_ref, own_ref, other_ref, w_ref, dep_ref, keep_ref, send_ref, gt, y_all):
    depth = w_ref.shape[1] // STEPS
    zi, xi, ci = at_ref[0], at_ref[1], at_ref[2]
    upper = zi >= 2
    a, b = own_ref[...], other_ref[...]
    cols = a.shape[1]
    first = jnp.where(upper, b, a).reshape(-1, 1, 16, cols)
    second = jnp.where(upper, a, b).reshape(-1, 1, 16, cols)
    whole = jnp.concatenate([first, second], 1).reshape(-1, cols)
    gt[...] = jnp.transpose(whole)
    size = keep_ref.shape[2]
    for z in range(STEPS):
        y_all[...] = jnp.transpose(mm(gt[...], w_ref[:, z * depth : (z + 1) * depth]))
        for d in range(4):
            spot = ((xi + d) % 4) * 2
            keep_ref[d, z ^ zi] = y_all[pl.ds(pl.multiple_of((spot + ci) * size, 16), size), :]
            send_ref[d, z ^ zi] = y_all[pl.ds(pl.multiple_of((spot + 1 - ci) * size, 16), size), :].astype(BF16)


def input_parts(place, own, other, weight, after):
    rows, depth = weight.shape
    cols = own.shape[-1]
    dims = (4, 4, depth // 32, cols)
    return pl.pallas_call(
        input_kernel,
        out_shape=(jax.ShapeDtypeStruct(dims, F32), jax.ShapeDtypeStruct(dims, BF16)),
        in_specs=[SMEM] + [VMEM] * 3 + [ANY],
        out_specs=(VMEM, VMEM),
        scratch_shapes=[
            pltpu.VMEM((cols, rows), BF16),
            pltpu.VMEM((depth // STEPS, cols), F32),
        ],
        compiler_params=WEIGHT_PARAMS,
        cost_estimate=cost(6),
        name="input_sums",
    )(place, own, other, weight, after)


def join_kernel(at_ref, own_ref, other_ref, out_ref):
    high = at_ref[0] % 2 == 1
    a, b = own_ref[...], other_ref[...]
    cols = a.shape[1]
    first = jnp.where(high, b, a).reshape(-1, 1, 16, cols)
    second = jnp.where(high, a, b).reshape(-1, 1, 16, cols)
    out_ref[...] = jnp.concatenate([first, second], 1).reshape(-1, cols)


A_PAIRS = [(0, 0), (1, 2), (2, 1), (3, 3)]
B_PAIRS = [(0, 2), (1, 0), (2, 3), (3, 1)]
B_BACK = [(b, a) for a, b in B_PAIRS]


def per_device(responses, weight, skew, section_perm, prefix_ids, prefix_scale, out_grad):
    zi, xi, ci = lax.axis_index("z"), lax.axis_index("x"), lax.axis_index("c")
    yi = lax.axis_index("y")
    q = lax.bitwise_and(zi, 1)
    place = jnp.stack([zi, xi, ci]).astype(jnp.int32)
    n = skew.shape[-1]
    width = GROUP * n
    cols = responses.shape[0]
    mine = responses.T
    along_z = jnp.stack([mine] + [xor(mine, "z", k) for k in (1, 2, 3)])
    g_send = lax.dynamic_index_in_dim(out_grad.reshape(-1, 2, 16, cols), 1 - q, 1, keepdims=False)
    g_rec = xor(g_send.reshape(-1, cols), "z", 1)
    scale_rec = xor(prefix_scale, "z", 1)
    x2 = shift(along_z, "x", 2)
    x1 = shift(along_z, "x", 1)
    x3 = shift(along_z, "x", 3)
    turned, mt1 = invert(place, section_perm, skew, along_z)
    ids = prefix_ids[None, :]
    ga_out, gb_out = cotangent(place, out_grad, g_rec, prefix_scale, scale_rec, ids, mt1)
    ga = lax.ppermute(ga_out, "z", A_PAIRS)
    gb = lax.ppermute(gb_out, "z", B_BACK)
    by_x = pl.pallas_call(
        gather_kernel,
        out_shape=jax.ShapeDtypeStruct((4,) + along_z.shape, BF16),
        in_specs=[VMEM] * 4 + [ANY],
        out_specs=VMEM,
        compiler_params=PARAMS,
        cost_estimate=cost(1),
        name="gather",
    )(along_z, x1, x2, x3, ga_out)
    by_core = xor(by_x, "c", 1)
    m0, mt0, m1, left, right = build(place, section_perm, turned, ga_out)
    z_own, z_send = hidden_halves(place, along_z, x1, x2, x3, by_core, weight)
    z_rec = xor(z_send, "z", 2)
    h_own, h_send = turn(ga, gb, mt0, (z_send,))
    h_rec = xor(h_send, "z", 2)
    za_out, zb = turn(z_own, z_rec, m0, (h_send,))
    za = lax.ppermute(za_out, "z", A_PAIRS)
    zb = lax.ppermute(zb, "z", B_PAIRS)
    keep, send = input_parts(place, h_own, h_rec, weight, za_out)
    part = keep + xor(send, "c", 1).astype(F32)
    total = part[0] + sum(shift(part[d].astype(BF16), "x", d).astype(F32) for d in (2, 1, 3))
    final = total[0] + sum(xor(total[k].astype(BF16), "z", k).astype(F32) for k in (1, 2, 3))
    input_grad = final.astype(BF16)
    rows_all = cols * lax.axis_size("y") * lax.axis_size("h")
    groups = left.shape[1]
    y0 = lax.bitwise_and(yi, 1).reshape(1)
    part_of = jax.ShapeDtypeStruct((groups * n // 2, width), F32)
    half_of = jax.ShapeDtypeStruct(za.shape, BF16)
    j_own, j_send, half, half_send = pl.pallas_call(
        functools.partial(last_kernel, 1.0 / rows_all**0.5),
        out_shape=(half_of, half_of, part_of, part_of),
        in_specs=[SMEM] * 2 + [VMEM] * 14 + [ANY],
        out_specs=(VMEM,) * 4,
        scratch_shapes=[
            pltpu.VMEM((2, groups, width, width), BF16),
            pltpu.VMEM((groups * n, width), F32),
            pltpu.VMEM(za.shape, F32),
            pltpu.VMEM(za.shape, F32),
        ],
        compiler_params=PARAMS,
        cost_estimate=cost(4),
        name="last",
    )(
        place, y0, out_grad, g_rec, prefix_scale, scale_rec, ids,
        m1, za, zb, ga, gb, z_own, z_rec, left, right, send,
    )
    j_rec = xor(j_send, "z", 1)
    judged = pl.pallas_call(
        join_kernel,
        out_shape=jax.ShapeDtypeStruct(out_grad.shape, BF16),
        in_specs=[SMEM] + [VMEM] * 2,
        out_specs=VMEM,
        compiler_params=PARAMS,
        name="join",
    )(place, j_own, j_rec)
    half = half + xor(half_send, "y", 1)
    half = half + xor(half, "y", 2)
    half = half + xor(half, "h", 1)
    other = xor(half, "y", 1)
    skew_grad = pl.pallas_call(
        unpack_kernel,
        out_shape=jax.ShapeDtypeStruct((2, n, n, GROUP * groups), F32),
        in_specs=[SMEM] + [VMEM] * 2,
        out_specs=VMEM,
        scratch_shapes=[
            pltpu.VMEM((groups * n, width), F32),
            pltpu.VMEM((n * n, GROUP * groups), F32),
        ],
        compiler_params=PARAMS,
        cost_estimate=cost(2),
        name="unpack",
    )(y0, half, other)
    return judged, input_grad, jnp.transpose(skew_grad, (0, 3, 1, 2))


def solution(mesh):
    wide = Mesh(mesh.devices.reshape(4, 2, 4, 4, 2), ("y", "h", "z", "x", "c"))
    dp, mp = ("y", "h"), ("z", "x", "c")
    in_specs = (
        P(dp, mp),
        P(mp, None),
        P(None, mp, None, None),
        P(),
        P(dp),
        P(None, mp),
        P(mp, dp),
    )
    out_specs = (P(mp, dp), P(mp, dp), P(None, mp, None, None))
    return jax.shard_map(per_device, mesh=wide, in_specs=in_specs, out_specs=out_specs, check_vma=False)
```

time: 169 us -> 128 us (0.76)
  Pallas kernels: 49.4 us -> 30.3 us
  local copies, waits for them, and re-layouts: 15.1 us -> 5.24 us
  other arithmetic: 11.2 us -> 3.72 us
  matrix products: 2.22 us -> 0 us
  waiting for transfers between devices: 41.4 us -> 39.6 us
    pallas_call x8 -> x11, Pallas kernels: 49.4 us -> 30.3 us  [the longest x1 7.39 us: invert(): pl.pallas_call(invert_kernel, out_shape=(jax.ShapeDtypeStruct((n * 128, n...]
    ppermute x18 -> x17, waiting for transfers between devices: 19 us -> 37.2 us  [xor(): lax.ppermute(x, axis, [(i, i ^ k) for i in range(lax.axis_size(axis))])]
    ppermute x3, waiting for transfers between devices: 13.4 us -> 2.37 us  [the longest x1 2.37 us: per_device(): gb = lax.ppermute(gb_out, 'z', B_BACK)]
    ppermute x1, waiting for transfers between devices: 8.37 us -> 0.01 us  [per_device(): zb = lax.ppermute(zb, 'z', B_PAIRS)]
    squeeze x6 -> x0, local copies, waits for them, and re-layouts: 5.41 us -> none  [the longest x1 2.38 us: per_device(): h_own, h_send = turn(ga, gb, mt[0])]
    select_n x9 -> x0, other arithmetic: 4.39 us -> none  [the longest x2 3.22 us: halves(): return (jnp.where(high, second, first), jnp.where(high, first, second))]
    ppermute x6, starting transfers between devices: 8.34 us -> 11.9 us  [shift(): return lax.ppermute(x, axis, [(i, (i + k) % n) for i in range(n)])]
    ppermute x18 -> x17, starting transfers between devices: 32.1 us -> 28.5 us  [xor(): lax.ppermute(x, axis, [(i, i ^ k) for i in range(lax.axis_size(axis))])]
  transfers between devices with their start and end apart: 28 -> 27, of which waited for: 8 -> 10; matrix products, arithmetic and copies ran while one was open for 14% -> 3% of each run, Pallas kernels for 29% -> 19%
where the time goes in v2:
time: 128 us
  starting transfers between devices  47.6 us (37%)
  waiting for transfers between devices  39.6 us (31%)
  Pallas kernels  30.3 us (24%)
  local copies, waits for them, and re-layouts  5.24 us (4%)
  other arithmetic  3.72 us (3%)
    ppermute x17, waiting for transfers between devices, xor(): lax.ppermute(x, axis, [(i, i ^ k) for i in range(lax.axis_size(axis))])  37.2 us
    ppermute x17, starting transfers between devices, xor(): lax.ppermute(x, axis, [(i, i ^ k) for i in range(lax.axis_size(axis))])  28.5 us
    ppermute x6, starting transfers between devices, shift(): return lax.ppermute(x, axis, [(i, (i + k) % n) for i in range(n)])  11.9 us
    pallas_call x1, Pallas kernels, invert(): pl.pallas_call(invert_kernel, out_shape=(jax.ShapeDtypeStruct((n * 128, n...  7.39 us
    pallas_call x1, Pallas kernels, input_parts(): pl.pallas_call(input_kernel, out_shape=(jax.ShapeDtypeStruct(dims, F32),...  5.64 us
    unnamed x50, local copies, waits for them, and re-layouts  4.18 us
    pallas_call x1, Pallas kernels, build(): pl.pallas_call(build_kernel, out_shape=(one, one, one, two, two), in_spec...  4.11 us
    ppermute x1, starting transfers between devices, per_device(): gb = lax.ppermute(gb_out, 'z', B_BACK)  3.83 us
  transfers between devices with their start and end apart: 27, of which 10 were waited for; matrix products, arithmetic and copies ran while one was open for 3% of the time, Pallas kernels for 19%

profile of v2, /device:TPU:24, one launch (start us, length us, event | category | flops | bytes accessed | tf_op | source)
XLA Modules:
  0.0 127.5 jit_solution(13737382803043389603)
XLA Ops:
  0.7 2.0 %collective-permute-start.2 = (bf16[144,256]{1,0:T(8,128)(2,1)}, bf16[144,256]{1,0:T(8,128)(2,1)S(1)}, u32[]{:S(2)}, u32[]{:S(2)}) collective-permute-start(bf16[144,256]{1,0:T(8,128)(2,1)} %bitcast.47), channel_id=1, source_target_pairs={{0,8},{8,0},{16,24},{24,16},{1,9},{9,1},{17,25},{25,17},{2,10},{10... | collective-permute-start | bytes 221192 | tf_op jit(solution)/shard_map/ppermute | solution.py:30
  2.7 3.3 %collective-permute-start.3 = (bf16[144,256]{1,0:T(8,128)(2,1)}, bf16[144,256]{1,0:T(8,128)(2,1)S(1)}, u32[]{:S(2)}, u32[]{:S(2)}) collective-permute-start(bf16[144,256]{1,0:T(8,128)(2,1)} %bitcast.48), channel_id=1, source_target_pairs={{0,16},{8,24},{16,0},{24,8},{1,17},{9,25},{17,1},{25,9},{2,18},{10... | collective-permute-start | bytes 221192 | tf_op jit(solution)/shard_map/ppermute | solution.py:30
  5.9 1.0 constant_dynamic-slice_fusion
  6.9 0.7 collective-permute-start
  7.6 1.5 %collective-permute-start.1 = (f32[16,1152]{1,0:T(8,128)}, f32[16,1152]{1,0:T(8,128)S(1)}, u32[]{:S(2)}, u32[]{:S(2)}) collective-permute-start(f32[16,1152]{1,0:T(8,128)} %mine_ref.3), channel_id=1, source_target_pairs={{0,8},{8,0},{16,24},{24,16},{1,9},{9,1},{17,25},{25,17},{2,10},{10... | collective-permute-start | bytes 221192 | tf_op jit(solution)/shard_map/ppermute | solution.py:30
  9.0 0.1 pad_add_fusion.at_ref
  9.1 2.2 %collective-permute-done.3 = bf16[144,256]{1,0:T(8,128)(2,1)S(1)} collective-permute-done((bf16[144,256]{1,0:T(8,128)(2,1)}, bf16[144,256]{1,0:T(8,128)(2,1)S(1)}, u32[]{:S(2)}, u32[]{:S(2)}) %collective-permute-start.3) | collective-permute-done | bytes 73760 | tf_op jit(solution)/shard_map/ppermute | solution.py:30
  11.3 1.8 %collective-permute-done.4 = bf16[144,256]{1,0:T(8,128)(2,1)S(1)} collective-permute-done((bf16[144,256]{1,0:T(8,128)(2,1)}, bf16[144,256]{1,0:T(8,128)(2,1)S(1)}, u32[]{:S(2)}, u32[]{:S(2)}) %collective-permute-start.4) | collective-permute-done | bytes 73760 | tf_op jit(solution)/shard_map/ppermute | solution.py:30
  13.1 0.9 pad_maximum_fusion.dep_ref.a_ref.own_ref
  14.0 1.6 %collective-permute-start.5 = (bf16[4,144,256]{2,1,0:T(8,128)(2,1)S(1)}, bf16[4,144,256]{2,1,0:T(8,128)(2,1)S(1)}, u32[]{:S(2)}, u32[]{:S(2)}) collective-permute-start(bf16[4,144,256]{2,1,0:T(8,128)(2,1)S(1)} %pad_maximum_fusion.dep_ref.a_ref.own_ref), channel_id=1, source_target_pairs={{0,2},{2,4},{4,6},{6,0},{1,3},{3,5},{5,7},{7,1},{8,10},{10,12},{12... | collective-permute-start | bytes 884744 | tf_op jit(solution)/shard_map/ppermute | solution.py:35
  15.5 2.7 %collective-permute-start.6 = (bf16[4,144,256]{2,1,0:T(8,128)(2,1)S(1)}, bf16[4,144,256]{2,1,0:T(8,128)(2,1)S(1)}, u32[]{:S(2)}, u32[]{:S(2)}) collective-permute-start(bf16[4,144,256]{2,1,0:T(8,128)(2,1)S(1)} %pad_maximum_fusion.dep_ref.a_ref.own_ref), channel_id=1, source_target_pairs={{0,4},{2,6},{4,0},{6,2},{1,5},{3,7},{5,1},{7,3},{8,12},{10,14},{12... | collective-permute-start | bytes 884744 | tf_op jit(solution)/shard_map/ppermute | solution.py:35
  18.3 1.4 %collective-permute-start.7 = (bf16[4,144,256]{2,1,0:T(8,128)(2,1)S(1)}, bf16[4,144,256]{2,1,0:T(8,128)(2,1)S(1)}, u32[]{:S(2)}, u32[]{:S(2)}) collective-permute-start(bf16[4,144,256]{2,1,0:T(8,128)(2,1)S(1)} %pad_maximum_fusion.dep_ref.a_ref.own_ref), channel_id=1, source_target_pairs={{0,6},{2,0},{4,2},{6,4},{1,7},{3,1},{5,3},{7,5},{8,14},{10,8},{12,... | collective-permute-start | bytes 884744 | tf_op jit(solution)/shard_map/ppermute | solution.py:35
  19.7 7.4 %invert.1 = (f32[4096,32]{1,0:T(8,128)S(1)}, bf16[9,2,128,128]{3,2,1,0:T(8,128)(2,1)S(1)}) custom-call(s32[3]{0:T(128)S(1)} %pad_add_fusion.at_ref, s32[2,32]{1,0:T(2,128)S(1)} %copy-done.12, f32[2,32,32,36]{3,2,1,0:T(8,128)S(1)} %bitcast.43, bf16[4,144,256]{2,1,0:T(8,128)(2,1)S(1)} %pad_maximum_fusion.dep_ref.a_ref.own_ref), custom_call_target="tpu_custom_call" | custom-call | flops 8049999872 | tf_op jit(solution)/shard_map/invert/pallas_call | solution.py:138
  27.1 0.0 copy-start.10
  27.2 2.1 %cotangent.1 = (bf16[576,256]{1,0:T(8,128)(2,1)S(1)}, bf16[576,256]{1,0:T(8,128)(2,1)S(1)}) custom-call(s32[3]{0:T(128)S(1)} %pad_add_fusion.at_ref, bf16[1152,256]{1,0:T(8,128)(2,1)S(1)} %copy-done, bf16[576,256]{1,0:T(8,128)(2,1)S(1)} %collective-permute-done.rec_ref, f32[16,1152]{1,0:T(8,128)S(1)} %copy-done.8, ...), custom_call_target="tpu_custom_call" | custom-call | flops 3449999872 | tf_op jit(solution)/shard_map/cotangent/pallas_call | solution.py:244
  29.3 0.0 slice-start
  29.3 0.1 gather.1
  29.4 0.1 collective-permute-start.8
  29.5 0.8 collective-permute-start.10
  30.3 3.8 %collective-permute-start.11 = (bf16[576,256]{1,0:T(8,128)(2,1)S(1)}, bf16[576,256]{1,0:T(8,128)(2,1)S(1)}, u32[]{:S(2)}, u32[]{:S(2)}) collective-permute-start(bf16[576,256]{1,0:T(8,128)(2,1)S(1)} %get-tuple-element.31), channel_id=1, source_target_pairs={{16,0},{0,8},{24,16},{8,24},{17,1},{1,9},{25,17},{9,25},{18,2},{2,... | collective-permute-start | bytes 884744 | tf_op jit(solution)/shard_map/ppermute | solution.py:434
  34.2 4.1 %build.1 = (bf16[9,2,128,128]{3,2,1,0:T(8,128)(2,1)S(1)}, bf16[9,2,128,128]{3,2,1,0:T(8,128)(2,1)S(1)}, bf16[9,2,128,128]{3,2,1,0:T(8,128)(2,1)S(1)}, bf16[2,9,2...) custom-call(s32[3]{0:T(128)S(1)} %pad_add_fusion.at_ref, s32[2,32]{1,0:T(2,128)S(1)} %copy-done.12, ...), custom_call_target="tpu_custom_call" | custom-call | flops 5750000128 | tf_op jit(solution)/shard_map/build/pallas_call | solution.py:159
  38.3 1.0 copy-done.16
  39.3 1.0 copy-done.18
  40.4 0.8 copy-done.20
  41.2 3.6 %hidden.1 = (bf16[576,256]{1,0:T(8,128)(2,1)S(1)}, bf16[576,256]{1,0:T(8,128)(2,1)S(1)}) custom-call(s32[3]{0:T(128)S(1)} %pad_add_fusion.at_ref, bf16[4,144,256]{2,1,0:T(8,128)(2,1)S(1)} %pad_maximum_fusion.dep_ref.a_ref.own_ref, bf16[4,144,256]{2,1,0:T(8,128)(2,1)S(1)} %collective-permute-done.5.b_ref.r1, ...), custom_call_target="tpu_custom_call" | custom-call | flops 6899999744 | tf_op jit(solution)/shard_map/hidden/pallas_call | solution.py:348
  44.8 0.5 collective-permute-start.9
  45.3 2.4 %collective-permute-done.11.b_ref.rest_4_ = bf16[576,256]{1,0:T(8,128)(2,1)S(1)} collective-permute-done((bf16[576,256]{1,0:T(8,128)(2,1)S(1)}, bf16[576,256]{1,0:T(8,128)(2,1)S(1)}, u32[]{:S(2)}, u32[]{:S(2)}) %collective-permute-start.11) | collective-permute-done | bytes 294944 | tf_op jit(solution)/shard_map/ppermute | solution.py:434
  47.7 0.5 turn.2
  48.2 0.2 copy-done.2
  48.4 0.1 collective-permute-start.14
  48.5 18.3 %collective-permute-done.9.b_ref.rest_6_ = bf16[576,256]{1,0:T(8,128)(2,1)S(1)} collective-permute-done((bf16[576,256]{1,0:T(8,128)(2,1)S(1)}, bf16[576,256]{1,0:T(8,128)(2,1)S(1)}, u32[]{:S(2)}, u32[]{:S(2)}) %collective-permute-start.9) | collective-permute-done | bytes 294944 | tf_op jit(solution)/shard_map/ppermute | solution.py:30
  66.9 0.4 turn.3
  67.3 0.2 copy-done.4
  67.6 0.7 copy-done.6
  68.3 4.8 %collective-permute-done.14.other_ref = bf16[576,256]{1,0:T(8,128)(2,1)S(1)} collective-permute-done((bf16[576,256]{1,0:T(8,128)(2,1)S(1)}, bf16[576,256]{1,0:T(8,128)(2,1)S(1)}, u32[]{:S(2)}, u32[]{:S(2)}) %collective-permute-start.14) | collective-permute-done | bytes 294944 | tf_op jit(solution)/shard_map/ppermute | solution.py:30
  73.1 5.6 %input_sums.1 = (f32[4,4,144,256]{3,2,1,0:T(8,128)S(1)}, bf16[4,4,144,256]{3,2,1,0:T(8,128)(2,1)}) custom-call(s32[3]{0:T(128)S(1)} %pad_add_fusion.at_ref, bf16[576,256]{1,0:T(8,128)(2,1)S(1)} %get-tuple-element.38.own_ref, bf16[576,256]{1,0:T(8,128)(2,1)S(1)} %collective-permute-done.14.other_ref, bf16[1152,4608]{1,0:T(8,128)(2,1)S(1)} %bitcast.42, ...), custom_call_target="tpu_custom_call" | custom-call | flops 6899999744 | tf_op jit(solution)/shard_map/input_sums/pallas_call | solution.py:385
  78.7 0.0 collective-permute-start.16
  78.8 1.6 %collective-permute-start.12 = (bf16[576,256]{1,0:T(8,128)(2,1)}, bf16[576,256]{1,0:T(8,128)(2,1)S(1)}, u32[]{:S(2)}, u32[]{:S(2)}) collective-permute-start(bf16[576,256]{1,0:T(8,128)(2,1)} %copy-done.7), channel_id=1, source_target_pairs={{0,0},{8,16},{16,8},{24,24},{1,1},{9,17},{17,9},{25,25},{2,2},{10,... | collective-permute-start | bytes 884744 | tf_op jit(solution)/shard_map/ppermute | solution.py:451
  80.4 0.9 collective-permute-start.13
  81.2 0.7 collective-permute-done.16
  81.9 1.8 %fusion.5 = (bf16[4,4,144,256]{3,2,1,0:T(8,128)(2,1)S(1)}, f32[4,4,144,256]{3,2,1,0:T(8,128)S(1)}) fusion(f32[4,4,144,256]{3,2,1,0:T(8,128)S(1)} %get-tuple-element.42, bf16[4,4,144,256]{3,2,1,0:T(8,128)(2,1)} %collective-permute-done.16), kind=kLoop, calls=%fused_computation.16 | loop fusion | flops 1769472 | bytes 7077888 | tf_op jit(solution)/shard_map/convert.5
  83.8 0.0 copy-start.9
  83.8 0.0 copy-start.11
  83.9 0.1 slice_bitcast_fusion.3
  83.9 3.0 %collective-permute-start.17 = (bf16[4,144,256]{2,1,0:T(8,128)(2,1)S(1)}, bf16[4,144,256]{2,1,0:T(8,128)(2,1)S(1)}, u32[]{:S(2)}, u32[]{:S(2)}) collective-permute-start(bf16[4,144,256]{2,1,0:T(8,128)(2,1)S(1)} %get-tuple-element.49), channel_id=1, source_target_pairs={{0,4},{2,6},{4,0},{6,2},{1,5},{3,7},{5,1},{7,3},{8,12},{10,14},{12... | collective-permute-start | bytes 884744 | tf_op jit(solution)/shard_map/ppermute | solution.py:35
  86.9 0.5 collective-permute-start.18
  87.4 2.7 %collective-permute-start.19 = (bf16[4,144,256]{2,1,0:T(8,128)(2,1)S(1)}, bf16[4,144,256]{2,1,0:T(8,128)(2,1)S(1)}, u32[]{:S(2)}, u32[]{:S(2)}) collective-permute-start(bf16[4,144,256]{2,1,0:T(8,128)(2,1)S(1)} %get-tuple-element.50), channel_id=1, source_target_pairs={{0,6},{2,0},{4,2},{6,4},{1,7},{3,1},{5,3},{7,5},{8,14},{10,8},{12,... | collective-permute-start | bytes 884744 | tf_op jit(solution)/shard_map/ppermute | solution.py:35
  90.2 2.9 %last.1 = (bf16[576,256]{1,0:T(8,128)(2,1)S(1)}, bf16[576,256]{1,0:T(8,128)(2,1)S(1)}, f32[144,128]{1,0:T(8,128)S(1)}, f32[144,128]{1,0:T(8,128)S(1)}) custom-call(s32[3]{0:T(128)S(1)} %pad_add_fusion.at_ref, s32[1]{0:T(128)} %bitcast.3.y0_ref, bf16[1152,256]{1,0:T(8,128)(2,1)S(1)} %copy-done, bf16[576,256]{1,0:T(8,128)(2,1)S(1)} %collective-permute-done.rec_ref, ...), custom_call_target="tpu_custom_call" | custom-call | flops 4600000000 | tf_op jit(solution)/shard_map/last/pallas_call | solution.py:463
  93.1 0.8 collective-permute-start.23
  93.9 3.6 %collective-permute-done.23 = f32[144,128]{1,0:T(8,128)S(1)} collective-permute-done((f32[144,128]{1,0:T(8,128)S(1)}, f32[144,128]{1,0:T(8,128)S(1)}, u32[]{:S(2)}, u32[]{:S(2)}) %collective-permute-start.23) | collective-permute-done | bytes 73760 | tf_op jit(solution)/shard_map/ppermute | solution.py:30
  97.5 1.3 %collective-permute-start.24 = (f32[144,128]{1,0:T(8,128)S(1)}, f32[144,128]{1,0:T(8,128)S(1)}, u32[]{:S(2)}, u32[]{:S(2)}) collective-permute-start(f32[144,128]{1,0:T(8,128)S(1)} %add.43), channel_id=1, source_target_pairs={{0,128},{64,192},{128,0},{192,64},{1,129},{65,193},{129,1},{193,65... | collective-permute-start | bytes 221192 | tf_op jit(solution)/shard_map/ppermute | solution.py:30
  98.8 4.6 %collective-permute-done.24 = f32[144,128]{1,0:T(8,128)S(1)} collective-permute-done((f32[144,128]{1,0:T(8,128)S(1)}, f32[144,128]{1,0:T(8,128)S(1)}, u32[]{:S(2)}, u32[]{:S(2)}) %collective-permute-start.24) | collective-permute-done | bytes 73760 | tf_op jit(solution)/shard_map/ppermute | solution.py:30
  103.5 6.1 %collective-permute-start.25 = (f32[144,128]{1,0:T(8,128)S(1)}, f32[144,128]{1,0:T(8,128)S(1)}, u32[]{:S(2)}, u32[]{:S(2)}) collective-permute-start(f32[144,128]{1,0:T(8,128)S(1)} %add.44), channel_id=1, source_target_pairs={{0,32},{32,0},{1,33},{33,1},{2,34},{34,2},{3,35},{35,3},{4,36},{36... | collective-permute-start | bytes 221192 | tf_op jit(solution)/shard_map/ppermute | solution.py:30
  109.6 5.5 %collective-permute-start.15 = (bf16[576,256]{1,0:T(8,128)(2,1)S(1)}, bf16[576,256]{1,0:T(8,128)(2,1)S(1)}, u32[]{:S(2)}, u32[]{:S(2)}) collective-permute-start(bf16[576,256]{1,0:T(8,128)(2,1)S(1)} %get-tuple-element.41), channel_id=1, source_target_pairs={{0,8},{8,0},{16,24},{24,16},{1,9},{9,1},{17,25},{25,17},{2,10},{10... | collective-permute-start | bytes 884744 | tf_op jit(solution)/shard_map/ppermute | solution.py:30
  115.1 0.8 collective-permute-start.26
  116.0 0.2 fusion.3
  116.2 3.3 %collective-permute-start.20 = (bf16[144,256]{1,0:T(8,128)(2,1)S(1)}, bf16[144,256]{1,0:T(8,128)(2,1)S(1)}, u32[]{:S(2)}, u32[]{:S(2)}) collective-permute-start(bf16[144,256]{1,0:T(8,128)(2,1)S(1)} %get-tuple-element.52), channel_id=1, source_target_pairs={{0,8},{8,0},{16,24},{24,16},{1,9},{9,1},{17,25},{25,17},{2,10},{10... | collective-permute-start | bytes 221192 | tf_op jit(solution)/shard_map/ppermute | solution.py:30
  119.5 0.6 collective-permute-start.21
  120.0 1.9 %collective-permute-start.22 = (bf16[144,256]{1,0:T(8,128)(2,1)S(1)}, bf16[144,256]{1,0:T(8,128)(2,1)S(1)}, u32[]{:S(2)}, u32[]{:S(2)}) collective-permute-start(bf16[144,256]{1,0:T(8,128)(2,1)S(1)} %get-tuple-element.53), channel_id=1, source_target_pairs={{0,24},{8,16},{16,8},{24,0},{1,25},{9,17},{17,9},{25,1},{2,26},{10... | collective-permute-start | bytes 221192 | tf_op jit(solution)/shard_map/ppermute | solution.py:30
  121.9 2.3 %unpack.1 = f32[2,32,32,36]{3,2,1,0:T(8,128)} custom-call(s32[1]{0:T(128)} %bitcast.3.y0_ref, f32[144,128]{1,0:T(8,128)S(1)} %add.45.mine_ref, f32[144,128]{1,0:T(8,128)S(1)} %collective-permute-done.26.other_ref), custom_call_target="tpu_custom_call" | custom-call | flops 2300000000 | tf_op jit(solution)/shard_map/unpack/pallas_call | solution.py:494
  124.2 0.7 collective-permute-done.15.other_ref
  124.9 1.4 %join.1 = bf16[1152,256]{1,0:T(8,128)(2,1)} custom-call(s32[3]{0:T(128)S(1)} %pad_add_fusion.at_ref, bf16[576,256]{1,0:T(8,128)(2,1)S(1)} %get-tuple-element.40.own_ref, bf16[576,256]{1,0:T(8,128)(2,1)S(1)} %collective-permute-done.15.other_ref), custom_call_target="tpu_custom_call" | custom-call | tf_op jit(solution)/shard_map/join/pallas_call | solution.py:482
  126.3 0.5 collective-permute-done.22
  126.8 0.7 fusion.2
  (63 shorter events, 0.2 us)
Async XLA Ops:
  0.6 19.1 %copy-start.1 = (f32[2,36,32,32]{1,3,2,0:T(8,128)S(1)}, f32[2,36,32,32]{1,3,2,0:T(8,128)}, u32[]{:S(2)}) copy-start(f32[2,36,32,32]{1,3,2,0:T(8,128)} %param.9) | copy-start | bytes 884740
  0.6 19.1 %copy-start.12 = (s32[2,32]{1,0:T(2,128)S(1)}, s32[2,32]{1,0:T(2,128)}, u32[]{:S(2)}) copy-start(s32[2,32]{1,0:T(2,128)} %perm_ref.3) | copy-start | bytes 772
  0.7 8.5 %collective-permute-start.2 = (bf16[144,256]{1,0:T(8,128)(2,1)}, bf16[144,256]{1,0:T(8,128)(2,1)S(1)}, u32[]{:S(2)}, u32[]{:S(2)}) collective-permute-start(bf16[144,256]{1,0:T(8,128)(2,1)} %bitcast.47), channel_id=1, source_target_pairs={{0,8},{8,0},{16,24},{24,16},{1,9},{9,1},{17,25},{25,17},{2,10},{10... | collective-permute-start | bytes 221192 | tf_op jit(solution)/shard_map/ppermute | solution.py:30
  2.7 8.6 %collective-permute-start.3 = (bf16[144,256]{1,0:T(8,128)(2,1)}, bf16[144,256]{1,0:T(8,128)(2,1)S(1)}, u32[]{:S(2)}, u32[]{:S(2)}) collective-permute-start(bf16[144,256]{1,0:T(8,128)(2,1)} %bitcast.48), channel_id=1, source_target_pairs={{0,16},{8,24},{16,0},{24,8},{1,17},{9,25},{17,1},{25,9},{2,18},{10... | collective-permute-start | bytes 221192 | tf_op jit(solution)/shard_map/ppermute | solution.py:30
  5.9 7.1 %collective-permute-start.4 = (bf16[144,256]{1,0:T(8,128)(2,1)}, bf16[144,256]{1,0:T(8,128)(2,1)S(1)}, u32[]{:S(2)}, u32[]{:S(2)}) collective-permute-start(bf16[144,256]{1,0:T(8,128)(2,1)} %bitcast.49), channel_id=1, source_target_pairs={{0,24},{8,16},{16,8},{24,0},{1,25},{9,17},{17,9},{25,1},{2,26},{10... | collective-permute-start | bytes 221192 | tf_op jit(solution)/shard_map/ppermute | solution.py:30
  6.9 20.2 %collective-permute-start = (bf16[576,256]{1,0:T(8,128)(2,1)S(1)}, bf16[576,256]{1,0:T(8,128)(2,1)S(1)}, u32[]{:S(2)}, u32[]{:S(2)}) collective-permute-start(bf16[576,256]{1,0:T(8,128)(2,1)S(1)} %bitcast.46), channel_id=1, source_target_pairs={{0,8},{8,0},{16,24},{24,16},{1,9},{9,1},{17,25},{25,17},{2,10},{10... | collective-permute-start | bytes 884744 | tf_op jit(solution)/shard_map/ppermute | solution.py:30
  7.6 19.6 %collective-permute-start.1 = (f32[16,1152]{1,0:T(8,128)}, f32[16,1152]{1,0:T(8,128)S(1)}, u32[]{:S(2)}, u32[]{:S(2)}) collective-permute-start(f32[16,1152]{1,0:T(8,128)} %mine_ref.3), channel_id=1, source_target_pairs={{0,8},{8,0},{16,24},{24,16},{1,9},{9,1},{17,25},{25,17},{2,10},{10... | collective-permute-start | bytes 221192 | tf_op jit(solution)/shard_map/ppermute | solution.py:30
  14.0 15.3 %collective-permute-start.5 = (bf16[4,144,256]{2,1,0:T(8,128)(2,1)S(1)}, bf16[4,144,256]{2,1,0:T(8,128)(2,1)S(1)}, u32[]{:S(2)}, u32[]{:S(2)}) collective-permute-start(bf16[4,144,256]{2,1,0:T(8,128)(2,1)S(1)} %pad_maximum_fusion.dep_ref.a_ref.own_ref), channel_id=1, source_target_pairs={{0,2},{2,4},{4,6},{6,0},{1,3},{3,5},{5,7},{7,1},{8,10},{10,12},{12... | collective-permute-start | bytes 884744 | tf_op jit(solution)/shard_map/ppermute | solution.py:35
  15.5 13.7 %collective-permute-start.6 = (bf16[4,144,256]{2,1,0:T(8,128)(2,1)S(1)}, bf16[4,144,256]{2,1,0:T(8,128)(2,1)S(1)}, u32[]{:S(2)}, u32[]{:S(2)}) collective-permute-start(bf16[4,144,256]{2,1,0:T(8,128)(2,1)S(1)} %pad_maximum_fusion.dep_ref.a_ref.own_ref), channel_id=1, source_target_pairs={{0,4},{2,6},{4,0},{6,2},{1,5},{3,7},{5,1},{7,3},{8,12},{10,14},{12... | collective-permute-start | bytes 884744 | tf_op jit(solution)/shard_map/ppermute | solution.py:35
  18.3 11.0 %collective-permute-start.7 = (bf16[4,144,256]{2,1,0:T(8,128)(2,1)S(1)}, bf16[4,144,256]{2,1,0:T(8,128)(2,1)S(1)}, u32[]{:S(2)}, u32[]{:S(2)}) collective-permute-start(bf16[4,144,256]{2,1,0:T(8,128)(2,1)S(1)} %pad_maximum_fusion.dep_ref.a_ref.own_ref), channel_id=1, source_target_pairs={{0,6},{2,0},{4,2},{6,4},{1,7},{3,1},{5,3},{7,5},{8,14},{10,8},{12,... | collective-permute-start | bytes 884744 | tf_op jit(solution)/shard_map/ppermute | solution.py:35
  19.7 7.5 %copy-start = (bf16[1152,256]{1,0:T(8,128)(2,1)S(1)}, bf16[1152,256]{1,0:T(8,128)(2,1)}, u32[]{:S(2)}) copy-start(bf16[1152,256]{1,0:T(8,128)(2,1)} %grad_ref.3) | copy-start | bytes 1769476
  19.7 7.5 %copy-start.8 = (f32[16,1152]{1,0:T(8,128)S(1)}, f32[16,1152]{1,0:T(8,128)}, u32[]{:S(2)}) copy-start(f32[16,1152]{1,0:T(8,128)} %mine_ref.3) | copy-start | bytes 221188
  19.7 7.5 %copy-start.13 = (s32[256]{0:T(256)S(1)}, s32[256]{0:T(256)}, u32[]{:S(2)}) copy-start(s32[256]{0:T(256)} %param.11) | copy-start | bytes 3076
  27.1 2.1 %copy-start.10 = (f32[16,1152]{1,0:T(8,128)}, f32[16,1152]{1,0:T(8,128)S(1)}, u32[]{:S(2)}) copy-start(f32[16,1152]{1,0:T(8,128)S(1)} %collective-permute-done.1.theirs_ref) | copy-start | bytes 221188
  29.3 11.9 %slice-start = ((s8[10616832]{0:T(1024)(128)(4,1)}), s8[4194304]{0:T(1024)(128)(4,1)S(1)}, s32[]{:S(2)}) async-start(s8[10616832]{0:T(1024)(128)(4,1)} %bitcast.41), calls=%async_computation | async-start | bytes 8388608
  29.4 11.8 %collective-permute-start.8 = (bf16[4,4,144,256]{3,2,1,0:T(8,128)(2,1)S(1)}, bf16[4,4,144,256]{3,2,1,0:T(8,128)(2,1)S(1)}, u32[]{:S(2)}, u32[]{:S(2)}) collective-permute-start(bf16[4,4,144,256]{3,2,1,0:T(8,128)(2,1)S(1)} %gather.1), channel_id=1, source_target_pairs={{0,1},{1,0},{2,3},{3,2},{4,5},{5,4},{6,7},{7,6},{8,9},{9,8},{10,11... | collective-permute-start | bytes 3538952 | tf_op jit(solution)/shard_map/ppermute | solution.py:30
  29.5 15.8 %collective-permute-start.10 = (bf16[576,256]{1,0:T(8,128)(2,1)S(1)}, bf16[576,256]{1,0:T(8,128)(2,1)S(1)}, u32[]{:S(2)}, u32[]{:S(2)}) collective-permute-start(bf16[576,256]{1,0:T(8,128)(2,1)S(1)} %get-tuple-element.26.dep_ref), channel_id=1, source_target_pairs={{0,0},{8,16},{16,8},{24,24},{1,1},{9,17},{17,9},{25,25},{2,2},{10,... | collective-permute-start | bytes 884744 | tf_op jit(solution)/shard_map/ppermute | solution.py:433
  30.3 17.4 %collective-permute-start.11 = (bf16[576,256]{1,0:T(8,128)(2,1)S(1)}, bf16[576,256]{1,0:T(8,128)(2,1)S(1)}, u32[]{:S(2)}, u32[]{:S(2)}) collective-permute-start(bf16[576,256]{1,0:T(8,128)(2,1)S(1)} %get-tuple-element.31), channel_id=1, source_target_pairs={{16,0},{0,8},{24,16},{8,24},{17,1},{1,9},{25,17},{9,25},{18,2},{2,... | collective-permute-start | bytes 884744 | tf_op jit(solution)/shard_map/ppermute | solution.py:434
  34.2 7.0 %slice-start.1 = ((s8[10616832]{0:T(1024)(128)(4,1)}), s8[4194304]{0:T(1024)(128)(4,1)S(1)}, s32[]{:S(2)}) async-start(s8[10616832]{0:T(1024)(128)(4,1)} %bitcast.41), calls=%async_computation.1 | async-start | bytes 8388608
  34.2 7.0 %slice-start.2 = ((s8[10616832]{0:T(1024)(128)(4,1)}), s8[2228224]{0:T(1024)(128)(4,1)S(1)}, s32[]{:S(2)}) async-start(s8[10616832]{0:T(1024)(128)(4,1)} %bitcast.41), calls=%async_computation.2 | async-start | bytes 4456448
  38.3 1.1 copy-start.16
  39.3 1.0 copy-start.18
  40.4 0.8 copy-start.20
  44.8 22.1 %copy-start.14 = (bf16[576,256]{1,0:T(8,128)(2,1)}, bf16[576,256]{1,0:T(8,128)(2,1)S(1)}, u32[]{:S(2)}) copy-start(bf16[576,256]{1,0:T(8,128)(2,1)S(1)} %get-tuple-element.28.a_ref.rest_5_) | copy-start | bytes 884740
  44.8 22.1 %collective-permute-start.9 = (bf16[576,256]{1,0:T(8,128)(2,1)S(1)}, bf16[576,256]{1,0:T(8,128)(2,1)S(1)}, u32[]{:S(2)}, u32[]{:S(2)}) collective-permute-start(bf16[576,256]{1,0:T(8,128)(2,1)S(1)} %get-tuple-element.29.rest_0_), channel_id=1, source_target_pairs={{0,16},{8,24},{16,0},{24,8},{1,17},{9,25},{17,1},{25,9},{2,18},{10... | collective-permute-start | bytes 884744 | tf_op jit(solution)/shard_map/ppermute | solution.py:30
  47.7 0.7 copy-start.2
  48.4 24.7 %collective-permute-start.14 = (bf16[576,256]{1,0:T(8,128)(2,1)S(1)}, bf16[576,256]{1,0:T(8,128)(2,1)S(1)}, u32[]{:S(2)}, u32[]{:S(2)}) collective-permute-start(bf16[576,256]{1,0:T(8,128)(2,1)S(1)} %get-tuple-element.33.rest_0_), channel_id=1, source_target_pairs={{0,16},{8,24},{16,0},{24,8},{1,17},{9,25},{17,1},{25,9},{2,18},{10... | collective-permute-start | bytes 884744 | tf_op jit(solution)/shard_map/ppermute | solution.py:30
  66.9 0.7 copy-start.4
  67.6 0.7 copy-start.6
  68.3 10.4 %copy-start.7 = (bf16[576,256]{1,0:T(8,128)(2,1)}, bf16[576,256]{1,0:T(8,128)(2,1)S(1)}, u32[]{:S(2)}) copy-start(bf16[576,256]{1,0:T(8,128)(2,1)S(1)} %get-tuple-element.34.dep_ref) | copy-start | bytes 884740
  78.7 3.2 %collective-permute-start.16 = (bf16[4,4,144,256]{3,2,1,0:T(8,128)(2,1)}, bf16[4,4,144,256]{3,2,1,0:T(8,128)(2,1)}, u32[]{:S(2)}, u32[]{:S(2)}) collective-permute-start(bf16[4,4,144,256]{3,2,1,0:T(8,128)(2,1)} %get-tuple-element.39.rest_9_), channel_id=1, source_target_pairs={{0,1},{1,0},{2,3},{3,2},{4,5},{5,4},{6,7},{7,6},{8,9},{9,8},{10,11... | collective-permute-start | bytes 3538952 | tf_op jit(solution)/shard_map/ppermute | solution.py:30
  78.8 11.4 %collective-permute-start.12 = (bf16[576,256]{1,0:T(8,128)(2,1)}, bf16[576,256]{1,0:T(8,128)(2,1)S(1)}, u32[]{:S(2)}, u32[]{:S(2)}) collective-permute-start(bf16[576,256]{1,0:T(8,128)(2,1)} %copy-done.7), channel_id=1, source_target_pairs={{0,0},{8,16},{16,8},{24,24},{1,1},{9,17},{17,9},{25,25},{2,2},{10,... | collective-permute-start | bytes 884744 | tf_op jit(solution)/shard_map/ppermute | solution.py:451
  80.4 9.8 %collective-permute-start.13 = (bf16[576,256]{1,0:T(8,128)(2,1)}, bf16[576,256]{1,0:T(8,128)(2,1)S(1)}, u32[]{:S(2)}, u32[]{:S(2)}) collective-permute-start(bf16[576,256]{1,0:T(8,128)(2,1)} %copy-done.6), channel_id=1, source_target_pairs={{0,16},{8,0},{16,24},{24,8},{1,17},{9,1},{17,25},{25,9},{2,18},{10... | collective-permute-start | bytes 884744 | tf_op jit(solution)/shard_map/ppermute | solution.py:452
  81.9 8.2 %copy-start.17 = (bf16[2,9,2,128,128]{4,3,2,1,0:T(8,128)(2,1)S(1)}, bf16[2,9,2,128,128]{4,3,2,1,0:T(8,128)(2,1)}, u32[]{:S(2)}) copy-start(bf16[2,9,2,128,128]{4,3,2,1,0:T(8,128)(2,1)} %copy-done.16) | copy-start | bytes 3538948
  81.9 8.2 %copy-start.19 = (bf16[2,9,2,128,128]{4,3,2,1,0:T(8,128)(2,1)S(1)}, bf16[2,9,2,128,128]{4,3,2,1,0:T(8,128)(2,1)}, u32[]{:S(2)}) copy-start(bf16[2,9,2,128,128]{4,3,2,1,0:T(8,128)(2,1)} %copy-done.18) | copy-start | bytes 3538948
  83.8 6.4 %copy-start.3 = (bf16[576,256]{1,0:T(8,128)(2,1)S(1)}, bf16[576,256]{1,0:T(8,128)(2,1)}, u32[]{:S(2)}) copy-start(bf16[576,256]{1,0:T(8,128)(2,1)} %copy-done.2) | copy-start | bytes 884740
  83.8 6.4 %copy-start.5 = (bf16[576,256]{1,0:T(8,128)(2,1)S(1)}, bf16[576,256]{1,0:T(8,128)(2,1)}, u32[]{:S(2)}) copy-start(bf16[576,256]{1,0:T(8,128)(2,1)} %copy-done.4) | copy-start | bytes 884740
  83.8 6.4 %copy-start.9 = (f32[16,1152]{1,0:T(8,128)S(1)}, f32[16,1152]{1,0:T(8,128)}, u32[]{:S(2)}) copy-start(f32[16,1152]{1,0:T(8,128)} %mine_ref.3) | copy-start | bytes 221188
  83.8 6.4 %copy-start.11 = (f32[16,1152]{1,0:T(8,128)S(1)}, f32[16,1152]{1,0:T(8,128)}, u32[]{:S(2)}) copy-start(f32[16,1152]{1,0:T(8,128)} %copy-done.10) | copy-start | bytes 221188
  83.8 6.4 %copy-start.15 = (bf16[576,256]{1,0:T(8,128)(2,1)S(1)}, bf16[576,256]{1,0:T(8,128)(2,1)}, u32[]{:S(2)}) copy-start(bf16[576,256]{1,0:T(8,128)(2,1)} %copy-done.14) | copy-start | bytes 884740
  83.8 6.4 %copy-start.21 = (bf16[9,2,128,128]{3,2,1,0:T(8,128)(2,1)S(1)}, bf16[9,2,128,128]{3,2,1,0:T(8,128)(2,1)}, u32[]{:S(2)}) copy-start(bf16[9,2,128,128]{3,2,1,0:T(8,128)(2,1)} %copy-done.20) | copy-start | bytes 1769476
  83.9 32.0 %collective-permute-start.17 = (bf16[4,144,256]{2,1,0:T(8,128)(2,1)S(1)}, bf16[4,144,256]{2,1,0:T(8,128)(2,1)S(1)}, u32[]{:S(2)}, u32[]{:S(2)}) collective-permute-start(bf16[4,144,256]{2,1,0:T(8,128)(2,1)S(1)} %get-tuple-element.49), channel_id=1, source_target_pairs={{0,4},{2,6},{4,0},{6,2},{1,5},{3,7},{5,1},{7,3},{8,12},{10,14},{12... | collective-permute-start | bytes 884744 | tf_op jit(solution)/shard_map/ppermute | solution.py:35
  86.9 29.1 %collective-permute-start.18 = (bf16[4,144,256]{2,1,0:T(8,128)(2,1)S(1)}, bf16[4,144,256]{2,1,0:T(8,128)(2,1)S(1)}, u32[]{:S(2)}, u32[]{:S(2)}) collective-permute-start(bf16[4,144,256]{2,1,0:T(8,128)(2,1)S(1)} %get-tuple-element.51), channel_id=1, source_target_pairs={{0,2},{2,4},{4,6},{6,0},{1,3},{3,5},{5,7},{7,1},{8,10},{10,12},{12... | collective-permute-start | bytes 884744 | tf_op jit(solution)/shard_map/ppermute | solution.py:35
  87.4 28.6 %collective-permute-start.19 = (bf16[4,144,256]{2,1,0:T(8,128)(2,1)S(1)}, bf16[4,144,256]{2,1,0:T(8,128)(2,1)S(1)}, u32[]{:S(2)}, u32[]{:S(2)}) collective-permute-start(bf16[4,144,256]{2,1,0:T(8,128)(2,1)S(1)} %get-tuple-element.50), channel_id=1, source_target_pairs={{0,6},{2,0},{4,2},{6,4},{1,7},{3,1},{5,3},{7,5},{8,14},{10,8},{12,... | collective-permute-start | bytes 884744 | tf_op jit(solution)/shard_map/ppermute | solution.py:35
  93.1 4.4 %collective-permute-start.23 = (f32[144,128]{1,0:T(8,128)S(1)}, f32[144,128]{1,0:T(8,128)S(1)}, u32[]{:S(2)}, u32[]{:S(2)}) collective-permute-start(f32[144,128]{1,0:T(8,128)S(1)} %get-tuple-element.44), channel_id=1, source_target_pairs={{0,64},{64,0},{128,192},{192,128},{1,65},{65,1},{129,193},{193,129... | collective-permute-start | bytes 221192 | tf_op jit(solution)/shard_map/ppermute | solution.py:30
  97.5 5.9 %collective-permute-start.24 = (f32[144,128]{1,0:T(8,128)S(1)}, f32[144,128]{1,0:T(8,128)S(1)}, u32[]{:S(2)}, u32[]{:S(2)}) collective-permute-start(f32[144,128]{1,0:T(8,128)S(1)} %add.43), channel_id=1, source_target_pairs={{0,128},{64,192},{128,0},{192,64},{1,129},{65,193},{129,1},{193,65... | collective-permute-start | bytes 221192 | tf_op jit(solution)/shard_map/ppermute | solution.py:30
  103.5 11.6 %collective-permute-start.25 = (f32[144,128]{1,0:T(8,128)S(1)}, f32[144,128]{1,0:T(8,128)S(1)}, u32[]{:S(2)}, u32[]{:S(2)}) collective-permute-start(f32[144,128]{1,0:T(8,128)S(1)} %add.44), channel_id=1, source_target_pairs={{0,32},{32,0},{1,33},{33,1},{2,34},{34,2},{3,35},{35,3},{4,36},{36... | collective-permute-start | bytes 221192 | tf_op jit(solution)/shard_map/ppermute | solution.py:30
  109.6 15.3 %collective-permute-start.15 = (bf16[576,256]{1,0:T(8,128)(2,1)S(1)}, bf16[576,256]{1,0:T(8,128)(2,1)S(1)}, u32[]{:S(2)}, u32[]{:S(2)}) collective-permute-start(bf16[576,256]{1,0:T(8,128)(2,1)S(1)} %get-tuple-element.41), channel_id=1, source_target_pairs={{0,8},{8,0},{16,24},{24,16},{1,9},{9,1},{17,25},{25,17},{2,10},{10... | collective-permute-start | bytes 884744 | tf_op jit(solution)/shard_map/ppermute | solution.py:30
  115.1 6.8 %collective-permute-start.26 = (f32[144,128]{1,0:T(8,128)S(1)}, f32[144,128]{1,0:T(8,128)S(1)}, u32[]{:S(2)}, u32[]{:S(2)}) collective-permute-start(f32[144,128]{1,0:T(8,128)S(1)} %add.45.mine_ref), channel_id=1, source_target_pairs={{0,64},{64,0},{128,192},{192,128},{1,65},{65,1},{129,193},{193,129... | collective-permute-start | bytes 221192 | tf_op jit(solution)/shard_map/ppermute | solution.py:30
  116.2 10.1 %collective-permute-start.20 = (bf16[144,256]{1,0:T(8,128)(2,1)S(1)}, bf16[144,256]{1,0:T(8,128)(2,1)S(1)}, u32[]{:S(2)}, u32[]{:S(2)}) collective-permute-start(bf16[144,256]{1,0:T(8,128)(2,1)S(1)} %get-tuple-element.52), channel_id=1, source_target_pairs={{0,8},{8,0},{16,24},{24,16},{1,9},{9,1},{17,25},{25,17},{2,10},{10... | collective-permute-start | bytes 221192 | tf_op jit(solution)/shard_map/ppermute | solution.py:30
  119.5 6.9 %collective-permute-start.21 = (bf16[144,256]{1,0:T(8,128)(2,1)S(1)}, bf16[144,256]{1,0:T(8,128)(2,1)S(1)}, u32[]{:S(2)}, u32[]{:S(2)}) collective-permute-start(bf16[144,256]{1,0:T(8,128)(2,1)S(1)} %get-tuple-element.54), channel_id=1, source_target_pairs={{0,16},{8,24},{16,0},{24,8},{1,17},{9,25},{17,1},{25,9},{2,18},{10... | collective-permute-start | bytes 221192 | tf_op jit(solution)/shard_map/ppermute | solution.py:30
  120.0 6.8 %collective-permute-start.22 = (bf16[144,256]{1,0:T(8,128)(2,1)S(1)}, bf16[144,256]{1,0:T(8,128)(2,1)S(1)}, u32[]{:S(2)}, u32[]{:S(2)}) collective-permute-start(bf16[144,256]{1,0:T(8,128)(2,1)S(1)} %get-tuple-element.53), channel_id=1, source_target_pairs={{0,24},{8,16},{16,8},{24,0},{1,25},{9,17},{17,9},{25,1},{2,26},{10... | collective-permute-start | bytes 221192 | tf_op jit(solution)/shard_map/ppermute | solution.py:30

commit v3 on v2

--- a/solution.py
+++ b/solution.py
@@ -11,7 +11,7 @@
 BF16 = jnp.bfloat16
 GROUP = 4
 VMEM_LIMIT = 12 * 1024 * 1024
-WEIGHT_LIMIT = 24 * 1024 * 1024
+WEIGHT_LIMIT = 20 * 1024 * 1024
 
 VMEM = pl.BlockSpec(memory_space=pltpu.VMEM)
 SMEM = pl.BlockSpec(memory_space=pltpu.SMEM)
@@ -44,7 +44,7 @@
     return hi, (x - hi.astype(F32)).astype(BF16)
 
 
-def fill_kernel(k_ref, dep_ref, mat, raw):
+def eliminated(k_ref, mat, raw):
     n = k_ref.shape[1]
     blocks = k_ref.shape[3]
     raw[...] = jnp.zeros_like(raw)
@@ -97,8 +97,9 @@
     return jnp.where(diagonal, jnp.concatenate([jnp.concatenate(rows, 0)] * GROUP, 1), 0.0)
 
 
-def invert_kernel(at_ref, perm_ref, k_ref, dep_ref, turned, mt_ref, mat, raw):
-    fill_kernel(k_ref, dep_ref, mat, raw)
+def invert_kernel(at_ref, perm_ref, k_ref, *rest):
+    turned, mt_ref, mat, raw = rest[-4:]
+    eliminated(k_ref, mat, raw)
     n = k_ref.shape[1]
     groups = mt_ref.shape[0]
     for u in range(n):
@@ -141,13 +142,13 @@
             jax.ShapeDtypeStruct((n * 128, n), F32),
             jax.ShapeDtypeStruct((groups, 2, width, width), BF16),
         ),
-        in_specs=[SMEM] * 2 + [VMEM, ANY],
+        in_specs=[SMEM] * 2 + [VMEM] + [ANY] * len(after),
         out_specs=(VMEM, VMEM),
         scratch_shapes=[pltpu.VMEM((n * n, 128), F32), pltpu.VMEM((n * n, 128), F32)],
         compiler_params=PARAMS,
         cost_estimate=cost(7),
         name="invert",
-    )(place, section_perm, jnp.transpose(skew, (0, 2, 3, 1)), after)
+    )(place, section_perm, jnp.transpose(skew, (0, 2, 3, 1)), *after)
 
 
 def build(place, section_perm, turned, after):
@@ -227,7 +228,7 @@
 
 
 def cotangent_kernel(at_ref, grad_ref, rec_ref, mine_ref, theirs_ref, ids_ref, mt_ref, *rest):
-    oa_ref, ob_ref, sa_ref, sb_ref = rest
+    oa_ref, ob_ref, sa_ref, sb_ref = rest[1:]
     high = at_ref[0] % 2 == 1
     ids = ids_ref[...]
     sa_ref[...] = scale_rows(mine_ref, ids, high)
@@ -239,18 +240,18 @@
         put(oa_ref, ob_ref, g, groups, y.astype(BF16))
 
 
-def cotangent(place, out_grad, rec, mine, theirs, ids, mt):
+def cotangent(place, out_grad, rec, mine, theirs, ids, mt, after):
     shape = jax.ShapeDtypeStruct(rec.shape, BF16)
     return pl.pallas_call(
         cotangent_kernel,
         out_shape=(shape, shape),
-        in_specs=[SMEM] + [VMEM] * 6,
+        in_specs=[SMEM] + [VMEM] * 6 + [ANY],
         out_specs=(VMEM, VMEM),
         scratch_shapes=[pltpu.VMEM(rec.shape, F32)] * 2,
         compiler_params=PARAMS,
         cost_estimate=cost(3),
         name="cotangent",
-    )(place, out_grad, rec, mine, theirs, ids, mt)
+    )(place, out_grad, rec, mine, theirs, ids, mt, after)
 
 
 def last_kernel(norm, at_ref, y0_ref, grad_ref, rec_ref, mine_ref, theirs_ref, ids_ref, *rest):
@@ -298,7 +299,7 @@
     send_ref[...] = out_ref[pl.ds(pl.multiple_of((1 - y0) * size, 8), size), :]
 
 
-def unpack_kernel(y0_ref, mine_ref, other_ref, out_ref, packed, planes):
+def unpack_kernel(y0_ref, mine_ref, other_ref, dep_ref, out_ref, packed, planes):
     size = mine_ref.shape[0]
     y0 = y0_ref[0]
     packed[pl.ds(pl.multiple_of(y0 * size, 8), size), :] = mine_ref[...]
@@ -397,6 +398,82 @@
     )(place, own, other, weight, after)
 
 
+def fold_kernel(keep_ref, rec_ref, dep_ref, own_ref, *send_refs):
+    own_ref[...] = keep_ref[0] + rec_ref[0].astype(F32)
+    for d, ref in enumerate(send_refs):
+        ref[...] = (keep_ref[d + 1] + rec_ref[d + 1].astype(F32)).astype(BF16)
+
+
+def fold(keep, rec, after):
+    piece = keep.shape[1:]
+    return pl.pallas_call(
+        fold_kernel,
+        out_shape=(jax.ShapeDtypeStruct(piece, F32),) + (jax.ShapeDtypeStruct(piece, BF16),) * 3,
+        in_specs=[VMEM] * 2 + [ANY],
+        out_specs=(VMEM,) * 4,
+        compiler_params=PARAMS,
+        cost_estimate=cost(1),
+        name="fold",
+    )(keep, rec, after)
+
+
+def fold_last_kernel(own_ref, a_ref, b_ref, c_ref, keep_ref, *send_refs):
+    for k in range(4):
+        y = own_ref[k] + a_ref[k].astype(F32) + b_ref[k].astype(F32) + c_ref[k].astype(F32)
+        if k == 0:
+            keep_ref[...] = y
+        else:
+            send_refs[k - 1][...] = y.astype(BF16)
+
+
+def fold_last(own, a, b, c):
+    piece = own.shape[1:]
+    return pl.pallas_call(
+        fold_last_kernel,
+        out_shape=(jax.ShapeDtypeStruct(piece, F32),) + (jax.ShapeDtypeStruct(piece, BF16),) * 3,
+        in_specs=[VMEM] * 4,
+        out_specs=(VMEM,) * 4,
+        compiler_params=PARAMS,
+        cost_estimate=cost(1),
+        name="fold_last",
+    )(own, a, b, c)
+
+
+def load_kernel(w_hbm, dep_ref, out_ref, sem):
+    copy = pltpu.make_async_copy(w_hbm, out_ref, sem)
+    copy.start()
+    copy.wait()
+
+
+def load(weight, after):
+    return pl.pallas_call(
+        load_kernel,
+        out_shape=jax.ShapeDtypeStruct(weight.shape, weight.dtype),
+        in_specs=[HBM, ANY],
+        out_specs=VMEM,
+        scratch_shapes=[pltpu.SemaphoreType.DMA(())],
+        compiler_params=WEIGHT_PARAMS,
+        cost_estimate=cost(4),
+        name="load",
+    )(weight, after)
+
+
+def add_kernel(a_ref, b_ref, dep_ref, out_ref):
+    out_ref[...] = a_ref[...] + b_ref[...]
+
+
+def add(a, b, after):
+    return pl.pallas_call(
+        add_kernel,
+        out_shape=jax.ShapeDtypeStruct(a.shape, a.dtype),
+        in_specs=[VMEM] * 2 + [ANY],
+        out_specs=VMEM,
+        compiler_params=PARAMS,
+        cost_estimate=cost(0.2),
+        name="add",
+    )(a, b, after)
+
+
 def join_kernel(at_ref, own_ref, other_ref, out_ref):
     high = at_ref[0] % 2 == 1
     a, b = own_ref[...], other_ref[...]
@@ -427,9 +504,9 @@
     x2 = shift(along_z, "x", 2)
     x1 = shift(along_z, "x", 1)
     x3 = shift(along_z, "x", 3)
-    turned, mt1 = invert(place, section_perm, skew, along_z)
+    turned, mt1 = invert(place, section_perm, skew, (along_z,))
     ids = prefix_ids[None, :]
-    ga_out, gb_out = cotangent(place, out_grad, g_rec, prefix_scale, scale_rec, ids, mt1)
+    ga_out, gb_out = cotangent(place, out_grad, g_rec, prefix_scale, scale_rec, ids, mt1, along_z)
     ga = lax.ppermute(ga_out, "z", A_PAIRS)
     gb = lax.ppermute(gb_out, "z", B_BACK)
     by_x = pl.pallas_call(
@@ -442,19 +519,17 @@
         name="gather",
     )(along_z, x1, x2, x3, ga_out)
     by_core = xor(by_x, "c", 1)
-    m0, mt0, m1, left, right = build(place, section_perm, turned, ga_out)
     z_own, z_send = hidden_halves(place, along_z, x1, x2, x3, by_core, weight)
     z_rec = xor(z_send, "z", 2)
-    h_own, h_send = turn(ga, gb, mt0, (z_send,))
+    m0, mt0, m1, left, right = build(place, section_perm, turned, z_send)
+    held = load(weight, z_send)
+    h_own, h_send = turn(ga, gb, mt0, (held,))
     h_rec = xor(h_send, "z", 2)
     za_out, zb = turn(z_own, z_rec, m0, (h_send,))
     za = lax.ppermute(za_out, "z", A_PAIRS)
     zb = lax.ppermute(zb, "z", B_PAIRS)
-    keep, send = input_parts(place, h_own, h_rec, weight, za_out)
-    part = keep + xor(send, "c", 1).astype(F32)
-    total = part[0] + sum(shift(part[d].astype(BF16), "x", d).astype(F32) for d in (2, 1, 3))
-    final = total[0] + sum(xor(total[k].astype(BF16), "z", k).astype(F32) for k in (1, 2, 3))
-    input_grad = final.astype(BF16)
+    keep, send = input_parts(place, h_own, h_rec, held, za_out)
+    send_rec = xor(send, "c", 1)
     rows_all = cols * lax.axis_size("y") * lax.axis_size("h")
     groups = left.shape[1]
     y0 = lax.bitwise_and(yi, 1).reshape(1)
@@ -472,7 +547,7 @@
             pltpu.VMEM(za.shape, F32),
         ],
         compiler_params=PARAMS,
-        cost_estimate=cost(4),
+        cost_estimate=cost(30),
         name="last",
     )(
         place, y0, out_grad, g_rec, prefix_scale, scale_rec, ids,
@@ -485,25 +560,30 @@
         in_specs=[SMEM] + [VMEM] * 2,
         out_specs=VMEM,
         compiler_params=PARAMS,
+        cost_estimate=cost(0.01),
         name="join",
     )(place, j_own, j_rec)
+    own, to1, to2, to3 = fold(keep, send_rec, half_send)
     half = half + xor(half_send, "y", 1)
-    half = half + xor(half, "y", 2)
-    half = half + xor(half, "h", 1)
+    ours, z1, z2, z3 = fold_last(own, shift(to2, "x", 2), shift(to1, "x", 1), shift(to3, "x", 3))
+    half = add(half, xor(half, "y", 2), pltpu.with_memory_space_constraint(judged, pltpu.HBM))
+    half = add(half, xor(half, "h", 1), ours)
+    final = ours + sum(xor(part, "z", k).astype(F32) for k, part in ((1, z1), (2, z2), (3, z3)))
+    input_grad = final.astype(BF16)
     other = xor(half, "y", 1)
     skew_grad = pl.pallas_call(
         unpack_kernel,
         out_shape=jax.ShapeDtypeStruct((2, n, n, GROUP * groups), F32),
-        in_specs=[SMEM] + [VMEM] * 2,
+        in_specs=[SMEM] + [VMEM] * 2 + [ANY],
         out_specs=VMEM,
         scratch_shapes=[
             pltpu.VMEM((groups * n, width), F32),
             pltpu.VMEM((n * n, GROUP * groups), F32),
         ],
         compiler_params=PARAMS,
-        cost_estimate=cost(2),
+        cost_estimate=cost(0.01),
         name="unpack",
-    )(y0, half, other)
+    )(y0, half, other, input_grad)
     return judged, input_grad, jnp.transpose(skew_grad, (0, 3, 1, 2))
 
 

time: 128 us -> 125 us (0.977)
  local copies, waits for them, and re-layouts: 5.24 us -> 11.5 us
  starting transfers between devices: 47.6 us -> 43.1 us
  other arithmetic: 3.72 us -> 1.05 us
  waiting for transfers between devices: 39.6 us -> 37.1 us
    ppermute x17, waiting for transfers between devices: 37.2 us -> 29.9 us  [xor(): lax.ppermute(x, axis, [(i, i ^ k) for i in range(lax.axis_size(axis))])]
    unnamed x50 -> x44, local copies, waits for them, and re-layouts: 4.18 us -> 10.6 us
    ppermute x1, waiting for transfers between devices: 2.37 us -> 7.16 us  [per_device(): gb = lax.ppermute(gb_out, 'z', B_BACK)]
    ppermute x17, starting transfers between devices: 28.5 us -> 24.3 us  [xor(): lax.ppermute(x, axis, [(i, i ^ k) for i in range(lax.axis_size(axis))])]
    another operation x2 -> x0, other arithmetic: 2.02 us -> none
    pallas_call x0 -> x5, Pallas kernels: none -> 1.3 us  [the longest x1 0.89 us: load(): pl.pallas_call(load_kernel, out_shape=jax.ShapeDtypeStruct(weight.shape,...]
  transfers between devices with their start and end apart: 27 -> 27, of which waited for: 10 -> 10; matrix products, arithmetic and copies ran while one was open for 3% -> 2% of each run, Pallas kernels for 19% -> 23%
where the time goes in v3:
time: 125 us; the launch traced here: 124 us
  starting transfers between devices  43.1 us (34%)
  waiting for transfers between devices  37.1 us (30%)
  Pallas kernels  30.4 us (24%)
  local copies, waits for them, and re-layouts  11.5 us (9%)
    ppermute x17, waiting for transfers between devices, xor(): lax.ppermute(x, axis, [(i, i ^ k) for i in range(lax.axis_size(axis))])  29.9 us
    ppermute x17, starting transfers between devices, xor(): lax.ppermute(x, axis, [(i, i ^ k) for i in range(lax.axis_size(axis))])  24.3 us
    ppermute x6, starting transfers between devices, shift(): return lax.ppermute(x, axis, [(i, (i + k) % n) for i in range(n)])  11.9 us
    unnamed x44, local copies, waits for them, and re-layouts  10.6 us
    pallas_call x1, Pallas kernels, invert(): pl.pallas_call(invert_kernel, out_shape=(jax.ShapeDtypeStruct((n * 128, n...  7.38 us
    ppermute x1, waiting for transfers between devices, per_device(): gb = lax.ppermute(gb_out, 'z', B_BACK)  7.16 us
    pallas_call x1, Pallas kernels, input_parts(): pl.pallas_call(input_kernel, out_shape=(jax.ShapeDtypeStruct(dims, F32),...  4.48 us
    pallas_call x1, Pallas kernels, build(): pl.pallas_call(build_kernel, out_shape=(one, one, one, two, two), in_spec...  4.1 us
  transfers between devices with their start and end apart: 27, of which 10 were waited for; matrix products, arithmetic and copies ran while one was open for 2% of the time, Pallas kernels for 23%

profile of v3, /device:TPU:24, one launch (start us, length us, event | category | flops | bytes accessed | tf_op | source)
XLA Modules:
  0.0 124.2 jit_solution(13231814207044094084)
XLA Ops:
  0.7 2.0 %collective-permute-start.2 = (bf16[144,256]{1,0:T(8,128)(2,1)}, bf16[144,256]{1,0:T(8,128)(2,1)S(1)}, u32[]{:S(2)}, u32[]{:S(2)}) collective-permute-start(bf16[144,256]{1,0:T(8,128)(2,1)} %bitcast.25), channel_id=1, source_target_pairs={{0,8},{8,0},{16,24},{24,16},{1,9},{9,1},{17,25},{25,17},{2,10},{10... | collective-permute-start | bytes 221192 | tf_op jit(solution)/shard_map/ppermute | solution.py:30
  2.7 3.3 %collective-permute-start.3 = (bf16[144,256]{1,0:T(8,128)(2,1)}, bf16[144,256]{1,0:T(8,128)(2,1)S(1)}, u32[]{:S(2)}, u32[]{:S(2)}) collective-permute-start(bf16[144,256]{1,0:T(8,128)(2,1)} %bitcast.26), channel_id=1, source_target_pairs={{0,16},{8,24},{16,0},{24,8},{1,17},{9,25},{17,1},{25,9},{2,18},{10... | collective-permute-start | bytes 221192 | tf_op jit(solution)/shard_map/ppermute | solution.py:30
  5.9 1.0 constant_dynamic-slice_fusion
  6.9 0.7 collective-permute-start
  7.6 1.5 %collective-permute-start.1 = (f32[16,1152]{1,0:T(8,128)}, f32[16,1152]{1,0:T(8,128)S(1)}, u32[]{:S(2)}, u32[]{:S(2)}) collective-permute-start(f32[16,1152]{1,0:T(8,128)} %mine_ref.3), channel_id=1, source_target_pairs={{0,8},{8,0},{16,24},{24,16},{1,9},{9,1},{17,25},{25,17},{2,10},{10... | collective-permute-start | bytes 221192 | tf_op jit(solution)/shard_map/ppermute | solution.py:30
  9.0 0.1 pad_add_fusion.at_ref
  9.1 2.2 %collective-permute-done.3 = bf16[144,256]{1,0:T(8,128)(2,1)S(1)} collective-permute-done((bf16[144,256]{1,0:T(8,128)(2,1)}, bf16[144,256]{1,0:T(8,128)(2,1)S(1)}, u32[]{:S(2)}, u32[]{:S(2)}) %collective-permute-start.3) | collective-permute-done | bytes 73760 | tf_op jit(solution)/shard_map/ppermute | solution.py:30
  11.3 1.8 %collective-permute-done.4 = bf16[144,256]{1,0:T(8,128)(2,1)S(1)} collective-permute-done((bf16[144,256]{1,0:T(8,128)(2,1)}, bf16[144,256]{1,0:T(8,128)(2,1)S(1)}, u32[]{:S(2)}, u32[]{:S(2)}) %collective-permute-start.4) | collective-permute-done | bytes 73760 | tf_op jit(solution)/shard_map/ppermute | solution.py:30
  13.1 0.9 pad_maximum_fusion.rest_0_.a_ref.own_ref
  14.0 1.6 %collective-permute-start.5 = (bf16[4,144,256]{2,1,0:T(8,128)(2,1)S(1)}, bf16[4,144,256]{2,1,0:T(8,128)(2,1)S(1)}, u32[]{:S(2)}, u32[]{:S(2)}) collective-permute-start(bf16[4,144,256]{2,1,0:T(8,128)(2,1)S(1)} %pad_maximum_fusion.rest_0_.a_ref.own_ref), channel_id=1, source_target_pairs={{0,2},{2,4},{4,6},{6,0},{1,3},{3,5},{5,7},{7,1},{8,10},{10,12},{12... | collective-permute-start | bytes 884744 | tf_op jit(solution)/shard_map/ppermute | solution.py:35
  15.5 2.7 %collective-permute-start.6 = (bf16[4,144,256]{2,1,0:T(8,128)(2,1)S(1)}, bf16[4,144,256]{2,1,0:T(8,128)(2,1)S(1)}, u32[]{:S(2)}, u32[]{:S(2)}) collective-permute-start(bf16[4,144,256]{2,1,0:T(8,128)(2,1)S(1)} %pad_maximum_fusion.rest_0_.a_ref.own_ref), channel_id=1, source_target_pairs={{0,4},{2,6},{4,0},{6,2},{1,5},{3,7},{5,1},{7,3},{8,12},{10,14},{12... | collective-permute-start | bytes 884744 | tf_op jit(solution)/shard_map/ppermute | solution.py:35
  18.3 1.4 %collective-permute-start.7 = (bf16[4,144,256]{2,1,0:T(8,128)(2,1)S(1)}, bf16[4,144,256]{2,1,0:T(8,128)(2,1)S(1)}, u32[]{:S(2)}, u32[]{:S(2)}) collective-permute-start(bf16[4,144,256]{2,1,0:T(8,128)(2,1)S(1)} %pad_maximum_fusion.rest_0_.a_ref.own_ref), channel_id=1, source_target_pairs={{0,6},{2,0},{4,2},{6,4},{1,7},{3,1},{5,3},{7,5},{8,14},{10,8},{12,... | collective-permute-start | bytes 884744 | tf_op jit(solution)/shard_map/ppermute | solution.py:35
  19.7 0.0 slice-start
  19.8 7.4 %invert.1 = (f32[4096,32]{1,0:T(8,128)S(1)}, bf16[9,2,128,128]{3,2,1,0:T(8,128)(2,1)S(1)}) custom-call(s32[3]{0:T(128)S(1)} %pad_add_fusion.at_ref, s32[2,32]{1,0:T(2,128)S(1)} %copy-done.6, f32[2,32,32,36]{3,2,1,0:T(8,128)S(1)} %bitcast.20, bf16[4,144,256]{2,1,0:T(8,128)(2,1)S(1)} %pad_maximum_fusion.rest_0_.a_ref.own_ref), custom_call_target="tpu_custom_call" | custom-call | flops 8049999872 | tf_op jit(solution)/shard_map/invert/pallas_call | solution.py:139
  27.2 0.0 slice-start.2
  27.2 2.1 %cotangent.1 = (bf16[576,256]{1,0:T(8,128)(2,1)S(1)}, bf16[576,256]{1,0:T(8,128)(2,1)S(1)}) custom-call(s32[3]{0:T(128)S(1)} %pad_add_fusion.at_ref, bf16[1152,256]{1,0:T(8,128)(2,1)S(1)} %copy-done.3, bf16[576,256]{1,0:T(8,128)(2,1)S(1)} %collective-permute-done.rec_ref, f32[16,1152]{1,0:T(8,128)S(1)} %copy-done.5, ...), custom_call_target="tpu_custom_call" | custom-call | flops 3449999872 | tf_op jit(solution)/shard_map/cotangent/pallas_call | solution.py:245
  29.3 0.1 gather.1
  29.4 0.1 collective-permute-start.8
  29.5 0.7 collective-permute-start.10
  30.2 3.5 %collective-permute-start.11 = (bf16[576,256]{1,0:T(8,128)(2,1)S(1)}, bf16[576,256]{1,0:T(8,128)(2,1)S(1)}, u32[]{:S(2)}, u32[]{:S(2)}) collective-permute-start(bf16[576,256]{1,0:T(8,128)(2,1)S(1)} %get-tuple-element.39), channel_id=1, source_target_pairs={{16,0},{0,8},{24,16},{8,24},{17,1},{1,9},{25,17},{9,25},{18,2},{2,... | collective-permute-start | bytes 884744 | tf_op jit(solution)/shard_map/ppermute | solution.py:511
  33.7 3.6 %hidden.1 = (bf16[576,256]{1,0:T(8,128)(2,1)S(1)}, bf16[576,256]{1,0:T(8,128)(2,1)S(1)}) custom-call(s32[3]{0:T(128)S(1)} %pad_add_fusion.at_ref, bf16[4,144,256]{2,1,0:T(8,128)(2,1)S(1)} %pad_maximum_fusion.rest_0_.a_ref.own_ref, bf16[4,144,256]{2,1,0:T(8,128)(2,1)S(1)} %collective-permute-done.5.b_ref.r1, ...), custom_call_target="tpu_custom_call" | custom-call | flops 6899999744 | tf_op jit(solution)/shard_map/hidden/pallas_call | solution.py:349
  37.4 0.7 copy-done.10
  38.1 0.4 collective-permute-start.9
  38.5 4.1 %build.1 = (bf16[9,2,128,128]{3,2,1,0:T(8,128)(2,1)S(1)}, bf16[9,2,128,128]{3,2,1,0:T(8,128)(2,1)S(1)}, bf16[9,2,128,128]{3,2,1,0:T(8,128)(2,1)S(1)}, bf16[2,9,2...) custom-call(s32[3]{0:T(128)S(1)} %pad_add_fusion.at_ref, s32[2,32]{1,0:T(2,128)S(1)} %copy-done.6, ...), custom_call_target="tpu_custom_call" | custom-call | flops 5750000128 | tf_op jit(solution)/shard_map/build/pallas_call | solution.py:160
  42.6 0.8 copy-done.8
  43.4 1.0 copy-done.13
  44.5 1.1 copy-done.15
  45.5 0.8 copy-done.17
  46.4 0.9 load.1.rest_0_.w_ref
  47.3 7.2 %collective-permute-done.11.b_ref.rest_4_ = bf16[576,256]{1,0:T(8,128)(2,1)S(1)} collective-permute-done((bf16[576,256]{1,0:T(8,128)(2,1)S(1)}, bf16[576,256]{1,0:T(8,128)(2,1)S(1)}, u32[]{:S(2)}, u32[]{:S(2)}) %collective-permute-start.11) | collective-permute-done | bytes 294944 | tf_op jit(solution)/shard_map/ppermute | solution.py:511
  54.4 0.4 turn.2
  54.9 0.1 collective-permute-start.14
  55.0 12.1 %collective-permute-done.9.b_ref.rest_6_ = bf16[576,256]{1,0:T(8,128)(2,1)S(1)} collective-permute-done((bf16[576,256]{1,0:T(8,128)(2,1)S(1)}, bf16[576,256]{1,0:T(8,128)(2,1)S(1)}, u32[]{:S(2)}, u32[]{:S(2)}) %collective-permute-start.9) | collective-permute-done | bytes 294944 | tf_op jit(solution)/shard_map/ppermute | solution.py:30
  67.1 1.1 copy-done.9
  68.1 1.0 copy-done.11
  69.1 0.5 turn.3
  69.6 0.7 collective-permute-start.12
  70.2 1.9 %collective-permute-start.13 = (bf16[576,256]{1,0:T(8,128)(2,1)S(1)}, bf16[576,256]{1,0:T(8,128)(2,1)S(1)}, u32[]{:S(2)}, u32[]{:S(2)}) collective-permute-start(bf16[576,256]{1,0:T(8,128)(2,1)S(1)} %get-tuple-element.43), channel_id=1, source_target_pairs={{0,16},{8,0},{16,24},{24,8},{1,17},{9,1},{17,25},{25,9},{2,18},{10... | collective-permute-start | bytes 884744 | tf_op jit(solution)/shard_map/ppermute | solution.py:530
  72.2 1.2 collective-permute-done.14.other_ref
  73.4 4.0 %copy-done.1 = bf16[1152,4608]{1,0:T(8,128)(2,1)S(1)} copy-done((bf16[1152,4608]{1,0:T(8,128)(2,1)S(1)}, bf16[1152,4608]{1,0:T(8,128)(2,1)}, u32[]{:S(2)}) %copy-start.1) | copy-done | bytes 10616856
  77.4 4.5 %input_sums.1 = (f32[4,4,144,256]{3,2,1,0:T(8,128)S(1)}, bf16[4,4,144,256]{3,2,1,0:T(8,128)(2,1)S(1)}) custom-call(s32[3]{0:T(128)S(1)} %pad_add_fusion.at_ref, bf16[576,256]{1,0:T(8,128)(2,1)S(1)} %get-tuple-element.46.own_ref, bf16[576,256]{1,0:T(8,128)(2,1)S(1)} %collective-permute-done.14.other_ref, bf16[1152,4608]{1,0:T(8,128)(2,1)S(1)} %copy-done.1, ...), custom_call_target="tpu_custom_call" | custom-call | flops 6899999744 | tf_op jit(solution)/shard_map/input_sums/pallas_call | solution.py:386
  81.9 0.1 collective-permute-start.16
  82.1 2.8 %last.1 = (bf16[576,256]{1,0:T(8,128)(2,1)S(1)}, bf16[576,256]{1,0:T(8,128)(2,1)S(1)}, f32[144,128]{1,0:T(8,128)S(1)}, f32[144,128]{1,0:T(8,128)S(1)}) custom-call(s32[3]{0:T(128)S(1)} %pad_add_fusion.at_ref, s32[1]{0:T(128)} %bitcast.3.y0_ref, bf16[1152,256]{1,0:T(8,128)(2,1)S(1)} %copy-done.3, bf16[576,256]{1,0:T(8,128)(2,1)S(1)} %collective-permute-done.rec_ref, ...), custom_call_target="tpu_custom_call" | custom-call | flops 34500001792 | tf_op jit(solution)/shard_map/last/pallas_call | solution.py:538
  84.9 4.2 %collective-permute-start.15 = (bf16[576,256]{1,0:T(8,128)(2,1)S(1)}, bf16[576,256]{1,0:T(8,128)(2,1)S(1)}, u32[]{:S(2)}, u32[]{:S(2)}) collective-permute-start(bf16[576,256]{1,0:T(8,128)(2,1)S(1)} %get-tuple-element.49), channel_id=1, source_target_pairs={{0,8},{8,0},{16,24},{24,16},{1,9},{9,1},{17,25},{25,17},{2,10},{10... | collective-permute-start | bytes 884744 | tf_op jit(solution)/shard_map/ppermute | solution.py:30
  89.1 0.3 fold.1
  89.4 3.0 %collective-permute-start.17 = (bf16[4,144,256]{2,1,0:T(8,128)(2,1)S(1)}, bf16[4,144,256]{2,1,0:T(8,128)(2,1)S(1)}, u32[]{:S(2)}, u32[]{:S(2)}) collective-permute-start(bf16[4,144,256]{2,1,0:T(8,128)(2,1)S(1)} %get-tuple-element.53), channel_id=1, source_target_pairs={{0,4},{2,6},{4,0},{6,2},{1,5},{3,7},{5,1},{7,3},{8,12},{10,14},{12... | collective-permute-start | bytes 884744 | tf_op jit(solution)/shard_map/ppermute | solution.py:35
  92.4 0.5 collective-permute-start.18
  92.8 2.8 %collective-permute-start.19 = (bf16[4,144,256]{2,1,0:T(8,128)(2,1)S(1)}, bf16[4,144,256]{2,1,0:T(8,128)(2,1)S(1)}, u32[]{:S(2)}, u32[]{:S(2)}) collective-permute-start(bf16[4,144,256]{2,1,0:T(8,128)(2,1)S(1)} %get-tuple-element.55), channel_id=1, source_target_pairs={{0,6},{2,0},{4,2},{6,4},{1,7},{3,1},{5,3},{7,5},{8,14},{10,8},{12,... | collective-permute-start | bytes 884744 | tf_op jit(solution)/shard_map/ppermute | solution.py:35
  95.6 0.7 collective-permute-start.23
  96.4 4.4 %collective-permute-done.23 = f32[144,128]{1,0:T(8,128)S(1)} collective-permute-done((f32[144,128]{1,0:T(8,128)S(1)}, f32[144,128]{1,0:T(8,128)S(1)}, u32[]{:S(2)}, u32[]{:S(2)}) %collective-permute-start.23) | collective-permute-done | bytes 73760 | tf_op jit(solution)/shard_map/ppermute | solution.py:30
  100.8 0.5 collective-permute-start.24
  101.3 1.4 %join.1.dep_ref = bf16[1152,256]{1,0:T(8,128)(2,1)} custom-call(s32[3]{0:T(128)S(1)} %pad_add_fusion.at_ref, bf16[576,256]{1,0:T(8,128)(2,1)S(1)} %get-tuple-element.48.own_ref, bf16[576,256]{1,0:T(8,128)(2,1)S(1)} %collective-permute-done.15.other_ref), custom_call_target="tpu_custom_call" | custom-call | flops 11500000 | tf_op jit(solution)/shard_map/join/pallas_call | solution.py:557
  102.7 4.0 %collective-permute-done.24.b_ref = f32[144,128]{1,0:T(8,128)S(1)} collective-permute-done((f32[144,128]{1,0:T(8,128)S(1)}, f32[144,128]{1,0:T(8,128)S(1)}, u32[]{:S(2)}, u32[]{:S(2)}) %collective-permute-start.24) | collective-permute-done | bytes 73760 | tf_op jit(solution)/shard_map/ppermute | solution.py:30
  106.7 6.1 %collective-permute-start.25 = (f32[144,128]{1,0:T(8,128)S(1)}, f32[144,128]{1,0:T(8,128)S(1)}, u32[]{:S(2)}, u32[]{:S(2)}) collective-permute-start(f32[144,128]{1,0:T(8,128)S(1)} %add.31.a_ref), channel_id=1, source_target_pairs={{0,32},{32,0},{1,33},{33,1},{2,34},{34,2},{3,35},{35,3},{4,36},{36... | collective-permute-start | bytes 221192 | tf_op jit(solution)/shard_map/ppermute | solution.py:30
  112.9 0.1 fold_last.1
  113.0 0.1 collective-permute-start.20
  113.1 2.4 %collective-permute-start.21 = (bf16[144,256]{1,0:T(8,128)(2,1)S(1)}, bf16[144,256]{1,0:T(8,128)(2,1)S(1)}, u32[]{:S(2)}, u32[]{:S(2)}) collective-permute-start(bf16[144,256]{1,0:T(8,128)(2,1)S(1)} %get-tuple-element.58), channel_id=1, source_target_pairs={{0,16},{8,24},{16,0},{24,8},{1,17},{9,25},{17,1},{25,9},{2,18},{10... | collective-permute-start | bytes 221192 | tf_op jit(solution)/shard_map/ppermute | solution.py:30
  115.5 1.9 %collective-permute-start.22 = (bf16[144,256]{1,0:T(8,128)(2,1)S(1)}, bf16[144,256]{1,0:T(8,128)(2,1)S(1)}, u32[]{:S(2)}, u32[]{:S(2)}) collective-permute-start(bf16[144,256]{1,0:T(8,128)(2,1)S(1)} %get-tuple-element.59), channel_id=1, source_target_pairs={{0,24},{8,16},{16,8},{24,0},{1,25},{9,17},{17,9},{25,1},{2,26},{10... | collective-permute-start | bytes 221192 | tf_op jit(solution)/shard_map/ppermute | solution.py:30
  117.5 0.1 collective-permute-start.26
  117.6 1.1 collective-permute-done.20
  118.7 3.0 %collective-permute-done.22 = bf16[144,256]{1,0:T(8,128)(2,1)S(1)} collective-permute-done((bf16[144,256]{1,0:T(8,128)(2,1)S(1)}, bf16[144,256]{1,0:T(8,128)(2,1)S(1)}, u32[]{:S(2)}, u32[]{:S(2)}) %collective-permute-start.22) | collective-permute-done | bytes 73760 | tf_op jit(solution)/shard_map/ppermute | solution.py:30
  121.7 0.0 copy-start.2
  121.8 0.2 collective-permute-done.26.other_ref
  121.9 2.3 %unpack.1 = f32[2,32,32,36]{3,2,1,0:T(8,128)} custom-call(s32[1]{0:T(128)} %bitcast.3.y0_ref, f32[144,128]{1,0:T(8,128)S(1)} %add.32.mine_ref, f32[144,128]{1,0:T(8,128)S(1)} %collective-permute-done.26.other_ref, bf16[144,256]{1,0:T(8,128)(2,1)S(1)} %add_convert_fusion.dep_ref), custom_call_target="tpu_custom_call" | custom-call | flops 11500000 | tf_op jit(solution)/shard_map/unpack/pallas_call | solution.py:574
  (56 shorter events, 0.2 us)
Async XLA Ops:
  0.6 19.1 %copy-start.4 = (f32[2,36,32,32]{1,3,2,0:T(8,128)S(1)}, f32[2,36,32,32]{1,3,2,0:T(8,128)}, u32[]{:S(2)}) copy-start(f32[2,36,32,32]{1,3,2,0:T(8,128)} %param.9) | copy-start | bytes 884740
  0.6 19.1 %copy-start.6 = (s32[2,32]{1,0:T(2,128)S(1)}, s32[2,32]{1,0:T(2,128)}, u32[]{:S(2)}) copy-start(s32[2,32]{1,0:T(2,128)} %perm_ref.3) | copy-start | bytes 772
  0.7 8.5 %collective-permute-start.2 = (bf16[144,256]{1,0:T(8,128)(2,1)}, bf16[144,256]{1,0:T(8,128)(2,1)S(1)}, u32[]{:S(2)}, u32[]{:S(2)}) collective-permute-start(bf16[144,256]{1,0:T(8,128)(2,1)} %bitcast.25), channel_id=1, source_target_pairs={{0,8},{8,0},{16,24},{24,16},{1,9},{9,1},{17,25},{25,17},{2,10},{10... | collective-permute-start | bytes 221192 | tf_op jit(solution)/shard_map/ppermute | solution.py:30
  2.7 8.6 %collective-permute-start.3 = (bf16[144,256]{1,0:T(8,128)(2,1)}, bf16[144,256]{1,0:T(8,128)(2,1)S(1)}, u32[]{:S(2)}, u32[]{:S(2)}) collective-permute-start(bf16[144,256]{1,0:T(8,128)(2,1)} %bitcast.26), channel_id=1, source_target_pairs={{0,16},{8,24},{16,0},{24,8},{1,17},{9,25},{17,1},{25,9},{2,18},{10... | collective-permute-start | bytes 221192 | tf_op jit(solution)/shard_map/ppermute | solution.py:30
  5.9 7.1 %collective-permute-start.4 = (bf16[144,256]{1,0:T(8,128)(2,1)}, bf16[144,256]{1,0:T(8,128)(2,1)S(1)}, u32[]{:S(2)}, u32[]{:S(2)}) collective-permute-start(bf16[144,256]{1,0:T(8,128)(2,1)} %bitcast.27), channel_id=1, source_target_pairs={{0,24},{8,16},{16,8},{24,0},{1,25},{9,17},{17,9},{25,1},{2,26},{10... | collective-permute-start | bytes 221192 | tf_op jit(solution)/shard_map/ppermute | solution.py:30
  6.9 20.2 %collective-permute-start = (bf16[576,256]{1,0:T(8,128)(2,1)S(1)}, bf16[576,256]{1,0:T(8,128)(2,1)S(1)}, u32[]{:S(2)}, u32[]{:S(2)}) collective-permute-start(bf16[576,256]{1,0:T(8,128)(2,1)S(1)} %bitcast.24), channel_id=1, source_target_pairs={{0,8},{8,0},{16,24},{24,16},{1,9},{9,1},{17,25},{25,17},{2,10},{10... | collective-permute-start | bytes 884744 | tf_op jit(solution)/shard_map/ppermute | solution.py:30
  7.6 19.6 %collective-permute-start.1 = (f32[16,1152]{1,0:T(8,128)}, f32[16,1152]{1,0:T(8,128)S(1)}, u32[]{:S(2)}, u32[]{:S(2)}) collective-permute-start(f32[16,1152]{1,0:T(8,128)} %mine_ref.3), channel_id=1, source_target_pairs={{0,8},{8,0},{16,24},{24,16},{1,9},{9,1},{17,25},{25,17},{2,10},{10... | collective-permute-start | bytes 221192 | tf_op jit(solution)/shard_map/ppermute | solution.py:30
  14.0 15.3 %collective-permute-start.5 = (bf16[4,144,256]{2,1,0:T(8,128)(2,1)S(1)}, bf16[4,144,256]{2,1,0:T(8,128)(2,1)S(1)}, u32[]{:S(2)}, u32[]{:S(2)}) collective-permute-start(bf16[4,144,256]{2,1,0:T(8,128)(2,1)S(1)} %pad_maximum_fusion.rest_0_.a_ref.own_ref), channel_id=1, source_target_pairs={{0,2},{2,4},{4,6},{6,0},{1,3},{3,5},{5,7},{7,1},{8,10},{10,12},{12... | collective-permute-start | bytes 884744 | tf_op jit(solution)/shard_map/ppermute | solution.py:35
  15.5 13.7 %collective-permute-start.6 = (bf16[4,144,256]{2,1,0:T(8,128)(2,1)S(1)}, bf16[4,144,256]{2,1,0:T(8,128)(2,1)S(1)}, u32[]{:S(2)}, u32[]{:S(2)}) collective-permute-start(bf16[4,144,256]{2,1,0:T(8,128)(2,1)S(1)} %pad_maximum_fusion.rest_0_.a_ref.own_ref), channel_id=1, source_target_pairs={{0,4},{2,6},{4,0},{6,2},{1,5},{3,7},{5,1},{7,3},{8,12},{10,14},{12... | collective-permute-start | bytes 884744 | tf_op jit(solution)/shard_map/ppermute | solution.py:35
  18.3 11.0 %collective-permute-start.7 = (bf16[4,144,256]{2,1,0:T(8,128)(2,1)S(1)}, bf16[4,144,256]{2,1,0:T(8,128)(2,1)S(1)}, u32[]{:S(2)}, u32[]{:S(2)}) collective-permute-start(bf16[4,144,256]{2,1,0:T(8,128)(2,1)S(1)} %pad_maximum_fusion.rest_0_.a_ref.own_ref), channel_id=1, source_target_pairs={{0,6},{2,0},{4,2},{6,4},{1,7},{3,1},{5,3},{7,5},{8,14},{10,8},{12,... | collective-permute-start | bytes 884744 | tf_op jit(solution)/shard_map/ppermute | solution.py:35
  19.7 7.5 %copy-start.3 = (bf16[1152,256]{1,0:T(8,128)(2,1)S(1)}, bf16[1152,256]{1,0:T(8,128)(2,1)}, u32[]{:S(2)}) copy-start(bf16[1152,256]{1,0:T(8,128)(2,1)} %grad_ref.3) | copy-start | bytes 1769476
  19.7 7.5 %copy-start.5 = (f32[16,1152]{1,0:T(8,128)S(1)}, f32[16,1152]{1,0:T(8,128)}, u32[]{:S(2)}) copy-start(f32[16,1152]{1,0:T(8,128)} %mine_ref.3) | copy-start | bytes 221188
  19.7 7.5 %copy-start.7 = (s32[256]{0:T(256)S(1)}, s32[256]{0:T(256)}, u32[]{:S(2)}) copy-start(s32[256]{0:T(256)} %param.11) | copy-start | bytes 3076
  19.7 14.0 %slice-start = ((s8[10616832]{0:T(1024)(128)(4,1)}), s8[4194304]{0:T(1024)(128)(4,1)S(1)}, s32[]{:S(2)}) async-start(s8[10616832]{0:T(1024)(128)(4,1)} %bitcast.17), calls=%async_computation | async-start | bytes 8388608
  19.8 14.0 %slice-start.1 = ((s8[10616832]{0:T(1024)(128)(4,1)}), s8[4194304]{0:T(1024)(128)(4,1)S(1)}, s32[]{:S(2)}) async-start(s8[10616832]{0:T(1024)(128)(4,1)} %bitcast.17), calls=%async_computation.1 | async-start | bytes 8388608
  27.2 6.5 %slice-start.2 = ((s8[10616832]{0:T(1024)(128)(4,1)}), s8[2228224]{0:T(1024)(128)(4,1)S(1)}, s32[]{:S(2)}) async-start(s8[10616832]{0:T(1024)(128)(4,1)} %bitcast.17), calls=%async_computation.2 | async-start | bytes 4456448
  29.4 4.3 %collective-permute-start.8 = (bf16[4,4,144,256]{3,2,1,0:T(8,128)(2,1)S(1)}, bf16[4,4,144,256]{3,2,1,0:T(8,128)(2,1)S(1)}, u32[]{:S(2)}, u32[]{:S(2)}) collective-permute-start(bf16[4,4,144,256]{3,2,1,0:T(8,128)(2,1)S(1)} %gather.1), channel_id=1, source_target_pairs={{0,1},{1,0},{2,3},{3,2},{4,5},{5,4},{6,7},{7,6},{8,9},{9,8},{10,11... | collective-permute-start | bytes 3538952 | tf_op jit(solution)/shard_map/ppermute | solution.py:30
  29.5 17.8 %collective-permute-start.10 = (bf16[576,256]{1,0:T(8,128)(2,1)S(1)}, bf16[576,256]{1,0:T(8,128)(2,1)S(1)}, u32[]{:S(2)}, u32[]{:S(2)}) collective-permute-start(bf16[576,256]{1,0:T(8,128)(2,1)S(1)} %get-tuple-element.34.dep_ref), channel_id=1, source_target_pairs={{0,0},{8,16},{16,8},{24,24},{1,1},{9,17},{17,9},{25,25},{2,2},{10,... | collective-permute-start | bytes 884744 | tf_op jit(solution)/shard_map/ppermute | solution.py:510
  30.2 24.2 %collective-permute-start.11 = (bf16[576,256]{1,0:T(8,128)(2,1)S(1)}, bf16[576,256]{1,0:T(8,128)(2,1)S(1)}, u32[]{:S(2)}, u32[]{:S(2)}) collective-permute-start(bf16[576,256]{1,0:T(8,128)(2,1)S(1)} %get-tuple-element.39), channel_id=1, source_target_pairs={{16,0},{0,8},{24,16},{8,24},{17,1},{1,9},{25,17},{9,25},{18,2},{2,... | collective-permute-start | bytes 884744 | tf_op jit(solution)/shard_map/ppermute | solution.py:511
  37.4 0.7 copy-start.10
  38.1 29.0 %collective-permute-start.9 = (bf16[576,256]{1,0:T(8,128)(2,1)S(1)}, bf16[576,256]{1,0:T(8,128)(2,1)S(1)}, u32[]{:S(2)}, u32[]{:S(2)}) collective-permute-start(bf16[576,256]{1,0:T(8,128)(2,1)S(1)} %get-tuple-element.35.dep_ref), channel_id=1, source_target_pairs={{0,16},{8,24},{16,0},{24,8},{1,17},{9,25},{17,1},{25,9},{2,18},{10... | collective-permute-start | bytes 884744 | tf_op jit(solution)/shard_map/ppermute | solution.py:30
  42.6 0.8 copy-start.8
  43.4 1.0 copy-start.13
  44.5 1.1 copy-start.15
  45.5 0.8 copy-start.17
  47.3 7.6 %copy-start = (bf16[1152,4608]{1,0:T(8,128)(2,1)}, bf16[1152,4608]{1,0:T(8,128)(2,1)S(1)}, u32[]{:S(2)}) copy-start(bf16[1152,4608]{1,0:T(8,128)(2,1)S(1)} %load.1.rest_0_.w_ref) | copy-start | bytes 31850500
  54.9 18.5 %collective-permute-start.14 = (bf16[576,256]{1,0:T(8,128)(2,1)S(1)}, bf16[576,256]{1,0:T(8,128)(2,1)S(1)}, u32[]{:S(2)}, u32[]{:S(2)}) collective-permute-start(bf16[576,256]{1,0:T(8,128)(2,1)S(1)} %get-tuple-element.41.rest_0_), channel_id=1, source_target_pairs={{0,16},{8,24},{16,0},{24,8},{1,17},{9,25},{17,1},{25,9},{2,18},{10... | collective-permute-start | bytes 884744 | tf_op jit(solution)/shard_map/ppermute | solution.py:30
  67.1 1.1 copy-start.9
  68.1 1.0 copy-start.11
  69.6 12.5 %collective-permute-start.12 = (bf16[576,256]{1,0:T(8,128)(2,1)S(1)}, bf16[576,256]{1,0:T(8,128)(2,1)S(1)}, u32[]{:S(2)}, u32[]{:S(2)}) collective-permute-start(bf16[576,256]{1,0:T(8,128)(2,1)S(1)} %get-tuple-element.42.dep_ref), channel_id=1, source_target_pairs={{0,0},{8,16},{16,8},{24,24},{1,1},{9,17},{17,9},{25,25},{2,2},{10,... | collective-permute-start | bytes 884744 | tf_op jit(solution)/shard_map/ppermute | solution.py:529
  70.2 11.8 %collective-permute-start.13 = (bf16[576,256]{1,0:T(8,128)(2,1)S(1)}, bf16[576,256]{1,0:T(8,128)(2,1)S(1)}, u32[]{:S(2)}, u32[]{:S(2)}) collective-permute-start(bf16[576,256]{1,0:T(8,128)(2,1)S(1)} %get-tuple-element.43), channel_id=1, source_target_pairs={{0,16},{8,0},{16,24},{24,8},{1,17},{9,1},{17,25},{25,9},{2,18},{10... | collective-permute-start | bytes 884744 | tf_op jit(solution)/shard_map/ppermute | solution.py:530
  73.4 4.0 %copy-start.1 = (bf16[1152,4608]{1,0:T(8,128)(2,1)S(1)}, bf16[1152,4608]{1,0:T(8,128)(2,1)}, u32[]{:S(2)}) copy-start(bf16[1152,4608]{1,0:T(8,128)(2,1)} %copy-done) | copy-start | bytes 31850500
  77.4 4.6 %copy-start.12 = (bf16[576,256]{1,0:T(8,128)(2,1)S(1)}, bf16[576,256]{1,0:T(8,128)(2,1)}, u32[]{:S(2)}) copy-start(bf16[576,256]{1,0:T(8,128)(2,1)} %copy-done.10) | copy-start | bytes 884740
  77.4 4.6 %copy-start.14 = (bf16[2,9,2,128,128]{4,3,2,1,0:T(8,128)(2,1)S(1)}, bf16[2,9,2,128,128]{4,3,2,1,0:T(8,128)(2,1)}, u32[]{:S(2)}) copy-start(bf16[2,9,2,128,128]{4,3,2,1,0:T(8,128)(2,1)} %copy-done.13) | copy-start | bytes 3538948
  77.4 4.6 %copy-start.16 = (bf16[2,9,2,128,128]{4,3,2,1,0:T(8,128)(2,1)S(1)}, bf16[2,9,2,128,128]{4,3,2,1,0:T(8,128)(2,1)}, u32[]{:S(2)}) copy-start(bf16[2,9,2,128,128]{4,3,2,1,0:T(8,128)(2,1)} %copy-done.15) | copy-start | bytes 3538948
  77.4 4.6 %copy-start.18 = (bf16[9,2,128,128]{3,2,1,0:T(8,128)(2,1)S(1)}, bf16[9,2,128,128]{3,2,1,0:T(8,128)(2,1)}, u32[]{:S(2)}) copy-start(bf16[9,2,128,128]{3,2,1,0:T(8,128)(2,1)} %copy-done.17) | copy-start | bytes 1769476
  81.9 7.2 %collective-permute-start.16 = (bf16[4,4,144,256]{3,2,1,0:T(8,128)(2,1)S(1)}, bf16[4,4,144,256]{3,2,1,0:T(8,128)(2,1)S(1)}, u32[]{:S(2)}, u32[]{:S(2)}) collective-permute-start(bf16[4,4,144,256]{3,2,1,0:T(8,128)(2,1)S(1)} %get-tuple-element.47.rest_9_), channel_id=1, source_target_pairs={{0,1},{1,0},{2,3},{3,2},{4,5},{5,4},{6,7},{7,6},{8,9},{9,8},{10,11... | collective-permute-start | bytes 3538952 | tf_op jit(solution)/shard_map/ppermute | solution.py:30
  84.9 16.4 %collective-permute-start.15 = (bf16[576,256]{1,0:T(8,128)(2,1)S(1)}, bf16[576,256]{1,0:T(8,128)(2,1)S(1)}, u32[]{:S(2)}, u32[]{:S(2)}) collective-permute-start(bf16[576,256]{1,0:T(8,128)(2,1)S(1)} %get-tuple-element.49), channel_id=1, source_target_pairs={{0,8},{8,0},{16,24},{24,16},{1,9},{9,1},{17,25},{25,17},{2,10},{10... | collective-permute-start | bytes 884744 | tf_op jit(solution)/shard_map/ppermute | solution.py:30
  89.4 23.4 %collective-permute-start.17 = (bf16[4,144,256]{2,1,0:T(8,128)(2,1)S(1)}, bf16[4,144,256]{2,1,0:T(8,128)(2,1)S(1)}, u32[]{:S(2)}, u32[]{:S(2)}) collective-permute-start(bf16[4,144,256]{2,1,0:T(8,128)(2,1)S(1)} %get-tuple-element.53), channel_id=1, source_target_pairs={{0,4},{2,6},{4,0},{6,2},{1,5},{3,7},{5,1},{7,3},{8,12},{10,14},{12... | collective-permute-start | bytes 884744 | tf_op jit(solution)/shard_map/ppermute | solution.py:35
  92.4 20.5 %collective-permute-start.18 = (bf16[4,144,256]{2,1,0:T(8,128)(2,1)S(1)}, bf16[4,144,256]{2,1,0:T(8,128)(2,1)S(1)}, u32[]{:S(2)}, u32[]{:S(2)}) collective-permute-start(bf16[4,144,256]{2,1,0:T(8,128)(2,1)S(1)} %get-tuple-element.54), channel_id=1, source_target_pairs={{0,2},{2,4},{4,6},{6,0},{1,3},{3,5},{5,7},{7,1},{8,10},{10,12},{12... | collective-permute-start | bytes 884744 | tf_op jit(solution)/shard_map/ppermute | solution.py:35
  92.8 20.0 %collective-permute-start.19 = (bf16[4,144,256]{2,1,0:T(8,128)(2,1)S(1)}, bf16[4,144,256]{2,1,0:T(8,128)(2,1)S(1)}, u32[]{:S(2)}, u32[]{:S(2)}) collective-permute-start(bf16[4,144,256]{2,1,0:T(8,128)(2,1)S(1)} %get-tuple-element.55), channel_id=1, source_target_pairs={{0,6},{2,0},{4,2},{6,4},{1,7},{3,1},{5,3},{7,5},{8,14},{10,8},{12,... | collective-permute-start | bytes 884744 | tf_op jit(solution)/shard_map/ppermute | solution.py:35
  95.6 5.1 %collective-permute-start.23 = (f32[144,128]{1,0:T(8,128)S(1)}, f32[144,128]{1,0:T(8,128)S(1)}, u32[]{:S(2)}, u32[]{:S(2)}) collective-permute-start(f32[144,128]{1,0:T(8,128)S(1)} %get-tuple-element.51.dep_ref), channel_id=1, source_target_pairs={{0,64},{64,0},{128,192},{192,128},{1,65},{65,1},{129,193},{193,129... | collective-permute-start | bytes 221192 | tf_op jit(solution)/shard_map/ppermute | solution.py:30
  100.8 5.9 %collective-permute-start.24 = (f32[144,128]{1,0:T(8,128)S(1)}, f32[144,128]{1,0:T(8,128)S(1)}, u32[]{:S(2)}, u32[]{:S(2)}) collective-permute-start(f32[144,128]{1,0:T(8,128)S(1)} %add.23.a_ref), channel_id=1, source_target_pairs={{0,128},{64,192},{128,0},{192,64},{1,129},{65,193},{129,1},{193,65... | collective-permute-start | bytes 221192 | tf_op jit(solution)/shard_map/ppermute | solution.py:30
  106.7 10.8 %collective-permute-start.25 = (f32[144,128]{1,0:T(8,128)S(1)}, f32[144,128]{1,0:T(8,128)S(1)}, u32[]{:S(2)}, u32[]{:S(2)}) collective-permute-start(f32[144,128]{1,0:T(8,128)S(1)} %add.31.a_ref), channel_id=1, source_target_pairs={{0,32},{32,0},{1,33},{33,1},{2,34},{34,2},{3,35},{35,3},{4,36},{36... | collective-permute-start | bytes 221192 | tf_op jit(solution)/shard_map/ppermute | solution.py:30
  113.0 5.6 %collective-permute-start.20 = (bf16[144,256]{1,0:T(8,128)(2,1)S(1)}, bf16[144,256]{1,0:T(8,128)(2,1)S(1)}, u32[]{:S(2)}, u32[]{:S(2)}) collective-permute-start(bf16[144,256]{1,0:T(8,128)(2,1)S(1)} %get-tuple-element.57), channel_id=1, source_target_pairs={{0,8},{8,0},{16,24},{24,16},{1,9},{9,1},{17,25},{25,17},{2,10},{10... | collective-permute-start | bytes 221192 | tf_op jit(solution)/shard_map/ppermute | solution.py:30
  113.1 5.5 %collective-permute-start.21 = (bf16[144,256]{1,0:T(8,128)(2,1)S(1)}, bf16[144,256]{1,0:T(8,128)(2,1)S(1)}, u32[]{:S(2)}, u32[]{:S(2)}) collective-permute-start(bf16[144,256]{1,0:T(8,128)(2,1)S(1)} %get-tuple-element.58), channel_id=1, source_target_pairs={{0,16},{8,24},{16,0},{24,8},{1,17},{9,25},{17,1},{25,9},{2,18},{10... | collective-permute-start | bytes 221192 | tf_op jit(solution)/shard_map/ppermute | solution.py:30
  115.5 6.2 %collective-permute-start.22 = (bf16[144,256]{1,0:T(8,128)(2,1)S(1)}, bf16[144,256]{1,0:T(8,128)(2,1)S(1)}, u32[]{:S(2)}, u32[]{:S(2)}) collective-permute-start(bf16[144,256]{1,0:T(8,128)(2,1)S(1)} %get-tuple-element.59), channel_id=1, source_target_pairs={{0,24},{8,16},{16,8},{24,0},{1,25},{9,17},{17,9},{25,1},{2,26},{10... | collective-permute-start | bytes 221192 | tf_op jit(solution)/shard_map/ppermute | solution.py:30
  117.5 4.4 %collective-permute-start.26 = (f32[144,128]{1,0:T(8,128)S(1)}, f32[144,128]{1,0:T(8,128)S(1)}, u32[]{:S(2)}, u32[]{:S(2)}) collective-permute-start(f32[144,128]{1,0:T(8,128)S(1)} %add.32.mine_ref), channel_id=1, source_target_pairs={{0,64},{64,0},{128,192},{192,128},{1,65},{65,1},{129,193},{193,129... | collective-permute-start | bytes 221192 | tf_op jit(solution)/shard_map/ppermute | solution.py:30
  121.7 2.5 %copy-start.2 = (bf16[144,256]{1,0:T(8,128)(2,1)}, bf16[144,256]{1,0:T(8,128)(2,1)S(1)}, u32[]{:S(2)}) copy-start(bf16[144,256]{1,0:T(8,128)(2,1)S(1)} %add_convert_fusion.dep_ref) | copy-start | bytes 221188

commit v4 on v3

--- a/solution.py
+++ b/solution.py
@@ -522,10 +522,10 @@
     z_own, z_send = hidden_halves(place, along_z, x1, x2, x3, by_core, weight)
     z_rec = xor(z_send, "z", 2)
     m0, mt0, m1, left, right = build(place, section_perm, turned, z_send)
-    held = load(weight, z_send)
-    h_own, h_send = turn(ga, gb, mt0, (held,))
+    h_own, h_send = turn(ga, gb, mt0, (z_send,))
+    held = load(pltpu.with_memory_space_constraint(weight, pltpu.HBM), h_send)
     h_rec = xor(h_send, "z", 2)
-    za_out, zb = turn(z_own, z_rec, m0, (h_send,))
+    za_out, zb = turn(z_own, z_rec, m0, (held,))
     za = lax.ppermute(za_out, "z", A_PAIRS)
     zb = lax.ppermute(zb, "z", B_PAIRS)
     keep, send = input_parts(place, h_own, h_rec, held, za_out)
@@ -563,7 +563,7 @@
         cost_estimate=cost(0.01),
         name="join",
     )(place, j_own, j_rec)
-    own, to1, to2, to3 = fold(keep, send_rec, half_send)
+    own, to1, to2, to3 = fold(keep, send_rec, za_out)
     half = half + xor(half_send, "y", 1)
     ours, z1, z2, z3 = fold_last(own, shift(to2, "x", 2), shift(to1, "x", 1), shift(to3, "x", 3))
     half = add(half, xor(half, "y", 2), pltpu.with_memory_space_constraint(judged, pltpu.HBM))

time: 125 us -> 124 us (level)
  Pallas kernels: 30.4 us -> 33.6 us
  waiting for transfers between devices: 37.1 us -> 34.9 us
  local copies, waits for them, and re-layouts: 11.5 us -> 9.89 us
    ppermute x1, waiting for transfers between devices: 7.16 us -> 0.01 us  [per_device(): gb = lax.ppermute(gb_out, 'z', B_BACK)]
    ppermute x17, starting transfers between devices: 24.3 us -> 28.4 us  [xor(): lax.ppermute(x, axis, [(i, i ^ k) for i in range(lax.axis_size(axis))])]
    pallas_call x1, Pallas kernels: 0.89 us -> 4.02 us  [load(): pl.pallas_call(load_kernel, out_shape=jax.ShapeDtypeStruct(weight.shape,...]
    ppermute x6, starting transfers between devices: 11.9 us -> 8.87 us  [shift(): return lax.ppermute(x, axis, [(i, (i + k) % n) for i in range(n)])]
    ppermute x17, waiting for transfers between devices: 29.9 us -> 32.9 us  [xor(): lax.ppermute(x, axis, [(i, i ^ k) for i in range(lax.axis_size(axis))])]
    ppermute x6, waiting for transfers between devices: 0.02 us -> 1.91 us  [shift(): return lax.ppermute(x, axis, [(i, (i + k) % n) for i in range(n)])]
    ppermute x1, starting transfers between devices: 1.92 us -> 0.08 us  [per_device(): zb = lax.ppermute(zb, 'z', B_PAIRS)]
    unnamed x44 -> x40, local copies, waits for them, and re-layouts: 10.6 us -> 8.91 us
  transfers between devices with their start and end apart: 27 -> 27, of which waited for: 10 -> 9; matrix products, arithmetic and copies ran while one was open for 2% -> 2% of each run, Pallas kernels for 23% -> 25%
where the time goes in v4:
time: 124 us
  starting transfers between devices  43.4 us (35%)
  waiting for transfers between devices  34.9 us (28%)
  Pallas kernels  33.6 us (27%)
  local copies, waits for them, and re-layouts  9.89 us (8%)
    ppermute x17, waiting for transfers between devices, xor(): lax.ppermute(x, axis, [(i, i ^ k) for i in range(lax.axis_size(axis))])  32.9 us
    ppermute x17, starting transfers between devices, xor(): lax.ppermute(x, axis, [(i, i ^ k) for i in range(lax.axis_size(axis))])  28.4 us
    unnamed x40, local copies, waits for them, and re-layouts  8.91 us
    ppermute x6, starting transfers between devices, shift(): return lax.ppermute(x, axis, [(i, (i + k) % n) for i in range(n)])  8.87 us
    pallas_call x1, Pallas kernels, invert(): pl.pallas_call(invert_kernel, out_shape=(jax.ShapeDtypeStruct((n * 128, n...  7.38 us
    pallas_call x1, Pallas kernels, input_parts(): pl.pallas_call(input_kernel, out_shape=(jax.ShapeDtypeStruct(dims, F32),...  4.49 us
    pallas_call x1, Pallas kernels, build(): pl.pallas_call(build_kernel, out_shape=(one, one, one, two, two), in_spec...  4.1 us
    pallas_call x1, Pallas kernels, load(): pl.pallas_call(load_kernel, out_shape=jax.ShapeDtypeStruct(weight.shape,...  4.02 us
  transfers between devices with their start and end apart: 27, of which 9 were waited for; matrix products, arithmetic and copies ran while one was open for 2% of the time, Pallas kernels for 25%

profile of v4, /device:TPU:24, one launch (start us, length us, event | category | flops | bytes accessed | tf_op | source)
XLA Modules:
  0.0 123.7 jit_solution(15267792875635016947)
XLA Ops:
  0.7 3.4 %collective-permute-start.3 = (bf16[144,256]{1,0:T(8,128)(2,1)}, bf16[144,256]{1,0:T(8,128)(2,1)S(1)}, u32[]{:S(2)}, u32[]{:S(2)}) collective-permute-start(bf16[144,256]{1,0:T(8,128)(2,1)} %bitcast.23), channel_id=1, source_target_pairs={{0,16},{8,24},{16,0},{24,8},{1,17},{9,25},{17,1},{25,9},{2,18},{10... | collective-permute-start | bytes 221192 | tf_op jit(solution)/shard_map/ppermute | solution.py:30
  4.0 1.9 %collective-permute-start.2 = (bf16[144,256]{1,0:T(8,128)(2,1)}, bf16[144,256]{1,0:T(8,128)(2,1)S(1)}, u32[]{:S(2)}, u32[]{:S(2)}) collective-permute-start(bf16[144,256]{1,0:T(8,128)(2,1)} %bitcast.24), channel_id=1, source_target_pairs={{0,8},{8,0},{16,24},{24,16},{1,9},{9,1},{17,25},{25,17},{2,10},{10... | collective-permute-start | bytes 221192 | tf_op jit(solution)/shard_map/ppermute | solution.py:30
  5.9 0.7 collective-permute-start.1
  6.6 1.0 constant_dynamic-slice_fusion
  7.6 1.4 %collective-permute-start = (bf16[576,256]{1,0:T(8,128)(2,1)S(1)}, bf16[576,256]{1,0:T(8,128)(2,1)S(1)}, u32[]{:S(2)}, u32[]{:S(2)}) collective-permute-start(bf16[576,256]{1,0:T(8,128)(2,1)S(1)} %bitcast.22), channel_id=1, source_target_pairs={{0,8},{8,0},{16,24},{24,16},{1,9},{9,1},{17,25},{25,17},{2,10},{10... | collective-permute-start | bytes 884744 | tf_op jit(solution)/shard_map/ppermute | solution.py:30
  9.0 0.1 pad_add_fusion.at_ref
  9.1 0.0 collective-permute-done.3
  9.1 0.0 collective-permute-done.2
  9.1 3.4 %collective-permute-done.4 = bf16[144,256]{1,0:T(8,128)(2,1)S(1)} collective-permute-done((bf16[144,256]{1,0:T(8,128)(2,1)}, bf16[144,256]{1,0:T(8,128)(2,1)S(1)}, u32[]{:S(2)}, u32[]{:S(2)}) %collective-permute-start.4) | collective-permute-done | bytes 73760 | tf_op jit(solution)/shard_map/ppermute | solution.py:30
  12.5 0.9 pad_maximum_fusion.rest_0_.a_ref.own_ref
  13.4 2.8 %collective-permute-start.7 = (bf16[4,144,256]{2,1,0:T(8,128)(2,1)S(1)}, bf16[4,144,256]{2,1,0:T(8,128)(2,1)S(1)}, u32[]{:S(2)}, u32[]{:S(2)}) collective-permute-start(bf16[4,144,256]{2,1,0:T(8,128)(2,1)S(1)} %pad_maximum_fusion.rest_0_.a_ref.own_ref), channel_id=1, source_target_pairs={{0,6},{2,0},{4,2},{6,4},{1,7},{3,1},{5,3},{7,5},{8,14},{10,8},{12,... | collective-permute-start | bytes 884744 | tf_op jit(solution)/shard_map/ppermute | solution.py:35
  16.3 0.8 collective-permute-start.6
  17.1 0.9 collective-permute-start.5
  18.0 0.0 copy-start.17
  18.0 7.4 %invert.1 = (f32[4096,32]{1,0:T(8,128)S(1)}, bf16[9,2,128,128]{3,2,1,0:T(8,128)(2,1)S(1)}) custom-call(s32[3]{0:T(128)S(1)} %pad_add_fusion.at_ref, s32[2,32]{1,0:T(2,128)S(1)} %copy-done.16, f32[2,32,32,36]{3,2,1,0:T(8,128)S(1)} %bitcast.18, bf16[4,144,256]{2,1,0:T(8,128)(2,1)S(1)} %pad_maximum_fusion.rest_0_.a_ref.own_ref), custom_call_target="tpu_custom_call" | custom-call | flops 8049999872 | tf_op jit(solution)/shard_map/invert/pallas_call | solution.py:139
  25.4 1.3 %copy-done.18 = f32[4096,32]{1,0:T(8,128)} copy-done((f32[4096,32]{1,0:T(8,128)}, f32[4096,32]{1,0:T(8,128)S(1)}, u32[]{:S(2)}) %copy-start.18) | copy-done | bytes 524312
  26.8 2.1 %cotangent.1 = (bf16[576,256]{1,0:T(8,128)(2,1)S(1)}, bf16[576,256]{1,0:T(8,128)(2,1)S(1)}) custom-call(s32[3]{0:T(128)S(1)} %pad_add_fusion.at_ref, bf16[1152,256]{1,0:T(8,128)(2,1)S(1)} %copy-done.2, bf16[576,256]{1,0:T(8,128)(2,1)S(1)} %collective-permute-done.rec_ref, f32[16,1152]{1,0:T(8,128)S(1)} %copy-done.12, ...), custom_call_target="tpu_custom_call" | custom-call | flops 3449999872 | tf_op jit(solution)/shard_map/cotangent/pallas_call | solution.py:245
  28.8 0.0 collective-permute-done.7.d_ref.r3
  28.9 0.0 collective-permute-done.6.c_ref.r2
  28.9 0.0 copy-start.7
  28.9 1.9 %collective-permute-done.5.b_ref.r1 = bf16[4,144,256]{2,1,0:T(8,128)(2,1)S(1)} collective-permute-done((bf16[4,144,256]{2,1,0:T(8,128)(2,1)S(1)}, bf16[4,144,256]{2,1,0:T(8,128)(2,1)S(1)}, u32[]{:S(2)}, u32[]{:S(2)}) %collective-permute-start.5) | collective-permute-done | bytes 294944 | tf_op jit(solution)/shard_map/ppermute | solution.py:35
  30.8 0.1 gather.1
  30.9 0.6 copy-done.10
  31.5 1.6 %collective-permute-start.10 = (bf16[576,256]{1,0:T(8,128)(2,1)}, bf16[576,256]{1,0:T(8,128)(2,1)S(1)}, u32[]{:S(2)}, u32[]{:S(2)}) collective-permute-start(bf16[576,256]{1,0:T(8,128)(2,1)} %copy-done.6), channel_id=1, source_target_pairs={{0,0},{8,16},{16,8},{24,24},{1,1},{9,17},{17,9},{25,25},{2,2},{10,... | collective-permute-start | bytes 884744 | tf_op jit(solution)/shard_map/ppermute | solution.py:510
  33.1 3.7 %collective-permute-start.11 = (bf16[576,256]{1,0:T(8,128)(2,1)}, bf16[576,256]{1,0:T(8,128)(2,1)S(1)}, u32[]{:S(2)}, u32[]{:S(2)}) collective-permute-start(bf16[576,256]{1,0:T(8,128)(2,1)} %copy-done.9), channel_id=1, source_target_pairs={{16,0},{0,8},{24,16},{8,24},{17,1},{1,9},{25,17},{9,25},{18,2},{2,... | collective-permute-start | bytes 884744 | tf_op jit(solution)/shard_map/ppermute | solution.py:511
  36.8 4.0 %copy-done = bf16[1152,4608]{1,0:T(8,128)(2,1)S(1)} copy-done((bf16[1152,4608]{1,0:T(8,128)(2,1)S(1)}, bf16[1152,4608]{1,0:T(8,128)(2,1)}, u32[]{:S(2)}) %copy-start) | copy-done | bytes 10616856
  40.9 1.0 copy-done.5
  41.8 1.0 copy-done.8
  42.8 1.0 copy-done.11
  43.7 3.6 %hidden.1 = (bf16[576,256]{1,0:T(8,128)(2,1)S(1)}, bf16[576,256]{1,0:T(8,128)(2,1)S(1)}) custom-call(s32[3]{0:T(128)S(1)} %pad_add_fusion.at_ref, bf16[4,144,256]{2,1,0:T(8,128)(2,1)S(1)} %pad_maximum_fusion.rest_0_.a_ref.own_ref, bf16[4,144,256]{2,1,0:T(8,128)(2,1)S(1)} %copy-done.11, bf16[4,144,256]{2,1,0:T(8,128)(2,1)S(1)} %copy-done.8, ...), custom_call_target="tpu_custom_call" | custom-call | flops 6899999744 | tf_op jit(solution)/shard_map/hidden/pallas_call | solution.py:349
  47.4 0.5 collective-permute-start.9
  47.9 4.1 %build.1 = (bf16[9,2,128,128]{3,2,1,0:T(8,128)(2,1)S(1)}, bf16[9,2,128,128]{3,2,1,0:T(8,128)(2,1)S(1)}, bf16[9,2,128,128]{3,2,1,0:T(8,128)(2,1)S(1)}, bf16[2,9,2...) custom-call(s32[3]{0:T(128)S(1)} %pad_add_fusion.at_ref, s32[2,32]{1,0:T(2,128)S(1)} %copy-done.16, ...), custom_call_target="tpu_custom_call" | custom-call | flops 5750000128 | tf_op jit(solution)/shard_map/build/pallas_call | solution.py:160
  52.0 0.5 turn.2
  52.5 2.7 %collective-permute-start.14 = (bf16[576,256]{1,0:T(8,128)(2,1)S(1)}, bf16[576,256]{1,0:T(8,128)(2,1)S(1)}, u32[]{:S(2)}, u32[]{:S(2)}) collective-permute-start(bf16[576,256]{1,0:T(8,128)(2,1)S(1)} %get-tuple-element.41.dep_ref), channel_id=1, source_target_pairs={{0,16},{8,24},{16,0},{24,8},{1,17},{9,25},{17,1},{25,9},{2,18},{10... | collective-permute-start | bytes 884744 | tf_op jit(solution)/shard_map/ppermute | solution.py:30
  55.2 4.0 %load.1.rest_0_.w_ref = bf16[1152,4608]{1,0:T(8,128)(2,1)S(1)} custom-call(bf16[1152,4608]{1,0:T(8,128)(2,1)} %w_hbm.1, bf16[576,256]{1,0:T(8,128)(2,1)S(1)} %get-tuple-element.41.dep_ref), custom_call_target="tpu_custom_call" | custom-call | flops 4600000000 | tf_op jit(solution)/shard_map/load/pallas_call | solution.py:449
  59.3 7.4 %collective-permute-done.9.b_ref.rest_6_ = bf16[576,256]{1,0:T(8,128)(2,1)S(1)} collective-permute-done((bf16[576,256]{1,0:T(8,128)(2,1)S(1)}, bf16[576,256]{1,0:T(8,128)(2,1)S(1)}, u32[]{:S(2)}, u32[]{:S(2)}) %collective-permute-start.9) | collective-permute-done | bytes 294944 | tf_op jit(solution)/shard_map/ppermute | solution.py:30
  66.7 0.5 turn.3
  67.1 0.1 collective-permute-start.13
  67.2 0.7 collective-permute-start.12
  67.9 11.5 %collective-permute-done.14.other_ref = bf16[576,256]{1,0:T(8,128)(2,1)S(1)} collective-permute-done((bf16[576,256]{1,0:T(8,128)(2,1)S(1)}, bf16[576,256]{1,0:T(8,128)(2,1)S(1)}, u32[]{:S(2)}, u32[]{:S(2)}) %collective-permute-start.14) | collective-permute-done | bytes 294944 | tf_op jit(solution)/shard_map/ppermute | solution.py:30
  79.4 4.5 %input_sums.1 = (f32[4,4,144,256]{3,2,1,0:T(8,128)S(1)}, bf16[4,4,144,256]{3,2,1,0:T(8,128)(2,1)S(1)}) custom-call(s32[3]{0:T(128)S(1)} %pad_add_fusion.at_ref, bf16[576,256]{1,0:T(8,128)(2,1)S(1)} %get-tuple-element.46.own_ref, bf16[576,256]{1,0:T(8,128)(2,1)S(1)} %collective-permute-done.14.other_ref, bf16[1152,4608]{1,0:T(8,128)(2,1)S(1)} %load.1.rest_0_.w_ref, ...), custom_call_target="tpu_custom_call" | custom-call | flops 6899999744 | tf_op jit(solution)/shard_map/input_sums/pallas_call | solution.py:386
  83.9 0.1 collective-permute-start.16
  84.0 2.8 %last.1 = (bf16[576,256]{1,0:T(8,128)(2,1)S(1)}, bf16[576,256]{1,0:T(8,128)(2,1)S(1)}, f32[144,128]{1,0:T(8,128)S(1)}, f32[144,128]{1,0:T(8,128)S(1)}) custom-call(s32[3]{0:T(128)S(1)} %pad_add_fusion.at_ref, s32[1]{0:T(128)} %bitcast.3.y0_ref, bf16[1152,256]{1,0:T(8,128)(2,1)S(1)} %copy-done.2, bf16[576,256]{1,0:T(8,128)(2,1)S(1)} %collective-permute-done.rec_ref, ...), custom_call_target="tpu_custom_call" | custom-call | flops 34500001792 | tf_op jit(solution)/shard_map/last/pallas_call | solution.py:538
  86.8 5.4 %collective-permute-start.15 = (bf16[576,256]{1,0:T(8,128)(2,1)S(1)}, bf16[576,256]{1,0:T(8,128)(2,1)S(1)}, u32[]{:S(2)}, u32[]{:S(2)}) collective-permute-start(bf16[576,256]{1,0:T(8,128)(2,1)S(1)} %get-tuple-element.49), channel_id=1, source_target_pairs={{0,8},{8,0},{16,24},{24,16},{1,9},{9,1},{17,25},{25,17},{2,10},{10... | collective-permute-start | bytes 884744 | tf_op jit(solution)/shard_map/ppermute | solution.py:30
  92.2 0.2 fold.1
  92.4 1.1 collective-permute-start.17
  93.6 0.7 collective-permute-start.18
  94.2 2.6 %collective-permute-start.19 = (bf16[4,144,256]{2,1,0:T(8,128)(2,1)S(1)}, bf16[4,144,256]{2,1,0:T(8,128)(2,1)S(1)}, u32[]{:S(2)}, u32[]{:S(2)}) collective-permute-start(bf16[4,144,256]{2,1,0:T(8,128)(2,1)S(1)} %get-tuple-element.54), channel_id=1, source_target_pairs={{0,6},{2,0},{4,2},{6,4},{1,7},{3,1},{5,3},{7,5},{8,14},{10,8},{12,... | collective-permute-start | bytes 884744 | tf_op jit(solution)/shard_map/ppermute | solution.py:35
  96.8 0.7 collective-permute-start.23
  97.5 3.6 %collective-permute-done.23 = f32[144,128]{1,0:T(8,128)S(1)} collective-permute-done((f32[144,128]{1,0:T(8,128)S(1)}, f32[144,128]{1,0:T(8,128)S(1)}, u32[]{:S(2)}, u32[]{:S(2)}) %collective-permute-start.23) | collective-permute-done | bytes 73760 | tf_op jit(solution)/shard_map/ppermute | solution.py:30
  101.2 1.3 %collective-permute-start.24 = (f32[144,128]{1,0:T(8,128)S(1)}, f32[144,128]{1,0:T(8,128)S(1)}, u32[]{:S(2)}, u32[]{:S(2)}) collective-permute-start(f32[144,128]{1,0:T(8,128)S(1)} %add.23.a_ref), channel_id=1, source_target_pairs={{0,128},{64,192},{128,0},{192,64},{1,129},{65,193},{129,1},{193,65... | collective-permute-start | bytes 221192 | tf_op jit(solution)/shard_map/ppermute | solution.py:30
  102.5 1.4 %join.1.dep_ref = bf16[1152,256]{1,0:T(8,128)(2,1)} custom-call(s32[3]{0:T(128)S(1)} %pad_add_fusion.at_ref, bf16[576,256]{1,0:T(8,128)(2,1)S(1)} %get-tuple-element.48.own_ref, bf16[576,256]{1,0:T(8,128)(2,1)S(1)} %collective-permute-done.15.other_ref), custom_call_target="tpu_custom_call" | custom-call | flops 11500000 | tf_op jit(solution)/shard_map/join/pallas_call | solution.py:557
  103.9 3.2 %collective-permute-done.24.b_ref = f32[144,128]{1,0:T(8,128)S(1)} collective-permute-done((f32[144,128]{1,0:T(8,128)S(1)}, f32[144,128]{1,0:T(8,128)S(1)}, u32[]{:S(2)}, u32[]{:S(2)}) %collective-permute-start.24) | collective-permute-done | bytes 73760 | tf_op jit(solution)/shard_map/ppermute | solution.py:30
  107.1 5.2 %collective-permute-start.25 = (f32[144,128]{1,0:T(8,128)S(1)}, f32[144,128]{1,0:T(8,128)S(1)}, u32[]{:S(2)}, u32[]{:S(2)}) collective-permute-start(f32[144,128]{1,0:T(8,128)S(1)} %add.31.a_ref), channel_id=1, source_target_pairs={{0,32},{32,0},{1,33},{33,1},{2,34},{34,2},{3,35},{35,3},{4,36},{36... | collective-permute-start | bytes 221192 | tf_op jit(solution)/shard_map/ppermute | solution.py:30
  112.3 0.1 fold_last.1
  112.5 0.1 collective-permute-start.20
  112.6 2.6 %collective-permute-start.21 = (bf16[144,256]{1,0:T(8,128)(2,1)S(1)}, bf16[144,256]{1,0:T(8,128)(2,1)S(1)}, u32[]{:S(2)}, u32[]{:S(2)}) collective-permute-start(bf16[144,256]{1,0:T(8,128)(2,1)S(1)} %get-tuple-element.57), channel_id=1, source_target_pairs={{0,16},{8,24},{16,0},{24,8},{1,17},{9,25},{17,1},{25,9},{2,18},{10... | collective-permute-start | bytes 221192 | tf_op jit(solution)/shard_map/ppermute | solution.py:30
  115.2 1.7 %collective-permute-start.22 = (bf16[144,256]{1,0:T(8,128)(2,1)S(1)}, bf16[144,256]{1,0:T(8,128)(2,1)S(1)}, u32[]{:S(2)}, u32[]{:S(2)}) collective-permute-start(bf16[144,256]{1,0:T(8,128)(2,1)S(1)} %get-tuple-element.58), channel_id=1, source_target_pairs={{0,24},{8,16},{16,8},{24,0},{1,25},{9,17},{17,9},{25,1},{2,26},{10... | collective-permute-start | bytes 221192 | tf_op jit(solution)/shard_map/ppermute | solution.py:30
  117.0 0.6 collective-permute-start.26
  117.5 1.2 collective-permute-done.20
  118.7 0.7 collective-permute-done.21
  119.4 2.0 %collective-permute-done.22 = bf16[144,256]{1,0:T(8,128)(2,1)S(1)} collective-permute-done((bf16[144,256]{1,0:T(8,128)(2,1)S(1)}, bf16[144,256]{1,0:T(8,128)(2,1)S(1)}, u32[]{:S(2)}, u32[]{:S(2)}) %collective-permute-start.22) | collective-permute-done | bytes 73760 | tf_op jit(solution)/shard_map/ppermute | solution.py:30
  121.4 0.0 copy-start.1
  121.4 2.3 %unpack.1 = f32[2,32,32,36]{3,2,1,0:T(8,128)} custom-call(s32[1]{0:T(128)} %bitcast.3.y0_ref, f32[144,128]{1,0:T(8,128)S(1)} %add.32.mine_ref, f32[144,128]{1,0:T(8,128)S(1)} %collective-permute-done.26.other_ref, bf16[144,256]{1,0:T(8,128)(2,1)S(1)} %add_convert_fusion.dep_ref), custom_call_target="tpu_custom_call" | custom-call | flops 11500000 | tf_op jit(solution)/shard_map/unpack/pallas_call | solution.py:574
  (51 shorter events, 0.2 us)
Async XLA Ops:
  0.6 17.3 %copy-start.16 = (s32[2,32]{1,0:T(2,128)S(1)}, s32[2,32]{1,0:T(2,128)}, u32[]{:S(2)}) copy-start(s32[2,32]{1,0:T(2,128)} %perm_ref.3) | copy-start | bytes 772
  0.6 17.3 %copy-start.3 = (f32[2,36,32,32]{1,3,2,0:T(8,128)S(1)}, f32[2,36,32,32]{1,3,2,0:T(8,128)}, u32[]{:S(2)}) copy-start(f32[2,36,32,32]{1,3,2,0:T(8,128)} %param.9) | copy-start | bytes 884740
  0.7 8.5 %collective-permute-start.3 = (bf16[144,256]{1,0:T(8,128)(2,1)}, bf16[144,256]{1,0:T(8,128)(2,1)S(1)}, u32[]{:S(2)}, u32[]{:S(2)}) collective-permute-start(bf16[144,256]{1,0:T(8,128)(2,1)} %bitcast.23), channel_id=1, source_target_pairs={{0,16},{8,24},{16,0},{24,8},{1,17},{9,25},{17,1},{25,9},{2,18},{10... | collective-permute-start | bytes 221192 | tf_op jit(solution)/shard_map/ppermute | solution.py:30
  4.0 5.1 %collective-permute-start.2 = (bf16[144,256]{1,0:T(8,128)(2,1)}, bf16[144,256]{1,0:T(8,128)(2,1)S(1)}, u32[]{:S(2)}, u32[]{:S(2)}) collective-permute-start(bf16[144,256]{1,0:T(8,128)(2,1)} %bitcast.24), channel_id=1, source_target_pairs={{0,8},{8,0},{16,24},{24,16},{1,9},{9,1},{17,25},{25,17},{2,10},{10... | collective-permute-start | bytes 221192 | tf_op jit(solution)/shard_map/ppermute | solution.py:30
  5.9 6.6 %collective-permute-start.4 = (bf16[144,256]{1,0:T(8,128)(2,1)}, bf16[144,256]{1,0:T(8,128)(2,1)S(1)}, u32[]{:S(2)}, u32[]{:S(2)}) collective-permute-start(bf16[144,256]{1,0:T(8,128)(2,1)} %bitcast.25), channel_id=1, source_target_pairs={{0,24},{8,16},{16,8},{24,0},{1,25},{9,17},{17,9},{25,1},{2,26},{10... | collective-permute-start | bytes 221192 | tf_op jit(solution)/shard_map/ppermute | solution.py:30
  5.9 20.8 %collective-permute-start.1 = (f32[16,1152]{1,0:T(8,128)}, f32[16,1152]{1,0:T(8,128)S(1)}, u32[]{:S(2)}, u32[]{:S(2)}) collective-permute-start(f32[16,1152]{1,0:T(8,128)} %mine_ref.3), channel_id=1, source_target_pairs={{0,8},{8,0},{16,24},{24,16},{1,9},{9,1},{17,25},{25,17},{2,10},{10... | collective-permute-start | bytes 221192 | tf_op jit(solution)/shard_map/ppermute | solution.py:30
  7.6 19.1 %collective-permute-start = (bf16[576,256]{1,0:T(8,128)(2,1)S(1)}, bf16[576,256]{1,0:T(8,128)(2,1)S(1)}, u32[]{:S(2)}, u32[]{:S(2)}) collective-permute-start(bf16[576,256]{1,0:T(8,128)(2,1)S(1)} %bitcast.22), channel_id=1, source_target_pairs={{0,8},{8,0},{16,24},{24,16},{1,9},{9,1},{17,25},{25,17},{2,10},{10... | collective-permute-start | bytes 884744 | tf_op jit(solution)/shard_map/ppermute | solution.py:30
  13.4 15.4 %collective-permute-start.7 = (bf16[4,144,256]{2,1,0:T(8,128)(2,1)S(1)}, bf16[4,144,256]{2,1,0:T(8,128)(2,1)S(1)}, u32[]{:S(2)}, u32[]{:S(2)}) collective-permute-start(bf16[4,144,256]{2,1,0:T(8,128)(2,1)S(1)} %pad_maximum_fusion.rest_0_.a_ref.own_ref), channel_id=1, source_target_pairs={{0,6},{2,0},{4,2},{6,4},{1,7},{3,1},{5,3},{7,5},{8,14},{10,8},{12,... | collective-permute-start | bytes 884744 | tf_op jit(solution)/shard_map/ppermute | solution.py:35
  16.3 12.6 %collective-permute-start.6 = (bf16[4,144,256]{2,1,0:T(8,128)(2,1)S(1)}, bf16[4,144,256]{2,1,0:T(8,128)(2,1)S(1)}, u32[]{:S(2)}, u32[]{:S(2)}) collective-permute-start(bf16[4,144,256]{2,1,0:T(8,128)(2,1)S(1)} %pad_maximum_fusion.rest_0_.a_ref.own_ref), channel_id=1, source_target_pairs={{0,4},{2,6},{4,0},{6,2},{1,5},{3,7},{5,1},{7,3},{8,12},{10,14},{12... | collective-permute-start | bytes 884744 | tf_op jit(solution)/shard_map/ppermute | solution.py:35
  17.1 13.7 %collective-permute-start.5 = (bf16[4,144,256]{2,1,0:T(8,128)(2,1)S(1)}, bf16[4,144,256]{2,1,0:T(8,128)(2,1)S(1)}, u32[]{:S(2)}, u32[]{:S(2)}) collective-permute-start(bf16[4,144,256]{2,1,0:T(8,128)(2,1)S(1)} %pad_maximum_fusion.rest_0_.a_ref.own_ref), channel_id=1, source_target_pairs={{0,2},{2,4},{4,6},{6,0},{1,3},{3,5},{5,7},{7,1},{8,10},{10,12},{12... | collective-permute-start | bytes 884744 | tf_op jit(solution)/shard_map/ppermute | solution.py:35
  18.0 8.8 %copy-start.2 = (bf16[1152,256]{1,0:T(8,128)(2,1)S(1)}, bf16[1152,256]{1,0:T(8,128)(2,1)}, u32[]{:S(2)}) copy-start(bf16[1152,256]{1,0:T(8,128)(2,1)} %grad_ref.3) | copy-start | bytes 1769476
  18.0 8.8 %copy-start.12 = (f32[16,1152]{1,0:T(8,128)S(1)}, f32[16,1152]{1,0:T(8,128)}, u32[]{:S(2)}) copy-start(f32[16,1152]{1,0:T(8,128)} %mine_ref.3) | copy-start | bytes 221188
  18.0 8.8 %copy-start.17 = (s32[256]{0:T(256)S(1)}, s32[256]{0:T(256)}, u32[]{:S(2)}) copy-start(s32[256]{0:T(256)} %param.11) | copy-start | bytes 3076
  25.4 1.4 %copy-start.18 = (f32[4096,32]{1,0:T(8,128)}, f32[4096,32]{1,0:T(8,128)S(1)}, u32[]{:S(2)}) copy-start(f32[4096,32]{1,0:T(8,128)S(1)} %get-tuple-element.32.turned) | copy-start | bytes 1572868
  26.7 2.1 %copy-start.14 = (f32[16,1152]{1,0:T(8,128)}, f32[16,1152]{1,0:T(8,128)S(1)}, u32[]{:S(2)}) copy-start(f32[16,1152]{1,0:T(8,128)S(1)} %collective-permute-done.1.theirs_ref) | copy-start | bytes 221188
  28.8 2.0 %copy-start.6 = (bf16[576,256]{1,0:T(8,128)(2,1)}, bf16[576,256]{1,0:T(8,128)(2,1)S(1)}, u32[]{:S(2)}) copy-start(bf16[576,256]{1,0:T(8,128)(2,1)S(1)} %get-tuple-element.34.dep_ref) | copy-start | bytes 884740
  28.8 2.0 %copy-start.9 = (bf16[576,256]{1,0:T(8,128)(2,1)}, bf16[576,256]{1,0:T(8,128)(2,1)S(1)}, u32[]{:S(2)}) copy-start(bf16[576,256]{1,0:T(8,128)(2,1)S(1)} %get-tuple-element.39) | copy-start | bytes 884740
  28.9 2.0 %copy-start.4 = (bf16[4,144,256]{2,1,0:T(8,128)(2,1)}, bf16[4,144,256]{2,1,0:T(8,128)(2,1)S(1)}, u32[]{:S(2)}) copy-start(bf16[4,144,256]{2,1,0:T(8,128)(2,1)S(1)} %collective-permute-done.7.d_ref.r3) | copy-start | bytes 884740
  28.9 2.0 %copy-start.7 = (bf16[4,144,256]{2,1,0:T(8,128)(2,1)}, bf16[4,144,256]{2,1,0:T(8,128)(2,1)S(1)}, u32[]{:S(2)}) copy-start(bf16[4,144,256]{2,1,0:T(8,128)(2,1)S(1)} %collective-permute-done.6.c_ref.r2) | copy-start | bytes 884740
  30.8 0.7 copy-start.10
  31.5 5.3 %collective-permute-start.8 = (bf16[4,4,144,256]{3,2,1,0:T(8,128)(2,1)S(1)}, bf16[4,4,144,256]{3,2,1,0:T(8,128)(2,1)S(1)}, u32[]{:S(2)}, u32[]{:S(2)}) collective-permute-start(bf16[4,4,144,256]{3,2,1,0:T(8,128)(2,1)S(1)} %gather.1), channel_id=1, source_target_pairs={{0,1},{1,0},{2,3},{3,2},{4,5},{5,4},{6,7},{7,6},{8,9},{9,8},{10,11... | collective-permute-start | bytes 3538952 | tf_op jit(solution)/shard_map/ppermute | solution.py:30
  31.5 20.5 %collective-permute-start.10 = (bf16[576,256]{1,0:T(8,128)(2,1)}, bf16[576,256]{1,0:T(8,128)(2,1)S(1)}, u32[]{:S(2)}, u32[]{:S(2)}) collective-permute-start(bf16[576,256]{1,0:T(8,128)(2,1)} %copy-done.6), channel_id=1, source_target_pairs={{0,0},{8,16},{16,8},{24,24},{1,1},{9,17},{17,9},{25,25},{2,2},{10,... | collective-permute-start | bytes 884744 | tf_op jit(solution)/shard_map/ppermute | solution.py:510
  33.1 18.9 %collective-permute-start.11 = (bf16[576,256]{1,0:T(8,128)(2,1)}, bf16[576,256]{1,0:T(8,128)(2,1)S(1)}, u32[]{:S(2)}, u32[]{:S(2)}) collective-permute-start(bf16[576,256]{1,0:T(8,128)(2,1)} %copy-done.9), channel_id=1, source_target_pairs={{16,0},{0,8},{24,16},{8,24},{17,1},{1,9},{25,17},{9,25},{18,2},{2,... | collective-permute-start | bytes 884744 | tf_op jit(solution)/shard_map/ppermute | solution.py:511
  36.8 4.0 %copy-start = (bf16[1152,4608]{1,0:T(8,128)(2,1)S(1)}, bf16[1152,4608]{1,0:T(8,128)(2,1)}, u32[]{:S(2)}) copy-start(bf16[1152,4608]{1,0:T(8,128)(2,1)} %w_hbm.1) | copy-start | bytes 31850500
  40.9 1.0 copy-start.5
  41.8 1.0 copy-start.8
  42.8 1.0 copy-start.11
  43.7 4.2 %copy-start.19 = (f32[4096,32]{1,0:T(8,128)S(1)}, f32[4096,32]{1,0:T(8,128)}, u32[]{:S(2)}) copy-start(f32[4096,32]{1,0:T(8,128)} %copy-done.18) | copy-start | bytes 1572868
  47.4 19.3 %collective-permute-start.9 = (bf16[576,256]{1,0:T(8,128)(2,1)S(1)}, bf16[576,256]{1,0:T(8,128)(2,1)S(1)}, u32[]{:S(2)}, u32[]{:S(2)}) collective-permute-start(bf16[576,256]{1,0:T(8,128)(2,1)S(1)} %get-tuple-element.35.dep_ref.rest_0_), channel_id=1, source_target_pairs={{0,16},{8,24},{16,0},{24,8},{1,17},{9,25},{17,1},{25,9},{2,18},{10... | collective-permute-start | bytes 884744 | tf_op jit(solution)/shard_map/ppermute | solution.py:30
  52.5 26.9 %collective-permute-start.14 = (bf16[576,256]{1,0:T(8,128)(2,1)S(1)}, bf16[576,256]{1,0:T(8,128)(2,1)S(1)}, u32[]{:S(2)}, u32[]{:S(2)}) collective-permute-start(bf16[576,256]{1,0:T(8,128)(2,1)S(1)} %get-tuple-element.41.dep_ref), channel_id=1, source_target_pairs={{0,16},{8,24},{16,0},{24,8},{1,17},{9,25},{17,1},{25,9},{2,18},{10... | collective-permute-start | bytes 884744 | tf_op jit(solution)/shard_map/ppermute | solution.py:30
  67.1 16.8 %collective-permute-start.13 = (bf16[576,256]{1,0:T(8,128)(2,1)S(1)}, bf16[576,256]{1,0:T(8,128)(2,1)S(1)}, u32[]{:S(2)}, u32[]{:S(2)}) collective-permute-start(bf16[576,256]{1,0:T(8,128)(2,1)S(1)} %get-tuple-element.43), channel_id=1, source_target_pairs={{0,16},{8,0},{16,24},{24,8},{1,17},{9,1},{17,25},{25,9},{2,18},{10... | collective-permute-start | bytes 884744 | tf_op jit(solution)/shard_map/ppermute | solution.py:530
  67.2 16.8 %collective-permute-start.12 = (bf16[576,256]{1,0:T(8,128)(2,1)S(1)}, bf16[576,256]{1,0:T(8,128)(2,1)S(1)}, u32[]{:S(2)}, u32[]{:S(2)}) collective-permute-start(bf16[576,256]{1,0:T(8,128)(2,1)S(1)} %get-tuple-element.42.dep_ref), channel_id=1, source_target_pairs={{0,0},{8,16},{16,8},{24,24},{1,1},{9,17},{17,9},{25,25},{2,2},{10,... | collective-permute-start | bytes 884744 | tf_op jit(solution)/shard_map/ppermute | solution.py:529
  79.4 4.6 %copy-start.13 = (f32[16,1152]{1,0:T(8,128)S(1)}, f32[16,1152]{1,0:T(8,128)}, u32[]{:S(2)}) copy-start(f32[16,1152]{1,0:T(8,128)} %mine_ref.3) | copy-start | bytes 221188
  79.4 4.6 %copy-start.15 = (f32[16,1152]{1,0:T(8,128)S(1)}, f32[16,1152]{1,0:T(8,128)}, u32[]{:S(2)}) copy-start(f32[16,1152]{1,0:T(8,128)} %copy-done.14) | copy-start | bytes 221188
  83.9 8.3 %collective-permute-start.16 = (bf16[4,4,144,256]{3,2,1,0:T(8,128)(2,1)S(1)}, bf16[4,4,144,256]{3,2,1,0:T(8,128)(2,1)S(1)}, u32[]{:S(2)}, u32[]{:S(2)}) collective-permute-start(bf16[4,4,144,256]{3,2,1,0:T(8,128)(2,1)S(1)} %get-tuple-element.47.rest_9_), channel_id=1, source_target_pairs={{0,1},{1,0},{2,3},{3,2},{4,5},{5,4},{6,7},{7,6},{8,9},{9,8},{10,11... | collective-permute-start | bytes 3538952 | tf_op jit(solution)/shard_map/ppermute | solution.py:30
  86.8 15.7 %collective-permute-start.15 = (bf16[576,256]{1,0:T(8,128)(2,1)S(1)}, bf16[576,256]{1,0:T(8,128)(2,1)S(1)}, u32[]{:S(2)}, u32[]{:S(2)}) collective-permute-start(bf16[576,256]{1,0:T(8,128)(2,1)S(1)} %get-tuple-element.49), channel_id=1, source_target_pairs={{0,8},{8,0},{16,24},{24,16},{1,9},{9,1},{17,25},{25,17},{2,10},{10... | collective-permute-start | bytes 884744 | tf_op jit(solution)/shard_map/ppermute | solution.py:30
  92.4 19.9 %collective-permute-start.17 = (bf16[4,144,256]{2,1,0:T(8,128)(2,1)S(1)}, bf16[4,144,256]{2,1,0:T(8,128)(2,1)S(1)}, u32[]{:S(2)}, u32[]{:S(2)}) collective-permute-start(bf16[4,144,256]{2,1,0:T(8,128)(2,1)S(1)} %get-tuple-element.52), channel_id=1, source_target_pairs={{0,4},{2,6},{4,0},{6,2},{1,5},{3,7},{5,1},{7,3},{8,12},{10,14},{12... | collective-permute-start | bytes 884744 | tf_op jit(solution)/shard_map/ppermute | solution.py:35
  93.6 18.8 %collective-permute-start.18 = (bf16[4,144,256]{2,1,0:T(8,128)(2,1)S(1)}, bf16[4,144,256]{2,1,0:T(8,128)(2,1)S(1)}, u32[]{:S(2)}, u32[]{:S(2)}) collective-permute-start(bf16[4,144,256]{2,1,0:T(8,128)(2,1)S(1)} %get-tuple-element.53), channel_id=1, source_target_pairs={{0,2},{2,4},{4,6},{6,0},{1,3},{3,5},{5,7},{7,1},{8,10},{10,12},{12... | collective-permute-start | bytes 884744 | tf_op jit(solution)/shard_map/ppermute | solution.py:35
  94.2 18.1 %collective-permute-start.19 = (bf16[4,144,256]{2,1,0:T(8,128)(2,1)S(1)}, bf16[4,144,256]{2,1,0:T(8,128)(2,1)S(1)}, u32[]{:S(2)}, u32[]{:S(2)}) collective-permute-start(bf16[4,144,256]{2,1,0:T(8,128)(2,1)S(1)} %get-tuple-element.54), channel_id=1, source_target_pairs={{0,6},{2,0},{4,2},{6,4},{1,7},{3,1},{5,3},{7,5},{8,14},{10,8},{12,... | collective-permute-start | bytes 884744 | tf_op jit(solution)/shard_map/ppermute | solution.py:35
  96.8 4.4 %collective-permute-start.23 = (f32[144,128]{1,0:T(8,128)S(1)}, f32[144,128]{1,0:T(8,128)S(1)}, u32[]{:S(2)}, u32[]{:S(2)}) collective-permute-start(f32[144,128]{1,0:T(8,128)S(1)} %get-tuple-element.60), channel_id=1, source_target_pairs={{0,64},{64,0},{128,192},{192,128},{1,65},{65,1},{129,193},{193,129... | collective-permute-start | bytes 221192 | tf_op jit(solution)/shard_map/ppermute | solution.py:30
  101.2 5.9 %collective-permute-start.24 = (f32[144,128]{1,0:T(8,128)S(1)}, f32[144,128]{1,0:T(8,128)S(1)}, u32[]{:S(2)}, u32[]{:S(2)}) collective-permute-start(f32[144,128]{1,0:T(8,128)S(1)} %add.23.a_ref), channel_id=1, source_target_pairs={{0,128},{64,192},{128,0},{192,64},{1,129},{65,193},{129,1},{193,65... | collective-permute-start | bytes 221192 | tf_op jit(solution)/shard_map/ppermute | solution.py:30
  107.1 9.8 %collective-permute-start.25 = (f32[144,128]{1,0:T(8,128)S(1)}, f32[144,128]{1,0:T(8,128)S(1)}, u32[]{:S(2)}, u32[]{:S(2)}) collective-permute-start(f32[144,128]{1,0:T(8,128)S(1)} %add.31.a_ref), channel_id=1, source_target_pairs={{0,32},{32,0},{1,33},{33,1},{2,34},{34,2},{3,35},{35,3},{4,36},{36... | collective-permute-start | bytes 221192 | tf_op jit(solution)/shard_map/ppermute | solution.py:30
  112.5 6.2 %collective-permute-start.20 = (bf16[144,256]{1,0:T(8,128)(2,1)S(1)}, bf16[144,256]{1,0:T(8,128)(2,1)S(1)}, u32[]{:S(2)}, u32[]{:S(2)}) collective-permute-start(bf16[144,256]{1,0:T(8,128)(2,1)S(1)} %get-tuple-element.56), channel_id=1, source_target_pairs={{0,8},{8,0},{16,24},{24,16},{1,9},{9,1},{17,25},{25,17},{2,10},{10... | collective-permute-start | bytes 221192 | tf_op jit(solution)/shard_map/ppermute | solution.py:30
  112.6 6.8 %collective-permute-start.21 = (bf16[144,256]{1,0:T(8,128)(2,1)S(1)}, bf16[144,256]{1,0:T(8,128)(2,1)S(1)}, u32[]{:S(2)}, u32[]{:S(2)}) collective-permute-start(bf16[144,256]{1,0:T(8,128)(2,1)S(1)} %get-tuple-element.57), channel_id=1, source_target_pairs={{0,16},{8,24},{16,0},{24,8},{1,17},{9,25},{17,1},{25,9},{2,18},{10... | collective-permute-start | bytes 221192 | tf_op jit(solution)/shard_map/ppermute | solution.py:30
  115.2 6.2 %collective-permute-start.22 = (bf16[144,256]{1,0:T(8,128)(2,1)S(1)}, bf16[144,256]{1,0:T(8,128)(2,1)S(1)}, u32[]{:S(2)}, u32[]{:S(2)}) collective-permute-start(bf16[144,256]{1,0:T(8,128)(2,1)S(1)} %get-tuple-element.58), channel_id=1, source_target_pairs={{0,24},{8,16},{16,8},{24,0},{1,25},{9,17},{17,9},{25,1},{2,26},{10... | collective-permute-start | bytes 221192 | tf_op jit(solution)/shard_map/ppermute | solution.py:30
  117.0 4.5 %collective-permute-start.26 = (f32[144,128]{1,0:T(8,128)S(1)}, f32[144,128]{1,0:T(8,128)S(1)}, u32[]{:S(2)}, u32[]{:S(2)}) collective-permute-start(f32[144,128]{1,0:T(8,128)S(1)} %add.32.mine_ref), channel_id=1, source_target_pairs={{0,64},{64,0},{128,192},{192,128},{1,65},{65,1},{129,193},{193,129... | collective-permute-start | bytes 221192 | tf_op jit(solution)/shard_map/ppermute | solution.py:30
  121.4 2.3 %copy-start.1 = (bf16[144,256]{1,0:T(8,128)(2,1)}, bf16[144,256]{1,0:T(8,128)(2,1)S(1)}, u32[]{:S(2)}) copy-start(bf16[144,256]{1,0:T(8,128)(2,1)S(1)} %add_convert_fusion.dep_ref) | copy-start | bytes 221188
